TPU v7x, 32 devices: a whole 2x2x4 slice. The times are simulated.
32 devices in a mesh: seq: 8 (over z, y), mp: 4 (over x, core).
Axes of the slice: x: 2, y: 2, z: 4, core: 2. Of those that a mesh axis runs over, the one named last changes fastest.
Arguments:
- block_input: bfloat16 [2, 16384, 512], P(None, ('seq', 'mp')), may hold values from -6 to 6
- cotangent: bfloat16 [2, 16384, 512], P(None, 'seq'), may hold values from -6 to 6
- span_offset: int32 [2], replicated, may hold values from 1 to 127
- doc_lengths: int32 [2, 8], replicated, may hold values from 1 to 15360, 16384 in all within a row
- ln1_gain: float32 [512], replicated, may hold values from 0.5 to 1.5
- ln1_bias: float32 [512], replicated, may hold values from -3 to 3
- w_query: bfloat16 [512, 512], P('seq', 'mp'), may hold values from -0.25 to 0.25
- w_key: bfloat16 [512, 512], P('seq', 'mp'), may hold values from -0.25 to 0.25
- w_value: bfloat16 [512, 512], P('seq', 'mp'), may hold values from -0.25 to 0.25
- query_bias: float32 [512], replicated, may hold values from -3 to 3
- value_bias: float32 [512], replicated, may hold values from -3 to 3
- w_out: bfloat16 [512, 512], P('mp', 'seq'), may hold values from -2 to 2
- out_bias: float32 [512], replicated, may hold values from -3 to 3
- ln2_gain: float32 [512], replicated, may hold values from 0.5 to 1.5
- ln2_bias: float32 [512], replicated, may hold values from -3 to 3
- w_up: bfloat16 [512, 2048], P('seq', 'mp'), may hold values from -0.25 to 0.25
- up_bias: float32 [2048], replicated, may hold values from -3 to 3
- w_down: bfloat16 [2048, 512], P('mp', 'seq'), may hold values from -0.75 to 0.75
- down_bias: float32 [512], replicated, may hold values from -3 to 3
Outputs:
- result: bfloat16 [2, 16384, 512], P(None, ('seq', 'mp'))
- input_grad: float32 [2, 16384, 512], P(None, ('seq', 'mp'))
- grad_ln1_gain: float32 [512], replicated
- grad_ln1_bias: float32 [512], replicated
- grad_w_query: float32 [512, 512], P('seq', 'mp')
- grad_w_key: float32 [512, 512], P('seq', 'mp')
- grad_w_value: float32 [512, 512], P('seq', 'mp')
- grad_query_bias: float32 [512], replicated
- grad_value_bias: float32 [512], replicated
- grad_w_out: float32 [512, 512], P('mp', 'seq')
- grad_out_bias: float32 [512], replicated
- grad_ln2_gain: float32 [512], replicated
- grad_ln2_bias: float32 [512], replicated
- grad_w_up: float32 [512, 2048], P('seq', 'mp')
- grad_up_bias: float32 [2048], replicated
- grad_w_down: float32 [2048, 512], P('mp', 'seq')
- grad_down_bias: float32 [512], replicated
Inputs may be any that keep to these rules, and one draw needn't show every extreme that they name: `doc_lengths`: each row's 8 lengths add up to 16384, and one document of each row has exactly 15360 positions.
All inputs are finite; a program needn't handle non-finite values.
Results may differ from a plain program's by a relative error of at most 0.012.
The roundings to bfloat16 on the way count: a program that leaves them out, or rounds other values in their place, can miss the bound.
Values may be sent and summed in bfloat16 or wider, within the bound.
No kernel may reach another device: no remote copies, remote signals or barrier semaphores. Data moves between devices by JAX's collectives and lax.ppermute only.
A program may use at most 128 MiB of HBM per device.

v0:
```python
from functools import partial
import math

import jax
import jax.numpy as jnp
from jax import lax
from jax.sharding import PartitionSpec as P

D = 512
FF = 2048
HEAD_DIM = 64
SPAN = 128
QBLOCK = 512


EPSILON = 1e-05
NEGATIVE = -1e30


def shifted(x, axis, by):
    count = lax.axis_size(axis)
    pairs = [(i, i + by) for i in range(count) if 0 <= i + by < count]
    return lax.ppermute(x, axis, pairs)


def normalize(inputs, norm_gain, norm_shift):
    row_mean = jnp.mean(inputs, axis=-1, keepdims=True)
    centred = inputs - row_mean
    variance = jnp.mean(centred * centred, axis=-1, keepdims=True)
    return centred * lax.rsqrt(variance + EPSILON) * norm_gain + norm_shift


def doc_index(positions, doc_ends):
    return jnp.sum((doc_ends[None, :] <= positions[:, None]).astype(jnp.int32), axis=1)


def span_index(positions, offset):
    return (positions - offset + SPAN) // SPAN


def block_masks(query_pos, key_pos, offset, doc_ends, summary_docs):
    query_doc = doc_index(query_pos, doc_ends)
    key_doc = doc_index(key_pos, doc_ends)
    query_span = span_index(query_pos, offset)
    key_span = span_index(key_pos, offset)
    local_ok = (key_pos[None, :] >= 0) & (key_pos[None, :] <= query_pos[:, None])
    local_ok = (
        local_ok
        & (key_span[None, :] == query_span[:, None])
        & (key_doc[None, :] == query_doc[:, None])
    )
    summary_ids = jnp.arange(summary_docs.shape[0], dtype=jnp.int32)
    summary_ok = (summary_ids[None, :] < query_span[:, None]) & (
        summary_docs[None, :] == query_doc[:, None]
    )
    return (local_ok, summary_ok)


def contract_rows(left, right):
    return lax.dot_general(
        left, right, (((0,), (0,)), ((), ())), preferred_element_type=jnp.float32
    )


def contract_cols(left, right):
    return lax.dot_general(
        left, right, (((1,), (1,)), ((), ())), preferred_element_type=jnp.float32
    )


def add_rows(target, first_row, addend):
    current = lax.dynamic_slice_in_dim(target, first_row, addend.shape[0], 0)
    return lax.dynamic_update_slice_in_dim(target, current + addend, first_row, 0)


def fetch_weights(w_query, w_key, w_value, w_out, w_up, w_down):
    wq_rows, wk_rows, wv_rows, wo_rows, wu_rows, wd_rows = (
        lax.all_gather(w_query, "seq", axis=0, tiled=True),
        lax.all_gather(w_key, "seq", axis=0, tiled=True),
        lax.all_gather(w_value, "seq", axis=0, tiled=True),
        lax.all_gather(w_out, "seq", axis=1, tiled=True),
        lax.all_gather(w_up, "seq", axis=0, tiled=True),
        lax.all_gather(w_down, "seq", axis=1, tiled=True),
    )
    return (wq_rows, wk_rows, wv_rows, wo_rows, wu_rows, wd_rows)


def reduce_weights(grad_query, grad_key, grad_value, grad_out, grad_up, grad_down):
    sum_q, sum_k, sum_v, sum_o, sum_u, sum_d = (
        lax.psum_scatter(grad_query, "seq", scatter_dimension=0, tiled=True),
        lax.psum_scatter(grad_key, "seq", scatter_dimension=0, tiled=True),
        lax.psum_scatter(grad_value, "seq", scatter_dimension=0, tiled=True),
        lax.psum_scatter(grad_out, "seq", scatter_dimension=1, tiled=True),
        lax.psum_scatter(grad_up, "seq", scatter_dimension=0, tiled=True),
        lax.psum_scatter(grad_down, "seq", scatter_dimension=1, tiled=True),
    )
    return (sum_q, sum_k, sum_v, sum_o, sum_u, sum_d)


def per_device(
    block_input,
    cotangent,
    span_offset,
    doc_lengths,
    ln1_gain,
    ln1_bias,
    w_query,
    w_key,
    w_value,
    query_bias,
    value_bias,
    w_out,
    out_bias,
    ln2_gain,
    ln2_bias,
    w_up,
    up_bias,
    w_down,
    down_bias,
):
    mp_index = lax.axis_index("mp")
    local_row_block = block_input.shape[1]
    dev_count = lax.axis_size("seq")
    dev_index = lax.axis_index("seq")
    group_rows = cotangent.shape[1]
    head_width = w_query.shape[1]
    hidden_width = w_up.shape[1]
    head_start = mp_index * head_width
    hidden_start = mp_index * hidden_width
    block_rows = QBLOCK
    local_heads = head_width // HEAD_DIM
    summary_own = group_rows // SPAN
    summary_total = summary_own * dev_count
    block_count = group_rows // block_rows
    score_scale = 1.0 / math.sqrt(HEAD_DIM)
    group_start = dev_index * group_rows
    row_start = mp_index * local_row_block
    bias_query = lax.dynamic_slice_in_dim(query_bias, head_start, head_width)
    bias_value = lax.dynamic_slice_in_dim(value_bias, head_start, head_width)
    bias_qkv = jnp.concatenate((bias_query, jnp.zeros_like(bias_query), bias_value))
    bias_up = lax.dynamic_slice_in_dim(up_bias, hidden_start, hidden_width)
    gelu_fn = partial(jax.nn.gelu, approximate=True)

    def micro_step(gathered, inputs, grad_group, offset, lengths):
        wq_full, wk_full, wv_full, wo_full, wu_full, wd_full = gathered
        w_qkv = jnp.concatenate((wq_full, wk_full, wv_full), axis=1)
        doc_ends = jnp.cumsum(lengths)
        inputs_wide = inputs.astype(jnp.float32)
        normed_own = normalize(inputs_wide, ln1_gain, ln1_bias)
        normed_group = lax.all_gather(normed_own.astype(jnp.bfloat16), "mp", axis=0, tiled=True)
        projected = jnp.dot(normed_group, w_qkv, preferred_element_type=jnp.float32) + bias_qkv
        queries = projected[:, :head_width].astype(jnp.bfloat16)
        key_rows = projected[:, head_width : 2 * head_width].astype(jnp.bfloat16)
        value_rows = projected[:, 2 * head_width :].astype(jnp.bfloat16)
        halo_keys, halo_values = shifted(
            (key_rows[group_rows - SPAN :], value_rows[group_rows - SPAN :]), "seq", 1
        )
        pad_keys = jnp.concatenate((halo_keys, key_rows), axis=0)
        pad_values = jnp.concatenate((halo_values, value_rows), axis=0)
        span_pos = group_start + offset - SPAN + jnp.arange(group_rows, dtype=jnp.int32)
        span_doc = doc_index(span_pos, doc_ends).reshape(summary_own, SPAN)
        own_ends = (
            offset - 1 + SPAN * (dev_index * summary_own + jnp.arange(summary_own, dtype=jnp.int32))
        )
        own_docs = doc_index(own_ends, doc_ends)
        group_member = (
            (span_pos.reshape(summary_own, SPAN) >= 0) & (span_doc == own_docs[:, None])
        ).astype(jnp.float32)
        inv_count = lax.rsqrt(jnp.sum(group_member, axis=1))
        member_low = group_member.astype(jnp.bfloat16)
        span_keys = lax.dynamic_slice_in_dim(pad_keys, offset, group_rows, 0).reshape(
            summary_own, SPAN, head_width
        )
        span_values = lax.dynamic_slice_in_dim(pad_values, offset, group_rows, 0).reshape(
            summary_own, SPAN, head_width
        )
        local_summary_keys = (
            jnp.einsum("js,jsd->jd", member_low, span_keys, preferred_element_type=jnp.float32)
            * inv_count[:, None]
        ).astype(jnp.bfloat16)
        own_svalues = (
            jnp.einsum("js,jsd->jd", member_low, span_values, preferred_element_type=jnp.float32)
            * inv_count[:, None]
        ).astype(jnp.bfloat16)
        summ_keys, summ_values = (
            lax.all_gather(local_summary_keys, "seq", axis=0, tiled=True),
            lax.all_gather(own_svalues, "seq", axis=0, tiled=True),
        )
        summ_keys3 = summ_keys.reshape(summary_total, local_heads, HEAD_DIM)
        summ_values3 = summ_values.reshape(summary_total, local_heads, HEAD_DIM)
        all_ends = offset - 1 + SPAN * jnp.arange(summary_total, dtype=jnp.int32)
        summary_docs = doc_index(all_ends, doc_ends)

        def block_parts(block_id):
            first_row = block_id * block_rows
            block_queries = lax.dynamic_slice_in_dim(queries, first_row, block_rows, 0).reshape(
                block_rows, local_heads, HEAD_DIM
            )
            block_keys = lax.dynamic_slice_in_dim(
                pad_keys, first_row, block_rows + SPAN, 0
            ).reshape(block_rows + SPAN, local_heads, HEAD_DIM)
            block_values = lax.dynamic_slice_in_dim(
                pad_values, first_row, block_rows + SPAN, 0
            ).reshape(block_rows + SPAN, local_heads, HEAD_DIM)
            query_pos = group_start + first_row + jnp.arange(block_rows, dtype=jnp.int32)
            key_pos = (
                group_start + first_row - SPAN + jnp.arange(block_rows + SPAN, dtype=jnp.int32)
            )
            local_ok, summary_ok = block_masks(query_pos, key_pos, offset, doc_ends, summary_docs)
            local_scores = (
                jnp.einsum(
                    "qhd,khd->hqk", block_queries, block_keys, preferred_element_type=jnp.float32
                )
                * score_scale
            )
            summary_scores = (
                jnp.einsum(
                    "qhd,jhd->hqj", block_queries, summ_keys3, preferred_element_type=jnp.float32
                )
                * score_scale
            )
            local_scores = jnp.where(local_ok[None], local_scores, NEGATIVE)
            summary_scores = jnp.where(summary_ok[None], summary_scores, NEGATIVE)
            return (block_queries, block_keys, block_values, local_scores, summary_scores)

        def forward_block(block_id):
            block_queries, block_keys, block_values, local_scores, summary_scores = block_parts(
                block_id
            )
            row_top = jnp.maximum(jnp.max(local_scores, axis=-1), jnp.max(summary_scores, axis=-1))
            local_exp = jnp.exp(local_scores - row_top[..., None])
            summary_exp = jnp.exp(summary_scores - row_top[..., None])
            exp_total = jnp.sum(local_exp, axis=-1) + jnp.sum(summary_exp, axis=-1)
            local_probs = (local_exp / exp_total[..., None]).astype(jnp.bfloat16)
            summary_probs = (summary_exp / exp_total[..., None]).astype(jnp.bfloat16)
            mixed = jnp.einsum(
                "hqk,khd->qhd", local_probs, block_values, preferred_element_type=jnp.float32
            )
            mixed = mixed + jnp.einsum(
                "hqj,jhd->qhd", summary_probs, summ_values3, preferred_element_type=jnp.float32
            )
            return (
                mixed.reshape(block_rows, head_width).astype(jnp.bfloat16),
                row_top + jnp.log(exp_total),
            )

        block_ids = jnp.arange(block_count, dtype=jnp.int32)
        attended_blocks, log_totals = lax.map(forward_block, block_ids)
        attended = attended_blocks.reshape(group_rows, head_width)
        attn_total = lax.psum_scatter(
            jnp.dot(attended, wo_full, preferred_element_type=jnp.float32),
            "mp",
            scatter_dimension=0,
            tiled=True,
        )
        resid_mid = inputs_wide + attn_total + out_bias
        second_normed_rows = normalize(resid_mid, ln2_gain, ln2_bias)
        normed_two_group = lax.all_gather(
            second_normed_rows.astype(jnp.bfloat16), "mp", axis=0, tiled=True
        )
        up_proj = jnp.dot(normed_two_group, wu_full, preferred_element_type=jnp.float32) + bias_up
        gelu_out, gelu_back = jax.vjp(gelu_fn, up_proj)
        activated = gelu_out.astype(jnp.bfloat16)
        mlp_total = lax.psum_scatter(
            jnp.dot(
                lax.slice_in_dim(activated, 0, local_row_block * lax.axis_size("mp"), axis=0),
                wd_full,
                preferred_element_type=jnp.float32,
            ),
            "mp",
            scatter_dimension=0,
            tiled=True,
        )
        result = resid_mid + mlp_total + down_bias
        grad_local = lax.dynamic_slice_in_dim(grad_group, row_start, local_row_block, 0)
        grad_own = grad_local.astype(jnp.float32)
        grad_wd = contract_rows(activated, grad_group)
        grad_act = contract_cols(grad_group, wd_full)
        grad_up = gelu_back(grad_act)[0].astype(jnp.bfloat16)
        grad_wu = contract_rows(normed_two_group, grad_up)
        grad_normed_two = lax.psum_scatter(
            contract_cols(grad_up, wu_full), "mp", scatter_dimension=0, tiled=True
        )
        norm_two_fwd, norm_two_back = jax.vjp(normalize, resid_mid, ln2_gain, ln2_bias)
        grad_mid_part, grad_gain_two, grad_shift_two = norm_two_back(grad_normed_two)
        grad_mid = grad_own + grad_mid_part
        grad_branch = grad_mid.astype(jnp.bfloat16)
        branch_group = lax.all_gather(grad_branch, "mp", axis=0, tiled=True)
        grad_wo = contract_rows(attended, branch_group)
        grad_attended = contract_cols(branch_group, wo_full).astype(jnp.bfloat16)

        def backward_block(running_sums, block_slot):
            pad_gk, pad_gv, summ_gk, summ_gv = running_sums
            block_id, log_total = block_slot
            first_row = block_id * block_rows
            block_queries, block_keys, block_values, local_scores, summary_scores = block_parts(
                block_id
            )
            block_grads = lax.dynamic_slice_in_dim(grad_attended, first_row, block_rows, 0).reshape(
                block_rows, local_heads, HEAD_DIM
            )
            local_probs = jnp.exp(local_scores - log_total[..., None])
            summary_probs = jnp.exp(summary_scores - log_total[..., None])
            local_gp = jnp.einsum(
                "qhd,khd->hqk", block_grads, block_values, preferred_element_type=jnp.float32
            )
            summary_gp = jnp.einsum(
                "qhd,jhd->hqj", block_grads, summ_values3, preferred_element_type=jnp.float32
            )
            row_delta = jnp.sum(local_probs * local_gp, axis=-1) + jnp.sum(
                summary_probs * summary_gp, axis=-1
            )
            local_gs = (local_probs * (local_gp - row_delta[..., None])).astype(jnp.bfloat16)
            summary_gs = (summary_probs * (summary_gp - row_delta[..., None])).astype(jnp.bfloat16)
            grad_q = jnp.einsum(
                "hqk,khd->qhd", local_gs, block_keys, preferred_element_type=jnp.float32
            )
            grad_q = grad_q + jnp.einsum(
                "hqj,jhd->qhd", summary_gs, summ_keys3, preferred_element_type=jnp.float32
            )
            grad_q = (grad_q * score_scale).reshape(block_rows, head_width).astype(jnp.bfloat16)
            grad_k = (
                jnp.einsum(
                    "hqk,qhd->khd", local_gs, block_queries, preferred_element_type=jnp.float32
                )
                * score_scale
            )
            grad_v = jnp.einsum(
                "hqk,qhd->khd",
                local_probs.astype(jnp.bfloat16),
                block_grads,
                preferred_element_type=jnp.float32,
            )
            pad_gk = add_rows(pad_gk, first_row, grad_k.reshape(block_rows + SPAN, head_width))
            pad_gv = add_rows(pad_gv, first_row, grad_v.reshape(block_rows + SPAN, head_width))
            summ_gk = summ_gk + (
                jnp.einsum(
                    "hqj,qhd->jhd", summary_gs, block_queries, preferred_element_type=jnp.float32
                )
                * score_scale
            ).reshape(summary_total, head_width)
            summ_gv = summ_gv + jnp.einsum(
                "hqj,qhd->jhd",
                summary_probs.astype(jnp.bfloat16),
                block_grads,
                preferred_element_type=jnp.float32,
            ).reshape(summary_total, head_width)
            return ((pad_gk, pad_gv, summ_gk, summ_gv), grad_q)

        pad_zero = jnp.zeros((group_rows + SPAN, head_width), jnp.float32)
        summ_zero = jnp.zeros((summary_total, head_width), jnp.float32)
        (pad_gk, pad_gv, summ_gk, summ_gv), grad_q_blocks = lax.scan(
            backward_block, (pad_zero, pad_zero, summ_zero, summ_zero), (block_ids, log_totals)
        )
        grad_queries = grad_q_blocks.reshape(group_rows, head_width)
        own_gk, own_gv = (
            lax.psum_scatter(summ_gk, "seq", scatter_dimension=0, tiled=True),
            lax.psum_scatter(summ_gv, "seq", scatter_dimension=0, tiled=True),
        )
        spread_keys = (
            group_member[:, :, None] * (own_gk * inv_count[:, None])[:, None, :]
        ).reshape(group_rows, head_width)
        spread_values = (
            group_member[:, :, None] * (own_gv * inv_count[:, None])[:, None, :]
        ).reshape(group_rows, head_width)
        pad_gk = add_rows(pad_gk, offset, spread_keys)
        pad_gv = add_rows(pad_gv, offset, spread_values)
        back_keys, back_values = shifted((pad_gk[:SPAN], pad_gv[:SPAN]), "seq", -1)
        grad_keys = pad_gk[SPAN:].at[group_rows - SPAN :].add(back_keys).astype(jnp.bfloat16)
        grad_values = pad_gv[SPAN:].at[group_rows - SPAN :].add(back_values).astype(jnp.bfloat16)
        grad_qkv = jnp.concatenate((grad_queries, grad_keys, grad_values), axis=1)
        grad_w_qkv = contract_rows(normed_group, grad_qkv)
        grad_normed_one = lax.psum_scatter(
            contract_cols(grad_qkv, w_qkv), "mp", scatter_dimension=0, tiled=True
        )
        norm_one_fwd, norm_one_back = jax.vjp(normalize, inputs_wide, ln1_gain, ln1_bias)
        grad_in_part, grad_gain_one, grad_shift_one = norm_one_back(grad_normed_one)
        grad_input = grad_mid + grad_in_part
        zero_model = jnp.zeros((D,), jnp.float32)
        grad_qbias = lax.dynamic_update_slice_in_dim(
            zero_model, jnp.sum(grad_queries.astype(jnp.float32), axis=0), head_start, 0
        )
        grad_vbias = lax.dynamic_update_slice_in_dim(
            zero_model, jnp.sum(grad_values.astype(jnp.float32), axis=0), head_start, 0
        )
        grad_ubias = lax.dynamic_update_slice_in_dim(
            jnp.zeros((FF,), jnp.float32),
            jnp.sum(grad_up.astype(jnp.float32), axis=0),
            hidden_start,
            0,
        )
        grad_obias = jnp.sum(grad_branch.astype(jnp.float32), axis=0)
        grad_down_bias_sum = jnp.sum(grad_own, axis=0)
        weight_grads = (
            grad_w_qkv[:, :head_width],
            grad_w_qkv[:, head_width : 2 * head_width],
            grad_w_qkv[:, 2 * head_width :],
            grad_wo,
            grad_wu,
            grad_wd,
        )
        small_grads = (
            grad_gain_one,
            grad_shift_one,
            grad_qbias,
            grad_vbias,
            grad_obias,
            grad_gain_two,
            grad_shift_two,
            grad_ubias,
            grad_down_bias_sum,
        )
        return (result, grad_input, weight_grads, small_grads)

    weight_init = tuple(
        (
            jnp.zeros(weight.shape, jnp.float32)
            for weight in (w_query, w_key, w_value, w_out, w_up, w_down)
        )
    )
    small_init = tuple(
        (
            jnp.zeros(flat_vector.shape, jnp.float32)
            for flat_vector in (
                ln1_gain,
                ln1_bias,
                query_bias,
                value_bias,
                out_bias,
                ln2_gain,
                ln2_bias,
                up_bias,
                down_bias,
            )
        )
    )

    def micro(running_sums, batch_slot):
        weight_acc, small_acc = running_sums
        inputs, grad_group, offset, lengths = batch_slot
        gathered = fetch_weights(w_query, w_key, w_value, w_out, w_up, w_down)
        result, grad_input, weight_grads, small_grads = micro_step(
            gathered, inputs, grad_group, offset, lengths
        )
        grad_query, grad_key, grad_value, grad_out, grad_up, grad_down = weight_grads
        weight_grads = reduce_weights(
            grad_query, grad_key, grad_value, grad_out, grad_up, grad_down
        )
        weight_acc = tuple((running + addend for running, addend in zip(weight_acc, weight_grads)))
        small_acc = tuple((running + addend for running, addend in zip(small_acc, small_grads)))
        return ((weight_acc, small_acc), (result.astype(jnp.bfloat16), grad_input))

    (weight_acc, small_acc), (results, input_grads) = lax.scan(
        micro, (weight_init, small_init), (block_input, cotangent, span_offset, doc_lengths)
    )
    (
        gain_one,
        shift_one,
        qbias_sum,
        vbias_sum,
        obias_sum,
        gain_two,
        shift_two,
        ubias_sum,
        dbias_sum,
    ) = small_acc
    small_sums = lax.psum(
        (
            gain_one,
            shift_one,
            qbias_sum,
            vbias_sum,
            obias_sum,
            gain_two,
            shift_two,
            ubias_sum,
            dbias_sum,
        ),
        ("seq", "mp"),
    )
    return (
        results,
        input_grads,
        small_sums[0],
        small_sums[1],
        weight_acc[0],
        weight_acc[1],
        weight_acc[2],
        small_sums[2],
        small_sums[3],
        weight_acc[3],
        small_sums[4],
        small_sums[5],
        small_sums[6],
        weight_acc[4],
        small_sums[7],
        weight_acc[5],
        small_sums[8],
    )


def solution(mesh):
    return jax.shard_map(
        per_device,
        mesh=mesh,
        in_specs=(
            P(None, ("seq", "mp"), None),
            P(None, "seq", None),
            P(),
            P(),
            P(),
            P(),
            P("seq", "mp"),
            P("seq", "mp"),
            P("seq", "mp"),
            P(),
            P(),
            P("mp", "seq"),
            P(),
            P(),
            P(),
            P("seq", "mp"),
            P(),
            P("mp", "seq"),
            P(),
        ),
        out_specs=(
            P(None, ("seq", "mp"), None),
            P(None, ("seq", "mp"), None),
            P(),
            P(),
            P("seq", "mp"),
            P("seq", "mp"),
            P("seq", "mp"),
            P(),
            P(),
            P("mp", "seq"),
            P(),
            P(),
            P(),
            P("seq", "mp"),
            P(),
            P("mp", "seq"),
            P(),
        ),
        check_vma=False,
    )
```

profile of v0, /device:TPU:0, one launch (start us, length us, event | category | flops | bytes accessed | tf_op | source)
XLA Modules:
  0.0 2381.2 jit_solution(13770440190175366796)
XLA Ops:
  11.9 2322.1 %while.134 = (s32[]{:T(128)}, f32[64,128]{1,0:T(8,128)}, f32[64,128]{1,0:T(8,128)}, f32[64,128]{1,0:T(8,128)}, f32[128,64]{0,1:T(8,128)}, /*index=5*/f32[64,512]...) while((s32[]{:T(128)}, f32[64,128]{1,0:T(8,128)}, ...), condition=%wide.region_49.50_spmd.clone, body=%wide.region_0.49_spmd.clone.sunk | while | flops 10474008576 | bytes 405598560 | solution.py:453
  22.6 32.3 %all_gather.116 = bf16[128,512]{0,1:T(8,128)(2,1)S(1)} all-gather(bf16[128,64]{0,1:T(8,128)(2,1)S(1)} %copy-done.51), channel_id=1, replica_groups=mesh['seq'=8,'mp'=4] {'seq'}, dimensions={1}, use_global_device_ids=true | all-gather | bytes 147456 | tf_op jit(solution)/shard_map/while/body/eval_jaxpr/all_gather | solution.py:81
  54.9 30.5 %all_gather.113 = bf16[512,128]{1,0:T(8,128)(2,1)S(1)} all-gather(bf16[64,128]{1,0:T(8,128)(2,1)S(1)} %copy-done.50), channel_id=1, replica_groups=mesh['seq'=8,'mp'=4] {'seq'}, dimensions={0}, use_global_device_ids=true | all-gather | bytes 147456 | tf_op jit(solution)/shard_map/while/body/eval_jaxpr/all_gather | solution.py:80
  85.4 30.5 %all_gather.112 = bf16[512,128]{1,0:T(8,128)(2,1)S(1)} all-gather(bf16[64,128]{1,0:T(8,128)(2,1)S(1)} %copy-done.49), channel_id=1, replica_groups=mesh['seq'=8,'mp'=4] {'seq'}, dimensions={0}, use_global_device_ids=true | all-gather | bytes 147456 | tf_op jit(solution)/shard_map/while/body/eval_jaxpr/all_gather | solution.py:79
  116.0 30.5 %all_gather.111 = bf16[512,128]{1,0:T(8,128)(2,1)S(1)} all-gather(bf16[64,128]{1,0:T(8,128)(2,1)S(1)} %copy-done.48), channel_id=1, replica_groups=mesh['seq'=8,'mp'=4] {'seq'}, dimensions={0}, use_global_device_ids=true | all-gather | bytes 147456 | tf_op jit(solution)/shard_map/while/body/eval_jaxpr/all_gather | solution.py:78
  160.7 33.6 %all_gather.114 = bf16[128,128]{1,0:T(8,128)(2,1)S(1)} all-gather(bf16[16,128]{1,0:T(8,128)(2,1)S(1)} %get-tuple-element.2383), channel_id=1, replica_groups=mesh['seq'=8,'mp'=4] {'seq'}, dimensions={0}, use_global_device_ids=true | all-gather | bytes 36864 | tf_op jit(solution)/shard_map/while/body/eval_jaxpr/all_gather | solution.py:186
  194.4 30.4 %all_gather.115 = bf16[128,128]{1,0:T(8,128)(2,1)S(1)} all-gather(bf16[16,128]{1,0:T(8,128)(2,1)S(1)} %get-tuple-element.2384), channel_id=1, replica_groups=mesh['seq'=8,'mp'=4] {'seq'}, dimensions={0}, use_global_device_ids=true | all-gather | bytes 36864 | tf_op jit(solution)/shard_map/while/body/eval_jaxpr/all_gather | solution.py:187
  225.0 41.4 %while.135 = (s32[]{:T(128)}, bf16[4,512,128]{2,1,0:T(8,128)(2,1)S(1)}, f32[4,2,512]{2,1,0:T(2,128)}, s32[4]{0:T(128)S(1)}, bf16[2176,128]{0,1:T(8,128)(2,1)}, /...) while((s32[]{:T(128)}, ...), condition=%wide.region_15.15_spmd, body=%wide.region_8.14_spmd.sunk | while | flops 212580736 | bytes 13743748 | solution.py:248
  270.0 43.1 %reduce-scatter.21.cloned.1.call-done = f32[512,512]{1,0:T(8,128)} async-done(((f32[2048,512]{1,0:T(8,128)}), f32[512,512]{1,0:T(8,128)}) %reduce-scatter.21.cloned.1.call-update) | async-done | bytes 1048592 | tf_op jit(solution)/shard_map/while/body/eval_jaxpr/reduce_scatter | solution.py:250
  316.0 31.4 %all_gather.118 = bf16[512,512]{1,0:T(8,128)(2,1)S(1)} all-gather(bf16[64,512]{1,0:T(8,128)(2,1)S(1)} %copy-done.31), channel_id=1, replica_groups=mesh['seq'=8,'mp'=4] {'seq'}, dimensions={0}, use_global_device_ids=true | all-gather | bytes 589824 | tf_op jit(solution)/shard_map/while/body/eval_jaxpr/all_gather | solution.py:82
  347.4 33.4 %all_gather.119 = bf16[512,512]{0,1:T(8,128)(2,1)} all-gather(bf16[512,64]{0,1:T(8,128)(2,1)S(1)} %copy-done.30), channel_id=1, replica_groups=mesh['seq'=8,'mp'=4] {'seq'}, dimensions={1}, use_global_device_ids=true | all-gather | bytes 589824 | tf_op jit(solution)/shard_map/while/body/eval_jaxpr/all_gather | solution.py:83
  383.9 5.4 convert_reduce_fusion.32
  392.6 44.9 %reduce-scatter.23.cloned.1.call-done = f32[512,512]{1,0:T(8,128)} async-done(((f32[2048,512]{1,0:T(8,128)}), f32[512,512]{1,0:T(8,128)}) %reduce-scatter.23.cloned.1.call-update) | async-done | bytes 1048592 | tf_op jit(solution)/shard_map/while/body/eval_jaxpr/reduce_scatter | solution.py:281
  444.1 22.7 all-gather.8.cloned.1.call-done
  472.0 89.4 %while.136 = (s32[]{:T(128)}, f32[2176,128]{1,0:T(8,128)}, f32[2176,128]{1,0:T(8,128)}, f32[128,128]{0,1:T(8,128)}, f32[128,128]{0,1:T(8,128)S(1)}, /*index=5*/b...) while((s32[]{:T(128)}, f32[2176,128]{1,0:T(8,128)}, ...), condition=%wide.region_27.27_spmd.clone, body=%wide.region_22.26_spmd.clone.sunk | while | flops 513129984 | bytes 38946836 | solution.py:352
  563.9 6.0 fusion.293
  569.9 3.9 fusion.292
  573.9 6.1 fusion.297
  580.7 43.8 %reduce-scatter.25.cloned.1.call-done = f32[16,128]{1,0:T(8,128)} async-done(((f32[128,128]{1,0:T(8,128)}), f32[16,128]{1,0:T(8,128)}) %reduce-scatter.25.cloned.1.call-update) | async-done | bytes 8208 | tf_op jit(solution)/shard_map/while/body/eval_jaxpr/reduce_scatter | solution.py:357
  624.5 63.7 %reduce-scatter.27.cloned.1.call-done = f32[16,128]{1,0:T(8,128)} async-done(((f32[128,128]{1,0:T(8,128)}), f32[16,128]{1,0:T(8,128)}) %reduce-scatter.27.cloned.1.call-update) | async-done | bytes 8208 | tf_op jit(solution)/shard_map/while/body/eval_jaxpr/reduce_scatter | solution.py:358
  690.7 4.7 dynamic_update_slice.115
  703.2 4.7 dynamic_update_slice.114
  709.9 4.8 collective-permute-done.2
  720.5 4.3 fusion.294
  727.1 27.3 %reduce-scatter.39.cloned.1.call-done = f32[512,64]{0,1:T(8,128)} async-done(((f32[512,512]{0,1:T(8,128)}), f32[512,64]{0,1:T(8,128)}) %reduce-scatter.39.cloned.1.call-update) | async-done | bytes 131088 | tf_op jit(solution)/shard_map/while/body/eval_jaxpr/reduce_scatter | solution.py:95
  755.4 64.9 %reduce-scatter.37.cloned.1.call-done = f32[64,512]{1,0:T(8,128)} async-done(((f32[512,512]{1,0:T(8,128)}), f32[64,512]{1,0:T(8,128)}) %reduce-scatter.37.cloned.1.call-update) | async-done | bytes 131088 | tf_op jit(solution)/shard_map/while/body/eval_jaxpr/reduce_scatter | solution.py:94
  821.4 45.0 %reduce-scatter.43.cloned.1.call-done = f32[512,512]{1,0:T(8,128)} async-done(((f32[2048,512]{1,0:T(8,128)}), f32[512,512]{1,0:T(8,128)}) %reduce-scatter.43.cloned.1.call-update) | async-done | bytes 1048592 | tf_op jit(solution)/shard_map/while/body/eval_jaxpr/reduce_scatter | solution.py:264
  872.2 58.8 %reduce-scatter.35.cloned.1.call-done = f32[128,64]{0,1:T(8,128)} async-done(((f32[128,512]{0,1:T(8,128)}), f32[128,64]{0,1:T(8,128)}) %reduce-scatter.35.cloned.1.call-update) | async-done | bytes 32784 | tf_op jit(solution)/shard_map/while/body/eval_jaxpr/reduce_scatter | solution.py:93
  931.8 62.7 %reduce-scatter.29.cloned.1.call-done = f32[64,128]{1,0:T(8,128)} async-done(((f32[512,128]{1,0:T(8,128)}), f32[64,128]{1,0:T(8,128)}) %reduce-scatter.29.cloned.1.call-update) | async-done | bytes 32784 | tf_op jit(solution)/shard_map/while/body/eval_jaxpr/reduce_scatter | solution.py:90
  995.8 62.2 %reduce-scatter.31.cloned.1.call-done = f32[64,128]{1,0:T(8,128)} async-done(((f32[512,128]{1,0:T(8,128)}), f32[64,128]{1,0:T(8,128)}) %reduce-scatter.31.cloned.1.call-update) | async-done | bytes 32784 | tf_op jit(solution)/shard_map/while/body/eval_jaxpr/reduce_scatter | solution.py:91
  1058.8 62.7 %reduce-scatter.33.cloned.1.call-done = f32[64,128]{1,0:T(8,128)} async-done(((f32[512,128]{1,0:T(8,128)}), f32[64,128]{1,0:T(8,128)}) %reduce-scatter.33.cloned.1.call-update) | async-done | bytes 32784 | tf_op jit(solution)/shard_map/while/body/eval_jaxpr/reduce_scatter | solution.py:92
  1122.2 45.1 %reduce-scatter.41.cloned.1.call-done = f32[512,512]{1,0:T(8,128)} async-done(((f32[2048,512]{1,0:T(8,128)}), f32[512,512]{1,0:T(8,128)}) %reduce-scatter.41.cloned.1.call-update) | async-done | bytes 1048592 | tf_op jit(solution)/shard_map/while/body/eval_jaxpr/reduce_scatter | solution.py:373
  1184.8 30.6 %all_gather.116 = bf16[128,512]{0,1:T(8,128)(2,1)S(1)} all-gather(bf16[128,64]{0,1:T(8,128)(2,1)S(1)} %copy-done.51), channel_id=1, replica_groups=mesh['seq'=8,'mp'=4] {'seq'}, dimensions={1}, use_global_device_ids=true | all-gather | bytes 147456 | tf_op jit(solution)/shard_map/while/body/eval_jaxpr/all_gather | solution.py:81
  1215.4 30.5 %all_gather.113 = bf16[512,128]{1,0:T(8,128)(2,1)S(1)} all-gather(bf16[64,128]{1,0:T(8,128)(2,1)S(1)} %copy-done.50), channel_id=1, replica_groups=mesh['seq'=8,'mp'=4] {'seq'}, dimensions={0}, use_global_device_ids=true | all-gather | bytes 147456 | tf_op jit(solution)/shard_map/while/body/eval_jaxpr/all_gather | solution.py:80
  1245.9 30.5 %all_gather.112 = bf16[512,128]{1,0:T(8,128)(2,1)S(1)} all-gather(bf16[64,128]{1,0:T(8,128)(2,1)S(1)} %copy-done.49), channel_id=1, replica_groups=mesh['seq'=8,'mp'=4] {'seq'}, dimensions={0}, use_global_device_ids=true | all-gather | bytes 147456 | tf_op jit(solution)/shard_map/while/body/eval_jaxpr/all_gather | solution.py:79
  1276.4 30.5 %all_gather.111 = bf16[512,128]{1,0:T(8,128)(2,1)S(1)} all-gather(bf16[64,128]{1,0:T(8,128)(2,1)S(1)} %copy-done.48), channel_id=1, replica_groups=mesh['seq'=8,'mp'=4] {'seq'}, dimensions={0}, use_global_device_ids=true | all-gather | bytes 147456 | tf_op jit(solution)/shard_map/while/body/eval_jaxpr/all_gather | solution.py:78
  1321.2 33.6 %all_gather.114 = bf16[128,128]{1,0:T(8,128)(2,1)S(1)} all-gather(bf16[16,128]{1,0:T(8,128)(2,1)S(1)} %get-tuple-element.2383), channel_id=1, replica_groups=mesh['seq'=8,'mp'=4] {'seq'}, dimensions={0}, use_global_device_ids=true | all-gather | bytes 36864 | tf_op jit(solution)/shard_map/while/body/eval_jaxpr/all_gather | solution.py:186
  1354.9 30.4 %all_gather.115 = bf16[128,128]{1,0:T(8,128)(2,1)S(1)} all-gather(bf16[16,128]{1,0:T(8,128)(2,1)S(1)} %get-tuple-element.2384), channel_id=1, replica_groups=mesh['seq'=8,'mp'=4] {'seq'}, dimensions={0}, use_global_device_ids=true | all-gather | bytes 36864 | tf_op jit(solution)/shard_map/while/body/eval_jaxpr/all_gather | solution.py:187
  1385.4 41.4 %while.135 = (s32[]{:T(128)}, bf16[4,512,128]{2,1,0:T(8,128)(2,1)S(1)}, f32[4,2,512]{2,1,0:T(2,128)}, s32[4]{0:T(128)S(1)}, bf16[2176,128]{0,1:T(8,128)(2,1)}, /...) while((s32[]{:T(128)}, ...), condition=%wide.region_15.15_spmd, body=%wide.region_8.14_spmd.sunk | while | flops 212580736 | bytes 13743748 | solution.py:248
  1430.4 42.2 %reduce-scatter.21.cloned.1.call-done = f32[512,512]{1,0:T(8,128)} async-done(((f32[2048,512]{1,0:T(8,128)}), f32[512,512]{1,0:T(8,128)}) %reduce-scatter.21.cloned.1.call-update) | async-done | bytes 1048592 | tf_op jit(solution)/shard_map/while/body/eval_jaxpr/reduce_scatter | solution.py:250
  1475.5 31.4 %all_gather.118 = bf16[512,512]{1,0:T(8,128)(2,1)S(1)} all-gather(bf16[64,512]{1,0:T(8,128)(2,1)S(1)} %copy-done.31), channel_id=1, replica_groups=mesh['seq'=8,'mp'=4] {'seq'}, dimensions={0}, use_global_device_ids=true | all-gather | bytes 589824 | tf_op jit(solution)/shard_map/while/body/eval_jaxpr/all_gather | solution.py:82
  1506.9 33.3 %all_gather.119 = bf16[512,512]{0,1:T(8,128)(2,1)} all-gather(bf16[512,64]{0,1:T(8,128)(2,1)S(1)} %copy-done.30), channel_id=1, replica_groups=mesh['seq'=8,'mp'=4] {'seq'}, dimensions={1}, use_global_device_ids=true | all-gather | bytes 589824 | tf_op jit(solution)/shard_map/while/body/eval_jaxpr/all_gather | solution.py:83
  1543.3 5.4 convert_reduce_fusion.32
  1552.1 45.1 %reduce-scatter.23.cloned.1.call-done = f32[512,512]{1,0:T(8,128)} async-done(((f32[2048,512]{1,0:T(8,128)}), f32[512,512]{1,0:T(8,128)}) %reduce-scatter.23.cloned.1.call-update) | async-done | bytes 1048592 | tf_op jit(solution)/shard_map/while/body/eval_jaxpr/reduce_scatter | solution.py:281
  1603.7 22.7 all-gather.8.cloned.1.call-done
  1631.6 89.4 %while.136 = (s32[]{:T(128)}, f32[2176,128]{1,0:T(8,128)}, f32[2176,128]{1,0:T(8,128)}, f32[128,128]{0,1:T(8,128)}, f32[128,128]{0,1:T(8,128)S(1)}, /*index=5*/b...) while((s32[]{:T(128)}, f32[2176,128]{1,0:T(8,128)}, ...), condition=%wide.region_27.27_spmd.clone, body=%wide.region_22.26_spmd.clone.sunk | while | flops 513129984 | bytes 38946836 | solution.py:352
  1723.5 6.0 fusion.293
  1729.5 3.9 fusion.292
  1733.5 6.1 fusion.297
  1740.3 43.8 %reduce-scatter.25.cloned.1.call-done = f32[16,128]{1,0:T(8,128)} async-done(((f32[128,128]{1,0:T(8,128)}), f32[16,128]{1,0:T(8,128)}) %reduce-scatter.25.cloned.1.call-update) | async-done | bytes 8208 | tf_op jit(solution)/shard_map/while/body/eval_jaxpr/reduce_scatter | solution.py:357
  1784.0 63.7 %reduce-scatter.27.cloned.1.call-done = f32[16,128]{1,0:T(8,128)} async-done(((f32[128,128]{1,0:T(8,128)}), f32[16,128]{1,0:T(8,128)}) %reduce-scatter.27.cloned.1.call-update) | async-done | bytes 8208 | tf_op jit(solution)/shard_map/while/body/eval_jaxpr/reduce_scatter | solution.py:358
  1850.3 4.8 dynamic_update_slice.115
  1862.9 4.8 dynamic_update_slice.114
  1869.7 4.8 collective-permute-done.2
  1880.4 4.3 fusion.294
  1887.0 27.1 %reduce-scatter.39.cloned.1.call-done = f32[512,64]{0,1:T(8,128)} async-done(((f32[512,512]{0,1:T(8,128)}), f32[512,64]{0,1:T(8,128)}) %reduce-scatter.39.cloned.1.call-update) | async-done | bytes 131088 | tf_op jit(solution)/shard_map/while/body/eval_jaxpr/reduce_scatter | solution.py:95
  1915.1 64.8 %reduce-scatter.37.cloned.1.call-done = f32[64,512]{1,0:T(8,128)} async-done(((f32[512,512]{1,0:T(8,128)}), f32[64,512]{1,0:T(8,128)}) %reduce-scatter.37.cloned.1.call-update) | async-done | bytes 131088 | tf_op jit(solution)/shard_map/while/body/eval_jaxpr/reduce_scatter | solution.py:94
  1981.0 45.1 %reduce-scatter.43.cloned.1.call-done = f32[512,512]{1,0:T(8,128)} async-done(((f32[2048,512]{1,0:T(8,128)}), f32[512,512]{1,0:T(8,128)}) %reduce-scatter.43.cloned.1.call-update) | async-done | bytes 1048592 | tf_op jit(solution)/shard_map/while/body/eval_jaxpr/reduce_scatter | solution.py:264
  2031.9 58.8 %reduce-scatter.35.cloned.1.call-done = f32[128,64]{0,1:T(8,128)} async-done(((f32[128,512]{0,1:T(8,128)}), f32[128,64]{0,1:T(8,128)}) %reduce-scatter.35.cloned.1.call-update) | async-done | bytes 32784 | tf_op jit(solution)/shard_map/while/body/eval_jaxpr/reduce_scatter | solution.py:93
  2091.4 62.7 %reduce-scatter.29.cloned.1.call-done = f32[64,128]{1,0:T(8,128)} async-done(((f32[512,128]{1,0:T(8,128)}), f32[64,128]{1,0:T(8,128)}) %reduce-scatter.29.cloned.1.call-update) | async-done | bytes 32784 | tf_op jit(solution)/shard_map/while/body/eval_jaxpr/reduce_scatter | solution.py:90
  2155.5 62.3 %reduce-scatter.31.cloned.1.call-done = f32[64,128]{1,0:T(8,128)} async-done(((f32[512,128]{1,0:T(8,128)}), f32[64,128]{1,0:T(8,128)}) %reduce-scatter.31.cloned.1.call-update) | async-done | bytes 32784 | tf_op jit(solution)/shard_map/while/body/eval_jaxpr/reduce_scatter | solution.py:91
  2218.5 62.9 %reduce-scatter.33.cloned.1.call-done = f32[64,128]{1,0:T(8,128)} async-done(((f32[512,128]{1,0:T(8,128)}), f32[64,128]{1,0:T(8,128)}) %reduce-scatter.33.cloned.1.call-update) | async-done | bytes 32784 | tf_op jit(solution)/shard_map/while/body/eval_jaxpr/reduce_scatter | solution.py:92
  2282.1 45.2 %reduce-scatter.41.cloned.1.call-done = f32[512,512]{1,0:T(8,128)} async-done(((f32[2048,512]{1,0:T(8,128)}), f32[512,512]{1,0:T(8,128)}) %reduce-scatter.41.cloned.1.call-update) | async-done | bytes 1048592 | tf_op jit(solution)/shard_map/while/body/eval_jaxpr/reduce_scatter | solution.py:373
  2334.0 40.4 %all-reduce = (f32[512]{0:T(512)}, f32[512]{0:T(512)}, f32[512]{0:T(512)}, f32[512]{0:T(512)}, f32[512]{0:T(512)}, /*index=5*/f32[512]{0:T(512)}, f32[512]{0:T(512)}, f32[2048]{0:T(1024)}, f32[512]{0:T(512)}) all-reduce(f32[512]{0:T(512)} %get-tuple-element.1259, ...), channel_id=1, replica_groups=mesh['seq'=8,'mp'=4] {'seq','mp'}, use_global_device_ids=true, to_apply=%region_50.51 | all-reduce | flops 6144 | bytes 49152 | tf_op jit(solution)/shard_map/psum | solution.py:467
  (1184 shorter events, 427.8 us)
Async XLA Ops:
  12.0 135.3 %all-gather.4.cloned.1.call-start = ((), (), s32[]{:S(2)}) async-start(), calls=%async_computation.12 | async-start | bytes 2621440 | tf_op jit(solution)/shard_map/while/body/eval_jaxpr/all_gather | solution.py:150
  17.8 295.2 %reduce-scatter.21.cloned.1.call-start = ((), (), s32[]{:S(2)}) async-start(), calls=%async_computation.13 | async-start | bytes 5242880 | tf_op jit(solution)/shard_map/while/body/eval_jaxpr/reduce_scatter | solution.py:250
  150.2 6.8 collective-permute-start.1
  155.1 3.5 collective-permute-start
  269.9 110.9 %all-gather.6.cloned.1.call-start = ((), (), s32[]{:S(2)}) async-start(), calls=%async_computation.14 | async-start | bytes 2621440 | tf_op jit(solution)/shard_map/while/body/eval_jaxpr/all_gather | solution.py:258
  315.9 121.6 %reduce-scatter.23.cloned.1.call-start = ((), (), s32[]{:S(2)}) async-start(), calls=%async_computation.15 | async-start | bytes 5242880 | tf_op jit(solution)/shard_map/while/body/eval_jaxpr/reduce_scatter | solution.py:281
  392.6 74.2 %all-gather.8.cloned.1.call-start = ((), (), s32[]{:S(2)}) async-start(), calls=%async_computation.16 | async-start | bytes 2621440 | tf_op jit(solution)/shard_map/while/body/eval_jaxpr/all_gather | solution.py:288
  444.0 180.4 %reduce-scatter.25.cloned.1.call-start = ((), (), s32[]{:S(2)}) async-start(), calls=%async_computation.17 | async-start | bytes 73728 | tf_op jit(solution)/shard_map/while/body/eval_jaxpr/reduce_scatter | solution.py:357
  563.0 125.2 %reduce-scatter.27.cloned.1.call-start = ((), (), s32[]{:S(2)}) async-start(), calls=%async_computation.18 | async-start | bytes 73728 | tf_op jit(solution)/shard_map/while/body/eval_jaxpr/reduce_scatter | solution.py:358
  563.8 190.6 %reduce-scatter.39.cloned.1.call-start = ((), (), s32[]{:S(2)}) async-start(), calls=%async_computation.24 | async-start | bytes 1179648 | tf_op jit(solution)/shard_map/while/body/eval_jaxpr/reduce_scatter | solution.py:95
  569.9 250.4 %reduce-scatter.37.cloned.1.call-start = ((), (), s32[]{:S(2)}) async-start(), calls=%async_computation.23 | async-start | bytes 1179648 | tf_op jit(solution)/shard_map/while/body/eval_jaxpr/reduce_scatter | solution.py:94
  573.8 292.6 %reduce-scatter.43.cloned.1.call-start = ((), (), s32[]{:S(2)}) async-start(), calls=%async_computation.26 | async-start | bytes 5242880 | tf_op jit(solution)/shard_map/while/body/eval_jaxpr/reduce_scatter | solution.py:264
  580.0 351.0 %reduce-scatter.35.cloned.1.call-start = ((), (), s32[]{:S(2)}) async-start(), calls=%async_computation.22 | async-start | bytes 294912 | tf_op jit(solution)/shard_map/while/body/eval_jaxpr/reduce_scatter | solution.py:93
  695.5 13.9 collective-permute-start.3
  702.3 292.2 %reduce-scatter.29.cloned.1.call-start = ((), (), s32[]{:S(2)}) async-start(), calls=%async_computation.19 | async-start | bytes 294912 | tf_op jit(solution)/shard_map/while/body/eval_jaxpr/reduce_scatter | solution.py:90
  708.0 6.7 collective-permute-start.2
  719.1 338.9 %reduce-scatter.31.cloned.1.call-start = ((), (), s32[]{:S(2)}) async-start(), calls=%async_computation.20 | async-start | bytes 294912 | tf_op jit(solution)/shard_map/while/body/eval_jaxpr/reduce_scatter | solution.py:91
  719.9 401.6 %reduce-scatter.33.cloned.1.call-start = ((), (), s32[]{:S(2)}) async-start(), calls=%async_computation.21 | async-start | bytes 294912 | tf_op jit(solution)/shard_map/while/body/eval_jaxpr/reduce_scatter | solution.py:92
  720.4 446.9 %reduce-scatter.41.cloned.1.call-start = ((), (), s32[]{:S(2)}) async-start(), calls=%async_computation.25 | async-start | bytes 5242880 | tf_op jit(solution)/shard_map/while/body/eval_jaxpr/reduce_scatter | solution.py:373
  724.9 333.1 %copy-start.41 = (f32[64,128]{1,0:T(8,128)S(1)}, f32[64,128]{1,0:T(8,128)}, u32[]{:S(2)}) copy-start(f32[64,128]{1,0:T(8,128)} %get-tuple-element.2661) | copy-start | bytes 98308 | tf_op jit(solution)/shard_map/while
  725.0 396.5 %copy-start.39 = (f32[64,128]{1,0:T(8,128)S(1)}, f32[64,128]{1,0:T(8,128)}, u32[]{:S(2)}) copy-start(f32[64,128]{1,0:T(8,128)} %get-tuple-element.2662) | copy-start | bytes 98308 | tf_op jit(solution)/shard_map/while
  725.0 442.4 %copy-start.4 = (bf16[2,512,512]{2,1,0:T(8,128)(2,1)S(1)}, bf16[2,512,512]{2,1,0:T(8,128)(2,1)}, u32[]{:S(2)}) copy-start(bf16[2,512,512]{2,1,0:T(8,128)(2,1)} %get-tuple-element.2736) | copy-start | bytes 3145732 | tf_op jit(solution)/shard_map/while
  725.0 442.4 %copy-start.34 = (f32[512]{0:T(512)S(1)}, f32[512]{0:T(512)}, u32[]{:S(2)}) copy-start(f32[512]{0:T(512)} %get-tuple-element.2737) | copy-start | bytes 6148 | tf_op jit(solution)/shard_map/while
  755.4 413.6 %copy-start.27 = (f32[512,64]{0,1:T(8,128)}, f32[512,64]{0,1:T(8,128)S(1)}, u32[]{:S(2)}) copy-start(f32[512,64]{0,1:T(8,128)S(1)} %select_add_fusion.27) | copy-start | bytes 393220 | tf_op jit(solution)/shard_map/while
  821.3 347.8 %copy-start.29 = (f32[64,512]{1,0:T(8,128)}, f32[64,512]{1,0:T(8,128)S(1)}, u32[]{:S(2)}) copy-start(f32[64,512]{1,0:T(8,128)S(1)} %select_add_fusion.26) | copy-start | bytes 393220 | tf_op jit(solution)/shard_map/while
  821.4 347.7 %copy-start.58 = (f32[512]{0:T(512)}, f32[512]{0:T(512)S(1)}, u32[]{:S(2)}) copy-start(f32[512]{0:T(512)S(1)} %get-tuple-element.2731) | copy-start | bytes 6148 | tf_op jit(solution)/shard_map/while
  821.4 347.7 %copy-start.60 = (f32[512]{0:T(512)}, f32[512]{0:T(512)S(1)}, u32[]{:S(2)}) copy-start(f32[512]{0:T(512)S(1)} %get-tuple-element.2730) | copy-start | bytes 6148 | tf_op jit(solution)/shard_map/while
  866.5 302.6 %copy-start.44 = (f32[512]{0:T(512)S(1)}, f32[512]{0:T(512)}, u32[]{:S(2)}) copy-start(f32[512]{0:T(512)} %copy-done.43) | copy-start | bytes 6148 | tf_op jit(solution)/shard_map/while
  866.5 302.7 %copy-start.36 = (f32[512]{0:T(512)S(1)}, f32[512]{0:T(512)}, u32[]{:S(2)}) copy-start(f32[512]{0:T(512)} %copy-done.35) | copy-start | bytes 6148 | tf_op jit(solution)/shard_map/while
  868.7 302.3 %copy-start.7 = (f32[512,512]{1,0:T(8,128)S(1)}, f32[512,512]{1,0:T(8,128)}, u32[]{:S(2)}) copy-start(f32[512,512]{1,0:T(8,128)} %copy-done.6) | copy-start | bytes 3145732 | tf_op jit(solution)/shard_map/while
  868.8 302.3 %copy-start.46 = (f32[512]{0:T(512)S(1)}, f32[512]{0:T(512)}, u32[]{:S(2)}) copy-start(f32[512]{0:T(512)} %copy-done.45) | copy-start | bytes 6148 | tf_op jit(solution)/shard_map/while
  868.9 302.1 %copy-start.65 = (f32[512]{0:T(512)S(1)}, f32[512]{0:T(512)}, u32[]{:S(2)}) copy-start(f32[512]{0:T(512)} %get-tuple-element.2666) | copy-start | bytes 6148 | tf_op jit(solution)/shard_map/while
  1174.2 133.5 %all-gather.4.cloned.1.call-start = ((), (), s32[]{:S(2)}) async-start(), calls=%async_computation.12 | async-start | bytes 2621440 | tf_op jit(solution)/shard_map/while/body/eval_jaxpr/all_gather | solution.py:150
  1180.1 292.5 %reduce-scatter.21.cloned.1.call-start = ((), (), s32[]{:S(2)}) async-start(), calls=%async_computation.13 | async-start | bytes 5242880 | tf_op jit(solution)/shard_map/while/body/eval_jaxpr/reduce_scatter | solution.py:250
  1310.7 6.8 collective-permute-start.1
  1315.6 3.5 collective-permute-start
  1430.4 109.9 %all-gather.6.cloned.1.call-start = ((), (), s32[]{:S(2)}) async-start(), calls=%async_computation.14 | async-start | bytes 2621440 | tf_op jit(solution)/shard_map/while/body/eval_jaxpr/all_gather | solution.py:258
  1475.4 121.7 %reduce-scatter.23.cloned.1.call-start = ((), (), s32[]{:S(2)}) async-start(), calls=%async_computation.15 | async-start | bytes 5242880 | tf_op jit(solution)/shard_map/while/body/eval_jaxpr/reduce_scatter | solution.py:281
  1552.0 74.4 %all-gather.8.cloned.1.call-start = ((), (), s32[]{:S(2)}) async-start(), calls=%async_computation.16 | async-start | bytes 2621440 | tf_op jit(solution)/shard_map/while/body/eval_jaxpr/all_gather | solution.py:288
  1603.6 180.4 %reduce-scatter.25.cloned.1.call-start = ((), (), s32[]{:S(2)}) async-start(), calls=%async_computation.17 | async-start | bytes 73728 | tf_op jit(solution)/shard_map/while/body/eval_jaxpr/reduce_scatter | solution.py:357
  1722.6 125.1 %reduce-scatter.27.cloned.1.call-start = ((), (), s32[]{:S(2)}) async-start(), calls=%async_computation.18 | async-start | bytes 73728 | tf_op jit(solution)/shard_map/while/body/eval_jaxpr/reduce_scatter | solution.py:358
  1723.4 190.7 %reduce-scatter.39.cloned.1.call-start = ((), (), s32[]{:S(2)}) async-start(), calls=%async_computation.24 | async-start | bytes 1179648 | tf_op jit(solution)/shard_map/while/body/eval_jaxpr/reduce_scatter | solution.py:95
  1729.5 250.4 %reduce-scatter.37.cloned.1.call-start = ((), (), s32[]{:S(2)}) async-start(), calls=%async_computation.23 | async-start | bytes 1179648 | tf_op jit(solution)/shard_map/while/body/eval_jaxpr/reduce_scatter | solution.py:94
  1733.5 292.6 %reduce-scatter.43.cloned.1.call-start = ((), (), s32[]{:S(2)}) async-start(), calls=%async_computation.26 | async-start | bytes 5242880 | tf_op jit(solution)/shard_map/while/body/eval_jaxpr/reduce_scatter | solution.py:264
  1739.6 351.0 %reduce-scatter.35.cloned.1.call-start = ((), (), s32[]{:S(2)}) async-start(), calls=%async_computation.22 | async-start | bytes 294912 | tf_op jit(solution)/shard_map/while/body/eval_jaxpr/reduce_scatter | solution.py:93
  1855.1 14.0 collective-permute-start.3
  1862.0 292.1 %reduce-scatter.29.cloned.1.call-start = ((), (), s32[]{:S(2)}) async-start(), calls=%async_computation.19 | async-start | bytes 294912 | tf_op jit(solution)/shard_map/while/body/eval_jaxpr/reduce_scatter | solution.py:90
  1867.8 6.7 collective-permute-start.2
  1878.9 338.9 %reduce-scatter.31.cloned.1.call-start = ((), (), s32[]{:S(2)}) async-start(), calls=%async_computation.20 | async-start | bytes 294912 | tf_op jit(solution)/shard_map/while/body/eval_jaxpr/reduce_scatter | solution.py:91
  1879.6 401.7 %reduce-scatter.33.cloned.1.call-start = ((), (), s32[]{:S(2)}) async-start(), calls=%async_computation.21 | async-start | bytes 294912 | tf_op jit(solution)/shard_map/while/body/eval_jaxpr/reduce_scatter | solution.py:92
  1880.3 446.9 %reduce-scatter.41.cloned.1.call-start = ((), (), s32[]{:S(2)}) async-start(), calls=%async_computation.25 | async-start | bytes 5242880 | tf_op jit(solution)/shard_map/while/body/eval_jaxpr/reduce_scatter | solution.py:373
  1884.8 332.9 %copy-start.41 = (f32[64,128]{1,0:T(8,128)S(1)}, f32[64,128]{1,0:T(8,128)}, u32[]{:S(2)}) copy-start(f32[64,128]{1,0:T(8,128)} %get-tuple-element.2661) | copy-start | bytes 98308 | tf_op jit(solution)/shard_map/while
  1884.9 396.5 %copy-start.39 = (f32[64,128]{1,0:T(8,128)S(1)}, f32[64,128]{1,0:T(8,128)}, u32[]{:S(2)}) copy-start(f32[64,128]{1,0:T(8,128)} %get-tuple-element.2662) | copy-start | bytes 98308 | tf_op jit(solution)/shard_map/while
  1884.9 442.4 %copy-start.4 = (bf16[2,512,512]{2,1,0:T(8,128)(2,1)S(1)}, bf16[2,512,512]{2,1,0:T(8,128)(2,1)}, u32[]{:S(2)}) copy-start(bf16[2,512,512]{2,1,0:T(8,128)(2,1)} %get-tuple-element.2736) | copy-start | bytes 3145732 | tf_op jit(solution)/shard_map/while
  1884.9 442.4 %copy-start.34 = (f32[512]{0:T(512)S(1)}, f32[512]{0:T(512)}, u32[]{:S(2)}) copy-start(f32[512]{0:T(512)} %get-tuple-element.2737) | copy-start | bytes 6148 | tf_op jit(solution)/shard_map/while
  1915.1 413.9 %copy-start.27 = (f32[512,64]{0,1:T(8,128)}, f32[512,64]{0,1:T(8,128)S(1)}, u32[]{:S(2)}) copy-start(f32[512,64]{0,1:T(8,128)S(1)} %select_add_fusion.27) | copy-start | bytes 393220 | tf_op jit(solution)/shard_map/while
  1980.8 348.2 %copy-start.29 = (f32[64,512]{1,0:T(8,128)}, f32[64,512]{1,0:T(8,128)S(1)}, u32[]{:S(2)}) copy-start(f32[64,512]{1,0:T(8,128)S(1)} %select_add_fusion.26) | copy-start | bytes 393220 | tf_op jit(solution)/shard_map/while
  1980.9 348.1 %copy-start.58 = (f32[512]{0:T(512)}, f32[512]{0:T(512)S(1)}, u32[]{:S(2)}) copy-start(f32[512]{0:T(512)S(1)} %get-tuple-element.2731) | copy-start | bytes 6148 | tf_op jit(solution)/shard_map/while
  1980.9 348.1 %copy-start.60 = (f32[512]{0:T(512)}, f32[512]{0:T(512)S(1)}, u32[]{:S(2)}) copy-start(f32[512]{0:T(512)S(1)} %get-tuple-element.2730) | copy-start | bytes 6148 | tf_op jit(solution)/shard_map/while
  2026.1 302.9 %copy-start.44 = (f32[512]{0:T(512)S(1)}, f32[512]{0:T(512)}, u32[]{:S(2)}) copy-start(f32[512]{0:T(512)} %copy-done.43) | copy-start | bytes 6148 | tf_op jit(solution)/shard_map/while
  2026.1 302.9 %copy-start.36 = (f32[512]{0:T(512)S(1)}, f32[512]{0:T(512)}, u32[]{:S(2)}) copy-start(f32[512]{0:T(512)} %copy-done.35) | copy-start | bytes 6148 | tf_op jit(solution)/shard_map/while
  2028.4 302.6 %copy-start.7 = (f32[512,512]{1,0:T(8,128)S(1)}, f32[512,512]{1,0:T(8,128)}, u32[]{:S(2)}) copy-start(f32[512,512]{1,0:T(8,128)} %copy-done.6) | copy-start | bytes 3145732 | tf_op jit(solution)/shard_map/while
  2028.4 302.6 %copy-start.46 = (f32[512]{0:T(512)S(1)}, f32[512]{0:T(512)}, u32[]{:S(2)}) copy-start(f32[512]{0:T(512)} %copy-done.45) | copy-start | bytes 6148 | tf_op jit(solution)/shard_map/while
  2028.6 302.4 %copy-start.65 = (f32[512]{0:T(512)S(1)}, f32[512]{0:T(512)}, u32[]{:S(2)}) copy-start(f32[512]{0:T(512)} %get-tuple-element.2666) | copy-start | bytes 6148 | tf_op jit(solution)/shard_map/while
  (182 other events, 6442.7 us)
Sparse Core Ops, SparseCore 0:
  18.0 25.2 all-gather.3
  270.0 43.0 reduce-scatter.20
  316.0 22.5 all-gather.5
  392.7 44.7 reduce-scatter.22
  444.2 22.5 all-gather.7
  563.1 61.2 reduce-scatter.24
  627.9 60.2 reduce-scatter.26
  692.0 62.4 reduce-scatter.38
  757.9 62.3 reduce-scatter.36
  822.9 43.5 reduce-scatter.42
  869.8 61.1 reduce-scatter.34
  934.2 60.2 reduce-scatter.28
  997.8 60.1 reduce-scatter.30
  1061.2 60.2 reduce-scatter.32
  1123.8 43.4 reduce-scatter.40
  1180.2 22.5 all-gather.3
  1430.5 42.0 reduce-scatter.20
  1475.5 22.5 all-gather.5
  1552.1 44.9 reduce-scatter.22
  1603.8 22.5 all-gather.7
  1722.7 61.2 reduce-scatter.24
  1787.4 60.2 reduce-scatter.26
  1851.5 62.5 reduce-scatter.38
  1917.4 62.4 reduce-scatter.36
  1982.6 43.5 reduce-scatter.42
  2029.3 61.2 reduce-scatter.34
  2093.8 60.2 reduce-scatter.28
  2157.4 60.2 reduce-scatter.30
  2221.1 60.2 reduce-scatter.32
  2283.7 43.5 reduce-scatter.40
where the time goes:
time: 2390 us; the launch traced here: 2380 us
  waiting for transfers between devices  1310 us (55%)
  blocking collectives  544 us (23%)
  local copies, waits for them, and re-layouts  188 us (8%)
  matrix products  149 us (6%)
  other arithmetic  140 us (6%)
    reduce_scatter x2, waiting for transfers between devices, reduce_weights(): lax.psum_scatter(grad_up, 'seq', scatter_dimension=0, tiled=True)  130 us
    reduce_scatter x2, waiting for transfers between devices, micro_step(): lax.psum_scatter(summ_gv, 'seq', scatter_dimension=0, tiled=True)  127 us
    reduce_scatter x2, waiting for transfers between devices, reduce_weights(): lax.psum_scatter(grad_value, 'seq', scatter_dimension=0, tiled=True)  126 us
    reduce_scatter x2, waiting for transfers between devices, reduce_weights(): lax.psum_scatter(grad_query, 'seq', scatter_dimension=0, tiled=True)  125 us
    reduce_scatter x2, waiting for transfers between devices, reduce_weights(): lax.psum_scatter(grad_key, 'seq', scatter_dimension=0, tiled=True)  124 us
    reduce_scatter x2, waiting for transfers between devices, reduce_weights(): lax.psum_scatter(grad_out, 'seq', scatter_dimension=1, tiled=True)  118 us
    reduce_scatter x2, waiting for transfers between devices, micro_step(): lax.psum_scatter(contract_cols(grad_qkv, w_qkv), 'mp', scatter_dimension=...  90.3 us
    reduce_scatter x2, waiting for transfers between devices, micro_step(): lax.psum_scatter(jnp.dot(lax.slice_in_dim(activated, 0, local_row_block *...  90.2 us
  transfers between devices with their start and end apart: 38, of which 30 were waited for; matrix products, arithmetic and copies ran while one was open for 5% of the time, Pallas kernels for 0%

commit v1 on v0

v1 whole, which is shorter than its diff:
```python
from functools import partial
import math

import jax
import jax.numpy as jnp
from jax import lax
from jax.experimental import pallas as pl
from jax.experimental.pallas import tpu as pltpu
from jax.sharding import PartitionSpec as P

D = 512
FF = 2048
HEAD_DIM = 64
SPAN = 128
LANES = 128
EPSILON = 1e-05
NEGATIVE = -1e30
SCALE = 1.0 / math.sqrt(HEAD_DIM)
F32 = jnp.float32
BF16 = jnp.bfloat16
AXES = ("seq", "mp")
MIB = 1 << 20
VMEM = pl.BlockSpec(memory_space=pltpu.VMEM)
SMEM = pl.BlockSpec(memory_space=pltpu.SMEM)
ANY = pl.BlockSpec(memory_space=pl.ANY)


def dot(left, right):
    return lax.dot_general(left, right, (((1,), (0,)), ((), ())), preferred_element_type=F32)


def dot_cols(left, right):
    return lax.dot_general(left, right, (((1,), (1,)), ((), ())), preferred_element_type=F32)


def unit(rows):
    centred = rows - jnp.mean(rows, axis=-1, keepdims=True)
    inverse = lax.rsqrt(jnp.mean(centred * centred, axis=-1, keepdims=True) + EPSILON)
    return centred * inverse, inverse


def unit_back(grad, hat, inverse):
    shift = jnp.mean(grad, axis=-1, keepdims=True)
    slope = jnp.mean(grad * hat, axis=-1, keepdims=True)
    return (grad - shift - hat * slope) * inverse


def row_info(info, mi):
    return info[0], info[1 + mi], [info[3 + 8 * mi + c] for c in range(8)]


def doc_start(positions, ends):
    start = jnp.zeros_like(positions)
    for end in ends:
        start = jnp.where(positions >= end, end, start)
    return start


def summary_range(summary_ids, offset, ends):
    last = offset - 1 + SPAN * summary_ids
    first = jnp.maximum(doc_start(last, ends), last - (SPAN - 1))
    return first, last


def iota(shape, dim):
    return lax.broadcasted_iota(jnp.int32, shape, dim)


def summary_kernel(info, x_ref, out_ref):
    rows = x_ref.shape[1]
    sums = []
    for mi in range(2):
        dev, offset, ends = row_info(info, mi)
        first, last = summary_range(dev * (rows // SPAN) + iota((8, 1), 0), offset, ends)
        pos = dev * rows + iota((1, rows), 1)
        member = jnp.where((pos >= first) & (pos <= last), 1.0, 0.0).astype(BF16)
        hat, _ = unit(x_ref[mi].astype(F32))
        high = hat.astype(BF16)
        rest = (hat - high.astype(F32)).astype(BF16)
        total = dot(member, high) + dot(member, rest)
        sums.append(total * lax.rsqrt((last - first + 1).astype(F32)))
    both = jnp.concatenate(sums, axis=0).astype(BF16)
    for lane in range(D // LANES):
        out_ref[16 * lane : 16 * lane + 16, :] = both[:, lane * LANES : (lane + 1) * LANES]


def picker(by):
    return jnp.where(iota((SPAN, 2 * SPAN), 1) == iota((SPAN, 2 * SPAN), 0) + by, 1.0, 0.0).astype(BF16)


def pick_rows(pick, rows):
    high = rows.astype(BF16)
    return dot(pick, high) + dot(pick, (rows - high.astype(F32)).astype(BF16))


def fill_masks(info, bias_ref, tiles, summaries, length):
    for mi in range(2):
        dev, offset, ends = row_info(info, mi)
        ends_col = offset - 1 + SPAN * iota((summaries, 1), 0)
        for t in range(tiles):
            base = SPAN * (dev * tiles + t) + offset - SPAN
            qpos = base + iota((1, SPAN), 1)
            qpos = jnp.where(qpos < 0, qpos + length, qpos)
            kpos = base + iota((SPAN, 1), 0)
            kpos = jnp.where(kpos < 0, kpos + length, kpos)
            span_first = jnp.where(qpos < base, base, jnp.where(qpos >= base + SPAN, base + length, base))
            doc_first = doc_start(qpos, ends)
            local_ok = (kpos >= jnp.maximum(doc_first, span_first)) & (kpos <= qpos)
            summary_ok = (ends_col >= doc_first) & (ends_col < span_first)
            bias_ref[mi, t, 0:SPAN, :] = jnp.where(local_ok, 0.0, NEGATIVE)
            bias_ref[mi, t, SPAN : SPAN + summaries, :] = jnp.where(summary_ok, 0.0, NEGATIVE)


def split_heads(pair):
    low = iota(pair.shape, 1) < HEAD_DIM
    zero = jnp.zeros_like(pair)
    return jnp.concatenate((jnp.where(low, pair, zero), jnp.where(low, zero, pair)), axis=0)


def join_heads(turned):
    half = turned.shape[1] // 2
    return jnp.concatenate((turned[:HEAD_DIM, :half], turned[HEAD_DIM:, half:]), axis=0).T


def attend_kernel(
    apart, info, block_of, row_of, slots_ref, x_ref, left_ref, gain, shift, qbias, vbias, near_ref, far_ref, *refs
):
    if apart:
        all_ref, *refs = refs
    (xs_ref, nb_ref, q_ref, k_ref, v_ref, att_ref, ks_ref, vs_ref, lse_ref, sums_ref, w_ref) = refs[:11]
    stack_ref, wide_ref, bias_ref, sem = refs[11:]
    rows = x_ref.shape[1]
    tiles = rows // SPAN
    summaries = ks_ref.shape[1]
    half, shard, _ = near_ref.shape
    length = summaries * SPAN

    def place(d, carry):
        for source, slot in ((near_ref, d), (far_ref, half + d)):
            first = pl.multiple_of(row_of[slot] * shard, 16)
            pltpu.make_async_copy(
                source.at[d, :, 0:384], w_ref.at[block_of[slot], pl.ds(first, shard), :], sem.at[0]
            ).start()
            if not apart:
                pltpu.make_async_copy(
                    source.at[d, 0:64, 384:512], stack_ref.at[slot], sem.at[1]
                ).start()
        return carry

    lax.fori_loop(0, half, place, 0)
    if apart:
        pltpu.make_async_copy(all_ref, stack_ref, sem.at[1]).start()
    fill_masks(info, bias_ref, tiles, summaries, length)
    for mi in range(2):
        wide_ref[0:SPAN, :] = left_ref[mi]
        wide_ref[SPAN : SPAN + rows, :] = x_ref[mi]
        pick = picker(info[1 + mi])
        for t in range(tiles):
            rolled = dot(pick, wide_ref[t * SPAN : (t + 2) * SPAN, :])
            xs_ref[mi, t * SPAN : (t + 1) * SPAN, :] = rolled.astype(BF16)
            hat, _ = unit(rolled)
            nb_ref[mi, t * SPAN : (t + 1) * SPAN, :] = (hat * gain[...] + shift[...]).astype(BF16)
    pltpu.make_async_copy(stack_ref, stack_ref, sem.at[1]).wait()
    pltpu.make_async_copy(w_ref, w_ref, sem.at[0]).wait()
    for mi in range(2):
        _, offset, ends = row_info(info, mi)
        first, last = summary_range(iota((summaries, 1), 0), offset, ends)
        root = jnp.sqrt((last - first + 1).astype(F32))
        for base in range(0, stack_ref.shape[0], 32):
            named = slots_ref[mi : mi + 1, 16 * base : 16 * base + 512]
            pick = jnp.where(iota((summaries, 1), 0) == named, 1.0, 0.0).astype(BF16)
            for lane in range(D // LANES):
                lanes = slice(lane * LANES, (lane + 1) * LANES)
                piece = stack_ref[base : base + 32, 16 * lane : 16 * lane + 16, :].reshape(512, LANES)
                found = dot(pick, piece)
                sums_ref[mi, :, lanes] = found if base == 0 else sums_ref[mi, :, lanes] + found
        summed = sums_ref[mi] * gain[...] + root * shift[...]
        high = summed.astype(BF16)
        rest = (summed - high.astype(F32)).astype(BF16)
        normed = nb_ref[mi]
        for m in range(4):
            lanes = slice(m * LANES, (m + 1) * LANES)
            w = w_ref[m]
            projected = dot(normed, w)
            q_ref[mi, :, lanes] = (projected[:, :128] + qbias[:, lanes]).astype(BF16)
            k_ref[mi, :, lanes] = projected[:, 128:256].astype(BF16)
            v_ref[mi, :, lanes] = (projected[:, 256:] + vbias[:, lanes]).astype(BF16)
            w_kv = w[:, 128:]
            pooled = dot(high, w_kv) + dot(rest, w_kv)
            ks_ref[mi, :, lanes] = pooled[:, :128].astype(BF16)
            vs_ref[mi, :, lanes] = (pooled[:, 128:] + root * vbias[:, lanes]).astype(BF16)

    def heads(i, carry):
        mi, pair = i // 4, i % 4
        lanes = pl.ds(pl.multiple_of(pair * LANES, LANES), LANES)
        skeys = ks_ref[mi, :, lanes]
        svalues = vs_ref[mi, :, lanes].T
        for t in range(tiles):
            here = slice(t * SPAN, (t + 1) * SPAN)
            queries = split_heads(q_ref[mi, here, lanes] * SCALE)
            keys = jnp.concatenate((k_ref[mi, here, lanes], skeys), axis=0)
            bias = bias_ref[mi, t]
            scores = dot_cols(keys, queries) + jnp.concatenate((bias, bias), axis=1)
            top = jnp.max(scores, axis=0, keepdims=True)
            grown = jnp.exp(scores - top)
            total = jnp.sum(grown, axis=0, keepdims=True)
            probs = (grown * (1.0 / total)).astype(BF16)
            values = jnp.concatenate((v_ref[mi, here, lanes].T, svalues), axis=1)
            att_ref[mi, here, lanes] = join_heads(dot(values, probs)).astype(BF16)
            lse_ref[i, t] = top + jnp.log(total)
        return carry

    lax.fori_loop(0, 8, heads, 0)


def gelu_pair(u):
    c0 = math.sqrt(2.0 / math.pi)
    square = u * u
    t = jnp.tanh(c0 * u * (1.0 + 0.044715 * square))
    half = 0.5 * (1.0 + t)
    slope = half + (0.5 * c0) * u * (1.0 - t * t) * (1.0 + (3 * 0.044715) * square)
    return u * half, slope


def mlp_kernel(
    block_of, row_of, xs_ref, att_ref, x_cot_ref, obias, gain, shift, ubias, dbias, near_ref, far_ref,
    result_ref, gmid_ref, gatt_ref, small_ref, gub_ref, keep_ref, send_ref,
    wo_ref, wu_ref, wd_ref, resid_ref, acc_ref, gn_ref, n_ref, nt_ref, ct_ref, gu_ref, gd_ref, go_ref,
    guw_ref, gdw_ref, gow_ref, sem, out_sem,
):
    total_rows = xs_ref.shape[0]
    half, shard, _ = near_ref.shape
    step = 256
    steps = total_rows // step

    def place(d, carry):
        for source, slot in ((near_ref, d), (far_ref, half + d)):
            rows = pl.ds(pl.multiple_of(row_of[slot] * shard, 16), shard)
            block = block_of[slot]
            narrow = pl.ds(pl.multiple_of(block * 128, 128), 128)
            broad = pl.ds(pl.multiple_of(block * 512, 512), 512)
            pltpu.make_async_copy(source.at[d, :, 0:128], wo_ref.at[rows, narrow], sem.at[0]).start()
            pltpu.make_async_copy(source.at[d, :, 128:640], wu_ref.at[rows, broad], sem.at[1]).start()
            pltpu.make_async_copy(source.at[d, :, 640:1152], wd_ref.at[rows, broad], sem.at[2]).start()
        return carry

    lax.fori_loop(0, half, place, 0)
    small_ref[...] = jnp.zeros_like(small_ref)
    gub_ref[...] = jnp.zeros_like(gub_ref)
    gow_ref[...] = jnp.zeros_like(gow_ref)
    pltpu.make_async_copy(wo_ref, wo_ref, sem.at[0]).wait()

    def first(r, carry):
        rows = pl.ds(pl.multiple_of(r * step, step), step)
        resid = xs_ref[rows, :].astype(F32) + dot_cols(att_ref[rows, :], wo_ref[...]) + obias[...]
        resid_ref[rows, :] = resid
        hat, _ = unit(resid)
        normed = (hat * gain[...] + shift[...]).astype(BF16)
        cot = x_cot_ref[rows, :]
        n_ref[rows, :] = normed
        nt_ref[:, rows] = normed.T
        ct_ref[:, rows] = cot.T
        acc_ref[rows, :] = resid + dbias[...]
        gn_ref[rows, :] = jnp.zeros((step, D), F32)
        small_ref[3:4, :] += jnp.sum(cot.astype(F32), axis=0, keepdims=True)
        return carry

    lax.fori_loop(0, steps, first, 0)
    pltpu.make_async_copy(wu_ref, wu_ref, sem.at[1]).wait()
    pltpu.make_async_copy(wd_ref, wd_ref, sem.at[2]).wait()

    def chunk(ch, carry):
        cols = pl.ds(pl.multiple_of(ch * 512, 512), 512)
        guw_ref[...] = jnp.zeros_like(guw_ref)
        gdw_ref[...] = jnp.zeros_like(gdw_ref)

        def block(r, inner):
            rows = pl.ds(pl.multiple_of(r * step, step), step)
            w_up, w_down = wu_ref[:, cols], wd_ref[:, cols]
            act, slope = gelu_pair(dot(n_ref[rows, :], w_up) + ubias[:, cols])
            act = act.astype(BF16)
            grad = (dot(x_cot_ref[rows, :], w_down) * slope).astype(BF16)
            acc_ref[rows, :] += dot_cols(act, w_down)
            gn_ref[rows, :] += dot_cols(grad, w_up)
            guw_ref[...] += dot(nt_ref[:, rows], grad)
            gdw_ref[...] += dot(ct_ref[:, rows], act)
            gub_ref[:, cols] += jnp.sum(grad.astype(F32), axis=0, keepdims=True)
            return inner

        lax.fori_loop(0, steps, block, 0)
        gu_ref[:, cols] = guw_ref[...].astype(BF16)
        gd_ref[:, cols] = gdw_ref[...].astype(BF16)
        return carry

    lax.fori_loop(0, 4, chunk, 0)

    def last(r, carry):
        rows = pl.ds(pl.multiple_of(r * step, step), step)
        result_ref[rows, :] = acc_ref[rows, :].astype(BF16)
        hat, inverse = unit(resid_ref[rows, :])
        grad = gn_ref[rows, :]
        small_ref[0:1, :] += jnp.sum(grad * hat, axis=0, keepdims=True)
        small_ref[1:2, :] += jnp.sum(grad, axis=0, keepdims=True)
        gmid = x_cot_ref[rows, :].astype(F32) + unit_back(grad * gain[...], hat, inverse)
        gmid_ref[rows, :] = gmid
        branch = gmid.astype(BF16)
        small_ref[2:3, :] += jnp.sum(branch.astype(F32), axis=0, keepdims=True)
        gatt_ref[rows, :] = dot(branch, wo_ref[...]).astype(BF16)
        gow_ref[...] += dot(branch.T, att_ref[rows, :])
        return carry

    lax.fori_loop(0, steps, last, 0)
    go_ref[...] = gow_ref[...].astype(BF16)

    def emit(d, carry):
        for target, slot in ((keep_ref, d), (send_ref, half + d)):
            rows = pl.ds(pl.multiple_of(row_of[slot] * shard, 16), shard)
            block = block_of[slot]
            narrow = pl.ds(pl.multiple_of(block * 128, 128), 128)
            broad = pl.ds(pl.multiple_of(block * 512, 512), 512)
            pltpu.make_async_copy(go_ref.at[rows, narrow], target.at[d, :, 0:128], out_sem.at[0]).start()
            pltpu.make_async_copy(gu_ref.at[rows, broad], target.at[d, :, 128:640], out_sem.at[1]).start()
            pltpu.make_async_copy(gd_ref.at[rows, broad], target.at[d, :, 640:1152], out_sem.at[2]).start()
        return carry

    lax.fori_loop(0, half, emit, 0)
    pltpu.make_async_copy(go_ref, go_ref, out_sem.at[0]).wait()
    pltpu.make_async_copy(gu_ref, gu_ref, out_sem.at[1]).wait()
    pltpu.make_async_copy(gd_ref, gd_ref, out_sem.at[2]).wait()


def attend_back_kernel(
    info, q_ref, k_ref, v_ref, ks_ref, vs_ref, lse_ref, gatt_ref,
    gq_ref, gk_ref, gv_ref, gks_ref, gvs_ref, bias_ref,
):
    rows = q_ref.shape[1]
    tiles = rows // SPAN
    summaries = ks_ref.shape[1]
    fill_masks(info, bias_ref, tiles, summaries, summaries * SPAN)

    def heads(i, carry):
        mi, pair = i // 4, i % 4
        lanes = pl.ds(pl.multiple_of(pair * LANES, LANES), LANES)
        skeys = ks_ref[mi, :, lanes]
        svalues = vs_ref[mi, :, lanes]
        skeys_t = skeys.T
        sum_k = jnp.zeros((summaries, LANES), F32)
        sum_v = jnp.zeros((summaries, LANES), F32)
        for t in range(tiles):
            here = slice(t * SPAN, (t + 1) * SPAN)
            queries = split_heads(q_ref[mi, here, lanes] * SCALE)
            grads = split_heads(gatt_ref[mi, here, lanes])
            own_keys = k_ref[mi, here, lanes]
            keys = jnp.concatenate((own_keys, skeys), axis=0)
            values = jnp.concatenate((v_ref[mi, here, lanes], svalues), axis=0)
            bias = bias_ref[mi, t]
            scores = dot_cols(keys, queries) + jnp.concatenate((bias, bias), axis=1)
            probs = jnp.exp(scores - lse_ref[i, t])
            gprobs = dot_cols(values, grads)
            delta = jnp.sum(probs * gprobs, axis=0, keepdims=True)
            gscores = (probs * (gprobs - delta)).astype(BF16)
            keys_t = jnp.concatenate((own_keys.T, skeys_t), axis=1)
            gq_ref[mi, here, lanes] = (join_heads(dot(keys_t, gscores)) * SCALE).astype(BF16)
            grad_k = dot(gscores, queries)
            grad_v = dot(probs.astype(BF16), grads)
            gk_ref[mi, here, lanes] = grad_k[:SPAN].astype(BF16)
            gv_ref[mi, here, lanes] = grad_v[:SPAN].astype(BF16)
            sum_k += grad_k[SPAN:]
            sum_v += grad_v[SPAN:]
        gks_ref[mi, :, lanes] = sum_k
        gvs_ref[mi, :, lanes] = sum_v
        return carry

    lax.fori_loop(0, 8, heads, 0)


def project_back_kernel(
    apart, info, block_of, row_of, slots_ref, xs_ref, nb_ref, gq_ref, gk_ref, gv_ref, gks_ref, gvs_ref, sums_ref,
    w_ref, gain, shift, gn_ref, small_ref, keep_ref, send_ref, *refs
):
    if apart:
        all_ref, *refs = refs
    gw_ref, gwb_ref, back_ref, stack_ref, sem = refs
    rows = xs_ref.shape[1]
    summaries = gks_ref.shape[1]
    half, shard, _ = keep_ref.shape
    small_ref[...] = jnp.zeros_like(small_ref)
    for mi in range(2):
        _, offset, ends = row_info(info, mi)
        first, last = summary_range(iota((summaries, 1), 0), offset, ends)
        root = jnp.sqrt((last - first + 1).astype(F32))
        sums = sums_ref[mi]
        pooled = (sums * gain[...] + root * shift[...]).astype(BF16).T
        normed = nb_ref[mi].T
        grad_n = jnp.zeros((rows, D), F32)
        grad_s = jnp.zeros((summaries, D), F32)
        for m in range(4):
            lanes = slice(m * LANES, (m + 1) * LANES)
            gq, gk, gv = gq_ref[mi, :, lanes], gk_ref[mi, :, lanes], gv_ref[mi, :, lanes]
            gks, gvs = gks_ref[mi, :, lanes], gvs_ref[mi, :, lanes]
            small_ref[2:3, lanes] += jnp.sum(gq.astype(F32), axis=0, keepdims=True)
            small_ref[3:4, lanes] += jnp.sum(gv.astype(F32), axis=0, keepdims=True) + jnp.sum(
                root * gvs, axis=0, keepdims=True
            )
            grads = jnp.concatenate((gq, gk, gv), axis=1)
            pooled_grads = jnp.concatenate((gks, gvs), axis=1).astype(BF16)
            w = w_ref[m]
            grad_n += dot_cols(grads, w)
            grad_s += dot_cols(pooled_grads, w[:, 128:])
            grad_w = dot(normed, grads)
            grad_kv = dot(pooled, pooled_grads)
            if mi == 0:
                gw_ref[m] = grad_w
            else:
                gw_ref[m] += grad_w
            gw_ref[m, :, 128:384] += grad_kv
        hat, _ = unit(xs_ref[mi].astype(F32))
        gn_ref[mi] = grad_n
        back_ref[mi] = grad_s.astype(BF16)
        small_ref[0:1, :] += jnp.sum(grad_n * hat, axis=0, keepdims=True) + jnp.sum(
            grad_s * sums, axis=0, keepdims=True
        )
        small_ref[1:2, :] += jnp.sum(grad_n, axis=0, keepdims=True) + jnp.sum(
            root * grad_s, axis=0, keepdims=True
        )
    for m in range(4):
        gwb_ref[m] = gw_ref[m].astype(BF16)
    for base in range(0, stack_ref.shape[0], 32):
        names = [slots_ref[mi : mi + 1, 16 * base : 16 * base + 512] for mi in range(2)]
        spread = [
            jnp.where(iota((summaries, 1), 0) == named, 1.0, 0.0).astype(BF16).T for named in names
        ]
        for lane in range(D // LANES):
            lanes = slice(lane * LANES, (lane + 1) * LANES)
            piece = dot(spread[0], back_ref[0, :, lanes]) + dot(spread[1], back_ref[1, :, lanes])
            stack_ref[base : base + 32, 16 * lane : 16 * lane + 16, :] = piece.astype(BF16).reshape(
                32, 16, LANES
            )

    def emit(d, carry):
        for target, slot in ((keep_ref, d), (send_ref, half + d)):
            first_row = pl.multiple_of(row_of[slot] * shard, 16)
            pltpu.make_async_copy(
                gwb_ref.at[block_of[slot], pl.ds(first_row, shard), :], target.at[d, :, 0:384], sem.at[0]
            ).start()
            if not apart:
                pltpu.make_async_copy(
                    stack_ref.at[slot], target.at[d, 0:64, 384:512], sem.at[1]
                ).start()
        return carry

    lax.fori_loop(0, half, emit, 0)
    if apart:
        pltpu.make_async_copy(stack_ref, all_ref, sem.at[1]).start()
    pltpu.make_async_copy(gwb_ref, gwb_ref, sem.at[0]).wait()
    pltpu.make_async_copy(stack_ref, stack_ref, sem.at[1]).wait()


def input_back_kernel(
    info, x_ref, gn_ref, gn_right, gmid_ref, gmid_right, pooled_ref, gain, out_ref
):
    rows = x_ref.shape[1]
    for mi in range(2):
        dev, offset, ends = row_info(info, mi)
        first, last = summary_range(dev * (rows // SPAN) + iota((8, 1), 0), offset, ends)
        lows = jnp.concatenate(
            [pooled_ref[16 * i + 8 * mi : 16 * i + 8 * mi + 8, :] for i in range(D // LANES)], axis=1
        )
        lows = (lows * lax.rsqrt((last - first + 1).astype(F32))).astype(BF16)
        ids = dev * (rows // SPAN) + iota((1, 8), 1)
        first, last = summary_range(ids, offset, ends)
        pos = dev * rows + iota((rows, 1), 0)
        member = jnp.where((pos >= first) & (pos <= last), 1.0, 0.0).astype(BF16)
        pick = picker(SPAN - offset)
        for t in range(rows // SPAN):
            here = slice(t * SPAN, (t + 1) * SPAN)
            if (t + 2) * SPAN <= rows:
                grad = gn_ref[mi, t * SPAN : (t + 2) * SPAN, :]
                gmid = gmid_ref[mi, t * SPAN : (t + 2) * SPAN, :]
            else:
                grad = jnp.concatenate((gn_ref[mi, here, :], gn_right[mi].astype(F32)), axis=0)
                gmid = jnp.concatenate((gmid_ref[mi, here, :], gmid_right[mi].astype(F32)), axis=0)
            grad = pick_rows(pick, grad) + dot(member[here], lows)
            hat, inverse = unit(x_ref[mi, here, :].astype(F32))
            out_ref[mi, here, :] = pick_rows(pick, gmid) + unit_back(grad * gain[...], hat, inverse)


def call(kernel, outs, in_specs, out_specs=None, scratch=(), limit=56, flops=0, moved=0):
    return pl.pallas_call(
        kernel,
        out_shape=outs,
        in_specs=in_specs,
        out_specs=out_specs if out_specs is not None else [VMEM] * len(outs),
        scratch_shapes=list(scratch),
        compiler_params=pltpu.CompilerParams(vmem_limit_bytes=limit * MIB),
        cost_estimate=pl.CostEstimate(flops=flops, bytes_accessed=moved, transcendentals=0),
    )


def per_device(
    block_input, cotangent, span_offset, doc_lengths, ln1_gain, ln1_bias, w_query, w_key, w_value,
    query_bias, value_bias, w_out, out_bias, ln2_gain, ln2_bias, w_up, up_bias, w_down, down_bias,
):
    groups, ranks = lax.axis_size("seq"), lax.axis_size("mp")
    count = groups * ranks
    mp_index = lax.axis_index("mp")
    dev = lax.axis_index("seq") * ranks + mp_index
    rows = block_input.shape[1]
    tiles = rows // SPAN
    summaries = tiles * count
    shard = w_query.shape[0]
    bits = count.bit_length() - 1
    stages = [(b, b) for b in range(bits - 1, 2, -1)] + [(1, 2), (2, 1)]
    direct = shard == 64

    def swap(value, stage):
        pairs = [(i, i ^ (1 << stage[i & 1])) for i in range(count)]
        return lax.ppermute(value, AXES, pairs)

    def turn(value, by):
        return lax.ppermute(value, AXES, [(i, (i + by) % count) for i in range(count)])

    core = dev & 1
    slot = jnp.arange(count, dtype=jnp.int32)
    far = slot // (count // 2)
    mask = far
    for i, (even, odd) in enumerate(stages):
        where = jnp.where((core ^ far) == 0, even, odd)
        mask = mask | (((slot >> i) & 1) << where)
    owner = dev ^ mask
    if not direct:
        owner = slot
    member_slot = jnp.arange(16, dtype=jnp.int32)
    slots = owner[:, None] * tiles + (member_slot % 8)[None, :]
    valid = (member_slot % 8 <= tiles)[None, :]
    slots = jnp.stack(
        [
            jnp.where(valid & (member_slot // 8 == mi)[None, :], slots, -1).reshape(-1)
            for mi in range(2)
        ]
    )
    block_of, row_of = owner % ranks, owner // ranks
    doc_ends = jnp.cumsum(doc_lengths, axis=1).astype(jnp.int32)
    info = jnp.concatenate((dev[None], span_offset, doc_ends.reshape(-1))).astype(jnp.int32)

    def gather(value):
        part = value[None]
        for stage in stages:
            part = jnp.concatenate((part, swap(part, stage)), axis=0)
        return part, swap(part, (0, 0))

    def scatter(keep, send, small=None):
        keep = keep.astype(F32)
        for stage in [(0, 0)] + stages[::-1]:
            if small is not None:
                high = small.astype(BF16)
                rest = (small - high.astype(F32)).astype(BF16)
                small = high.astype(F32) + rest.astype(F32)
                pad = jnp.concatenate((high, rest, jnp.zeros((8, D), BF16)), axis=0)
                flat = send.reshape(-1, D)
                got = swap(jnp.concatenate((flat, pad), axis=0), stage)
                size = flat.shape[0]
                small = small + (got[size : size + 4].astype(F32) + got[size + 4 : size + 8].astype(F32))
                got = got[:size].reshape(send.shape)
            else:
                got = swap(send, stage)
            total = keep + got.astype(F32)
            half = total.shape[0] // 2
            if half:
                keep, send = total[:half], total[half:].astype(BF16)
        return total[0], small

    def gather_whole(value):
        both = lax.all_gather(value, "seq", axis=0, tiled=True)
        both = lax.all_gather(both, "mp", axis=0)
        return both[: ranks // 2], both[ranks // 2 :]

    def scatter_whole(keep, send):
        both = jnp.concatenate((keep, send), axis=0).astype(F32)
        total = lax.psum_scatter(both, "mp", scatter_dimension=0, tiled=True)[0]
        return lax.psum_scatter(total, "seq", scatter_dimension=0, tiled=True)

    def row(vector):
        return vector[None, :]

    def shape(dims, kind):
        return jax.ShapeDtypeStruct(dims, kind)

    half, tall = (count // 2, shard) if direct else (ranks // 2, shard * groups)
    width = 4 * LANES if direct else 3 * LANES
    apart = not direct
    cot_own = lax.dynamic_slice_in_dim(cotangent, mp_index * rows, rows, 1)
    edges = turn(jnp.stack((block_input[:, rows - SPAN :], cot_own[:, rows - SPAN :])), 1)
    own_sums = call(summary_kernel, [shape((64, LANES), BF16)], [SMEM, VMEM])(info, block_input)[0]

    w_qkv = jnp.concatenate((w_query, w_key, w_value), axis=1)
    w_rest = jnp.concatenate((w_out.T, w_up, w_down.T), axis=1)
    if direct:
        near_a, far_a = gather(jnp.concatenate((w_qkv, own_sums), axis=1))
        near_b, far_b = gather(w_rest)
        more = ()
    else:
        near_a, far_a = gather_whole(w_qkv)
        near_b, far_b = gather_whole(w_rest)
        more = (lax.all_gather(own_sums, AXES, axis=0),)
        block_of, row_of = jnp.arange(ranks, dtype=jnp.int32), jnp.zeros((ranks,), jnp.int32)

    wide = (2, rows, D)
    xs, nb, q, k, v, att, ks, vs, lse, sums, w_full = call(
        partial(attend_kernel, apart),
        [shape(wide, BF16)] * 6
        + [shape((2, summaries, D), BF16)] * 2
        + [shape((8, tiles, 1, 2 * SPAN), F32), shape((2, summaries, D), F32)]
        + [shape((4, D, 3 * LANES), BF16)],
        [SMEM, SMEM, SMEM] + [VMEM] * 7 + [ANY] * (2 + len(more)),
        scratch=[
            pltpu.VMEM((count, 64, LANES), BF16),
            pltpu.VMEM((rows + SPAN, D), BF16),
            pltpu.VMEM((2, tiles, SPAN + summaries, SPAN), F32),
            pltpu.SemaphoreType.DMA((2,)),
        ],
        flops=6 << 30,
        moved=8 << 20,
    )(
        info, block_of, row_of, slots, block_input, edges[0], row(ln1_gain), row(ln1_bias),
        row(query_bias), row(value_bias), near_a, far_a, *more,
    )
    flat = (2 * rows, D)
    cot_wide = jnp.concatenate((edges[1], cot_own), axis=1)
    cot_s = jnp.stack(
        [lax.dynamic_slice_in_dim(cot_wide[i], span_offset[i], rows, 0) for i in range(2)]
    )
    result, gmid, gatt, small_b, grad_ub, keep_b, send_b = call(
        mlp_kernel,
        [shape(flat, BF16), shape(flat, F32), shape(flat, BF16), shape((8, D), F32), shape((1, FF), F32)]
        + [shape((half, tall, 1152), BF16)] * 2,
        [SMEM, SMEM] + [VMEM] * 8 + [ANY] * 2,
        [VMEM] * 5 + [ANY] * 2,
        scratch=[
            pltpu.VMEM((D, D), BF16), pltpu.VMEM((D, FF), BF16), pltpu.VMEM((D, FF), BF16),
            pltpu.VMEM(flat, F32), pltpu.VMEM(flat, F32), pltpu.VMEM(flat, F32),
            pltpu.VMEM(flat, BF16), pltpu.VMEM((D, 2 * rows), BF16), pltpu.VMEM((D, 2 * rows), BF16),
            pltpu.VMEM((D, FF), BF16), pltpu.VMEM((D, FF), BF16), pltpu.VMEM((D, D), BF16),
            pltpu.VMEM((D, D), F32), pltpu.VMEM((D, D), F32), pltpu.VMEM((D, D), F32),
            pltpu.SemaphoreType.DMA((3,)), pltpu.SemaphoreType.DMA((3,)),
        ],
        flops=14 << 30,
        moved=24 << 20,
    )(
        block_of, row_of, xs.reshape(flat), att.reshape(flat), cot_s.reshape(flat), row(out_bias),
        row(ln2_gain), row(ln2_bias), row(up_bias), row(down_bias), near_b, far_b,
    )
    early = lax.psum((small_b[:4], grad_ub), AXES)
    back = turn(
        jnp.stack((result.reshape(wide)[:, :SPAN], gmid.reshape(wide)[:, :SPAN].astype(BF16))), -1
    )
    sum_b = scatter(keep_b, send_b)[0] if direct else scatter_whole(keep_b, send_b)
    gq, gk, gv, gks, gvs = call(
        attend_back_kernel,
        [shape(wide, BF16)] * 3 + [shape((2, summaries, D), F32)] * 2,
        [SMEM] + [VMEM] * 7,
        scratch=[pltpu.VMEM((2, tiles, SPAN + summaries, SPAN), F32)],
        flops=8 << 30,
        moved=8 << 20,
    )(info, q, k, v, ks, vs, lse, gatt.reshape(wide))
    gn, small_a, keep_a, send_a, *more = call(
        partial(project_back_kernel, apart),
        [shape(wide, F32), shape((8, D), F32)]
        + [shape((half, tall, width), BF16)] * 2
        + [shape((count, 64, LANES), BF16)] * apart,
        [SMEM] * 3 + [VMEM] * 12,
        [VMEM] * 2 + [ANY] * (2 + apart),
        scratch=[
            pltpu.VMEM((4, D, 3 * LANES), F32), pltpu.VMEM((4, D, 3 * LANES), BF16),
            pltpu.VMEM((2, summaries, D), BF16), pltpu.VMEM((count, 64, LANES), BF16),
            pltpu.SemaphoreType.DMA((2,)),
        ],
        flops=4 << 30,
        moved=8 << 20,
    )(
        info, block_of, row_of, slots, xs, nb, gq, gk, gv, gks, gvs, sums, w_full, row(ln1_gain),
        row(ln1_bias),
    )
    gn_back = turn(gn[:, :SPAN].astype(BF16), -1)
    if direct:
        sum_a, late = scatter(keep_a, send_a, small_a[:4])
        pooled = sum_a[:, 384:]
    else:
        sum_a, late = scatter_whole(keep_a, send_a), lax.psum(small_a[:4], AXES)
        pooled = lax.psum_scatter(more[0].astype(F32), AXES, scatter_dimension=0, tiled=True)[0]
    input_grad = call(
        input_back_kernel,
        [shape(wide, F32)],
        [SMEM] + [VMEM] * 7,
    )(info, block_input, gn, gn_back, gmid.reshape(wide), back[1], pooled, row(ln1_gain))[0]
    result_wide = jnp.concatenate((result.reshape(wide), back[0]), axis=1)
    result_own = jnp.stack(
        [lax.dynamic_slice_in_dim(result_wide[i], SPAN - span_offset[i], rows, 0) for i in range(2)]
    )
    small_sum, ub_sum = early
    return (
        result_own,
        input_grad,
        late[0],
        late[1],
        sum_a[:, :128],
        sum_a[:, 128:256],
        sum_a[:, 256:384],
        late[2],
        late[3],
        sum_b[:, :128].T,
        small_sum[2],
        small_sum[0],
        small_sum[1],
        sum_b[:, 128:640],
        ub_sum[0],
        sum_b[:, 640:].T,
        small_sum[3],
    )


def solution(mesh):
    vector, matrix, turned = P(), P("seq", "mp"), P("mp", "seq")
    own, group = P(None, ("seq", "mp"), None), P(None, "seq", None)
    return jax.shard_map(
        per_device,
        mesh=mesh,
        in_specs=(own, group, vector, vector, vector, vector, matrix, matrix, matrix, vector, vector)
        + (turned, vector, vector, vector, matrix, vector, turned, vector),
        out_specs=(own, own, vector, vector, matrix, matrix, matrix, vector, vector, turned, vector)
        + (vector, vector, matrix, vector, turned, vector),
        check_vma=False,
    )
```

time: 2390 us -> 277 us (0.12)
  waiting for transfers between devices: 1310 us -> 59.6 us
  blocking collectives: 544 us -> 44.7 us
  local copies, waits for them, and re-layouts: 188 us -> 24.4 us
  matrix products: 149 us -> 0 us
  other arithmetic: 140 us -> 17.3 us
  Pallas kernels: 0 us -> 94.2 us
    reduce_scatter x24 -> x0, waiting for transfers between devices: 1250 us -> none  [the longest x2 130 us: reduce_weights(): lax.psum_scatter(grad_up, 'seq', scatter_dimension=0, tiled=True)]
    all_gather x16 -> x0, blocking collectives: 504 us -> none  [the longest x2 67.2 us: micro_step(): lax.all_gather(local_summary_keys, 'seq', axis=0, tiled=True)]
    dot_general x140 -> x0, matrix products: 149 us -> none  [the longest x8 33.3 us: contract_rows(): lax.dot_general(left, right, (((0,), (0,)), ((), ())), preferred_element_...]
    pallas_call x0 -> x6, Pallas kernels: none -> 94.2 us  [the longest x1 34.7 us: per_device(): call(mlp_kernel, [shape(flat, BF16), shape(flat, F32), shape(flat, BF16),...]
    dynamic_slice x109 -> x1, local copies, waits for them, and re-layouts: 84.9 us -> 1.29 us  [per_device(): cot_own = lax.dynamic_slice_in_dim(cotangent, mp_index * rows, rows, 1)]
    dynamic_update_slice x52 -> x0, local copies, waits for them, and re-layouts: 56.8 us -> none  [the longest x28 50.3 us: add_rows(): lax.dynamic_update_slice_in_dim(target, current + addend, first_row, 0)]
    ppermute x8 -> x23, waiting for transfers between devices: 10.6 us -> 59.6 us  [the longest x20 59.6 us: swap(): return lax.ppermute(value, AXES, pairs)]
    all_gather x6 -> x0, waiting for transfers between devices: 45.4 us -> none  [the longest x2 45.3 us: micro_step(): branch_group = lax.all_gather(grad_branch, 'mp', axis=0, tiled=True)]
  transfers between devices with their start and end apart: 38 -> 23, of which waited for: 30 -> 12; matrix products, arithmetic and copies ran while one was open for 5% -> 12% of each run, Pallas kernels for 0% -> 11%
where the time goes in v1:
time: 277 us; the launch traced here: 276 us
  Pallas kernels  94.2 us (34%)
  waiting for transfers between devices  59.6 us (22%)
  blocking collectives  44.7 us (16%)
  starting transfers between devices  27.7 us (10%)
  local copies, waits for them, and re-layouts  24.4 us (9%)
  other arithmetic  17.3 us (6%)
  between operations  7.72 us (3%)
    ppermute x20, waiting for transfers between devices, swap(): return lax.ppermute(value, AXES, pairs)  59.6 us
    psum x1, blocking collectives, per_device(): early = lax.psum((small_b[:4], grad_ub), AXES)  44.7 us
    pallas_call x1, Pallas kernels, per_device(): call(mlp_kernel, [shape(flat, BF16), shape(flat, F32), shape(flat, BF16),...  34.7 us
    ppermute x20, starting transfers between devices, swap(): return lax.ppermute(value, AXES, pairs)  23.5 us
    pallas_call x1, Pallas kernels, per_device(): call(partial(attend_kernel, apart), [shape(wide, BF16)] * 6 + [shape((2,...  20.8 us
    pallas_call x1, Pallas kernels, per_device(): call(attend_back_kernel, [shape(wide, BF16)] * 3 + [shape((2, summaries,...  17.2 us
    pallas_call x1, Pallas kernels, per_device(): call(partial(project_back_kernel, apart), [shape(wide, F32), shape((8, D)...  12.1 us
    pallas_call x1, Pallas kernels, per_device(): call(input_back_kernel, [shape(wide, F32)], [SMEM] + [VMEM] * 7)  6.67 us
  transfers between devices with their start and end apart: 23, of which 12 were waited for; matrix products, arithmetic and copies ran while one was open for 12% of the time, Pallas kernels for 11%

profile of v1, /device:TPU:0, one launch (start us, length us, event | category | flops | bytes accessed | tf_op | source)
XLA Modules:
  0.0 275.7 jit_solution(3832170003804005668)
XLA Ops:
  0.7 0.9 maximum_bitcast_fusion
  1.5 4.1 %collective-permute-start.6 = (bf16[1,64,1152]{2,1,0:T(8,128)(2,1)S(1)}, bf16[1,64,1152]{2,1,0:T(8,128)(2,1)S(1)}, u32[]{:S(2)}, u32[]{:S(2)}) collective-permute-start(bf16[1,64,1152]{2,1,0:T(8,128)(2,1)S(1)} %maximum_bitcast_fusion), channel_id=1, source_target_pairs={{0,16},{1,17},{2,18},{3,19},{4,20},{5,21},{6,22},{7,23},{8,24},{9,... | collective-permute-start | bytes 442376 | tf_op jit(solution)/shard_map/ppermute | solution.py:518
  5.6 0.9 reduce_window_sum.11
  6.6 1.2 pad_add_fusion.1.info
  7.8 2.8 %shard_map.314 = bf16[64,128]{1,0:T(8,128)(2,1)} custom-call(s32[19]{0:T(128)} %pad_add_fusion.1.info, bf16[2,512,512]{2,1,0:T(8,128)(2,1)} %x_ref.5), custom_call_target="tpu_custom_call" | custom-call | tf_op jit(solution)/shard_map/pallas_call | solution.py:594
  10.6 0.8 maximum_bitcast_fusion.1
  11.5 1.1 collective-permute-done.6
  12.7 1.5 collective-permute-start.7
  14.2 1.0 slice_bitcast_fusion.5
  15.2 1.0 dynamic-slice_bitcast_fusion
  16.3 6.0 %collective-permute-done.7 = bf16[2,64,1152]{2,1,0:T(8,128)(2,1)S(1)} collective-permute-done((bf16[2,64,1152]{2,1,0:T(8,128)(2,1)S(1)}, bf16[2,64,1152]{2,1,0:T(8,128)(2,1)S(1)}, u32[]{:S(2)}, u32[]{:S(2)}) %collective-permute-start.7) | collective-permute-done | bytes 294944 | tf_op jit(solution)/shard_map/ppermute | solution.py:518
  22.4 1.4 collective-permute-start.8
  23.8 0.7 constant_dynamic-update-slice_fusion.9
  24.9 7.4 %collective-permute-done.8 = bf16[4,64,1152]{2,1,0:T(8,128)(2,1)S(1)} collective-permute-done((bf16[4,64,1152]{2,1,0:T(8,128)(2,1)S(1)}, bf16[4,64,1152]{2,1,0:T(8,128)(2,1)S(1)}, u32[]{:S(2)}, u32[]{:S(2)}) %collective-permute-start.8) | collective-permute-done | bytes 589856 | tf_op jit(solution)/shard_map/ppermute | solution.py:518
  32.5 6.3 %collective-permute-start.9 = (bf16[8,64,1152]{2,1,0:T(8,128)(2,1)S(1)}, bf16[8,64,1152]{2,1,0:T(8,128)(2,1)S(1)}, u32[]{:S(2)}, u32[]{:S(2)}) collective-permute-start(bf16[8,64,1152]{2,1,0:T(8,128)(2,1)S(1)} %pad_maximum_fusion), channel_id=1, source_target_pairs={{0,4},{1,3},{2,6},{3,1},{4,0},{5,7},{6,2},{7,5},{8,12},{9,11},{10,... | collective-permute-start | bytes 3538952 | tf_op jit(solution)/shard_map/ppermute | solution.py:518
  39.0 0.7 constant_dynamic-update-slice_fusion.8
  39.6 0.7 constant_dynamic-update-slice_fusion.7
  40.4 7.8 %collective-permute-done.3 = bf16[4,64,512]{2,1,0:T(8,128)(2,1)S(1)} collective-permute-done((bf16[4,64,512]{2,1,0:T(8,128)(2,1)S(1)}, bf16[4,64,512]{2,1,0:T(8,128)(2,1)S(1)}, u32[]{:S(2)}, u32[]{:S(2)}) %collective-permute-start.3) | collective-permute-done | bytes 262176 | tf_op jit(solution)/shard_map/ppermute | solution.py:518
  48.4 0.9 constant_dynamic-update-slice_fusion.6
  49.3 5.0 %collective-permute-done.9 = bf16[8,64,1152]{2,1,0:T(8,128)(2,1)S(1)} collective-permute-done((bf16[8,64,1152]{2,1,0:T(8,128)(2,1)S(1)}, bf16[8,64,1152]{2,1,0:T(8,128)(2,1)S(1)}, u32[]{:S(2)}, u32[]{:S(2)}) %collective-permute-start.9) | collective-permute-done | bytes 1179680 | tf_op jit(solution)/shard_map/ppermute | solution.py:518
  54.3 1.2 constant_dynamic-update-slice_fusion.5.near_ref
  56.1 3.8 %collective-permute-done.4 = bf16[8,64,512]{2,1,0:T(8,128)(2,1)S(1)} collective-permute-done((bf16[8,64,512]{2,1,0:T(8,128)(2,1)S(1)}, bf16[8,64,512]{2,1,0:T(8,128)(2,1)S(1)}, u32[]{:S(2)}, u32[]{:S(2)}) %collective-permute-start.4) | collective-permute-done | bytes 524320 | tf_op jit(solution)/shard_map/ppermute | solution.py:518
  60.0 0.6 and_select_fusion.2
  64.7 0.6 pad_add_fusion.slots_ref
  65.3 1.3 constant_dynamic-slice_fusion
  66.7 0.7 slice_bitcast_fusion.3
  68.0 1.1 pad_maximum_fusion.1
  69.1 1.0 copy-done.16
  70.1 20.8 %shard_map.315 = (bf16[2,512,512]{2,1,0:T(8,128)(2,1)}, bf16[2,512,512]{2,1,0:T(8,128)(2,1)}, bf16[2,512,512]{2,1,0:T(8,128)(2,1)}, bf16[2,512,512]{2,1,0:T(8,12...) custom-call(s32[19]{0:T(128)} %pad_add_fusion.1.info, ...), custom_call_target="tpu_custom_call" | custom-call | flops 6442450944 | bytes 8388608 | tf_op jit(solution)/shard_map/pallas_call | solution.py:609
  90.9 34.7 %shard_map.316 = (bf16[1024,512]{1,0:T(8,128)(2,1)}, f32[1024,512]{1,0:T(8,128)}, bf16[1024,512]{1,0:T(8,128)(2,1)}, f32[8,512]{1,0:T(8,128)}, f32[1,2048]{1,0:T...) custom-call(s32[32]{0:T(128)} %get-tuple-element.108.block_of, s32[32]{0:T(128)} %get-tuple-element.107.row_of, ...), custom_call_target="tpu_custom_call" | custom-call | flops 15032385536 | bytes 25165824 | tf_op jit(solution)/shard_map/pallas_call | solution.py:633
  125.6 17.2 %shard_map.317 = (bf16[2,512,512]{2,1,0:T(8,128)(2,1)}, bf16[2,512,512]{2,1,0:T(8,128)(2,1)}, bf16[2,512,512]{2,1,0:T(8,128)(2,1)}, f32[2,128,512]{2,1,0:T(8,128)}, f32[2,128,512]{2,1,0:T(8,128)}) custom-call(s32[19]{0:T(128)} %pad_add_fusion.1.info, bf16[2,512,512]{2,1,0:T(8,128)(2,1)} %get-tuple-element.49.q_ref, ...), custom_call_target="tpu_custom_call" | custom-call | flops 8589934592 | bytes 8388608 | tf_op jit(solution)/shard_map/pallas_call | solution.py:658
  142.8 12.1 %shard_map.318 = (f32[2,512,512]{2,1,0:T(8,128)}, f32[8,512]{1,0:T(8,128)}, bf16[16,64,512]{2,1,0:T(8,128)(2,1)}, bf16[16,64,512]{2,1,0:T(8,128)(2,1)}) custom-call(s32[19]{0:T(128)} %pad_add_fusion.1.info, s32[32]{0:T(128)} %get-tuple-element.108.block_of, s32[32]{0:T(128)} %get-tuple-element.107.row_of, s32[2,512]{1,0:T(2,128)} %pad_add_fusion.slots_ref, ...), custom_call_target="tpu_custom_call" | custom-call | flops 4294967296 | bytes 8388608 | tf_op jit(solution)/shard_map/pallas_call | solution.py:666
  154.9 0.8 fusion.6
  155.7 3.8 %concatenate.73 = bf16[1040,512]{1,0:T(8,128)(2,1)S(1)} concatenate(bf16[1024,512]{1,0:T(8,128)(2,1)} %bitcast.90, bf16[4,512]{1,0:T(4,128)(2,1)S(1)} %get-tuple-element.78, bf16[4,512]{1,0:T(4,128)(2,1)S(1)} %get-tuple-element.77, bf16[8,512]{1,0:T(8,128)(2,1)S(1)} %broadcast.274), dimensions={0} | concatenate | bytes 2129920 | tf_op jit(solution)/shard_map/concatenate | solution.py:561
  162.9 1.8 slice.403
  164.6 3.7 %collective-permute-start.12 = (bf16[2,128,512]{2,1,0:T(8,128)(2,1)}, bf16[2,128,512]{2,1,0:T(8,128)(2,1)S(1)}, u32[]{:S(2)}, u32[]{:S(2)}) collective-permute-start(bf16[2,128,512]{2,1,0:T(8,128)(2,1)} %slice.403), channel_id=1, source_target_pairs={{0,31},{1,0},{2,1},{3,2},{4,3},{5,4},{6,5},{7,6},{8,7},{9,8},{10,9... | collective-permute-start | bytes 786440 | tf_op jit(solution)/shard_map/ppermute | solution.py:521
  168.4 1.1 fusion.3
  169.5 0.9 copy-done.2
  170.8 0.8 fusion.27
  171.7 0.9 pad_maximum_fusion.4
  172.6 0.8 pad_maximum_fusion.7
  173.8 44.7 %all-reduce = (f32[4,512]{1,0:T(4,128)S(1)}, f32[2048]{0:T(1024)}) all-reduce(f32[4,512]{1,0:T(4,128)S(1)} %slice.257, f32[2048]{0:T(1024)S(1)} %bitcast.98), channel_id=1, replica_groups=mesh['seq'=8,'mp'=4] {'seq','mp'}, use_global_device_ids=true, to_apply=%region_1.2 | all-reduce | flops 4096 | bytes 32768 | tf_op jit(solution)/shard_map/psum | solution.py:653
  218.5 0.6 fusion.34
  219.1 1.1 slice.280
  220.5 0.8 fusion.31
  221.3 2.3 collective-permute-start.15
  223.7 1.8 slice_bitcast_fusion
  225.5 2.7 collective-permute-done.15
  228.4 2.2 convert_add_fusion
  230.8 2.7 collective-permute-start.19
  233.5 0.6 fusion.1
  234.5 4.2 %collective-permute-done.16 = bf16[144,512]{1,0:T(8,128)(2,1)S(1)} collective-permute-done((bf16[144,512]{1,0:T(8,128)(2,1)S(1)}, bf16[144,512]{1,0:T(8,128)(2,1)S(1)}, u32[]{:S(2)}, u32[]{:S(2)}) %collective-permute-start.16) | collective-permute-done | bytes 147488 | tf_op jit(solution)/shard_map/ppermute | solution.py:518
  238.7 9.2 %collective-permute-done.19 = bf16[8,64,1152]{2,1,0:T(8,128)(2,1)S(1)} collective-permute-done((bf16[8,64,1152]{2,1,0:T(8,128)(2,1)S(1)}, bf16[8,64,1152]{2,1,0:T(8,128)(2,1)S(1)}, u32[]{:S(2)}, u32[]{:S(2)}) %collective-permute-start.19) | collective-permute-done | bytes 1179680 | tf_op jit(solution)/shard_map/ppermute | solution.py:518
  248.3 1.4 collective-permute-start.20
  249.8 1.1 pad_maximum_fusion.2
  250.9 4.5 %collective-permute-done.17 = bf16[80,512]{1,0:T(8,128)(2,1)S(1)} collective-permute-done((bf16[80,512]{1,0:T(8,128)(2,1)S(1)}, bf16[80,512]{1,0:T(8,128)(2,1)S(1)}, u32[]{:S(2)}, u32[]{:S(2)}) %collective-permute-start.17) | collective-permute-done | bytes 81952 | tf_op jit(solution)/shard_map/ppermute | solution.py:518
  255.4 2.9 %collective-permute-done.20 = bf16[4,64,1152]{2,1,0:T(8,128)(2,1)S(1)} collective-permute-done((bf16[4,64,1152]{2,1,0:T(8,128)(2,1)S(1)}, bf16[4,64,1152]{2,1,0:T(8,128)(2,1)S(1)}, u32[]{:S(2)}, u32[]{:S(2)}) %collective-permute-start.20) | collective-permute-done | bytes 589856 | tf_op jit(solution)/shard_map/ppermute | solution.py:518
  258.5 0.7 fusion.33
  259.2 0.7 copy-done.4
  259.9 6.7 %shard_map.319 = f32[2,512,512]{2,1,0:T(8,128)} custom-call(s32[19]{0:T(128)} %pad_add_fusion.1.info, bf16[2,512,512]{2,1,0:T(8,128)(2,1)} %x_ref.5, f32[2,512,512]{2,1,0:T(8,128)} %get-tuple-element.63.gn_ref, bf16[2,128,512]{2,1,0:T(8,128)(2,1)} %copy-done.4, f32[2,512,512]{2,1,0:T(8,128)} %bitcast.85, bf16[2,128,512]{2,1,0:T(8,128)(2,1)} %get-tuple-element.81.gmid_right, ...), custom_call_target="tpu_custom_call" | custom-call | tf_op jit(solution)/shard_map/pallas_call | solution.py:691
  266.6 2.1 collective-permute-start.22
  269.4 5.0 %collective-permute-done.22 = bf16[1,64,1152]{2,1,0:T(8,128)(2,1)S(1)} collective-permute-done((bf16[1,64,1152]{2,1,0:T(8,128)(2,1)S(1)}, bf16[1,64,1152]{2,1,0:T(8,128)(2,1)S(1)}, u32[]{:S(2)}, u32[]{:S(2)}) %collective-permute-start.22) | collective-permute-done | bytes 147488 | tf_op jit(solution)/shard_map/ppermute | solution.py:518
  274.4 0.7 slice_bitcast_fusion.6
  275.1 0.6 slice_bitcast_fusion.8
  (114 shorter events, 6.9 us)
Async XLA Ops:
  1.5 11.1 %collective-permute-start.6 = (bf16[1,64,1152]{2,1,0:T(8,128)(2,1)S(1)}, bf16[1,64,1152]{2,1,0:T(8,128)(2,1)S(1)}, u32[]{:S(2)}, u32[]{:S(2)}) collective-permute-start(bf16[1,64,1152]{2,1,0:T(8,128)(2,1)S(1)} %maximum_bitcast_fusion), channel_id=1, source_target_pairs={{0,16},{1,17},{2,18},{3,19},{4,20},{5,21},{6,22},{7,23},{8,24},{9,... | collective-permute-start | bytes 442376 | tf_op jit(solution)/shard_map/ppermute | solution.py:518
  10.6 13.1 %copy-start.5 = (bf16[512,64]{0,1:T(8,128)(2,1)S(1)}, bf16[512,64]{0,1:T(8,128)(2,1)}, u32[]{:S(2)}) copy-start(bf16[512,64]{0,1:T(8,128)(2,1)} %param.36) | copy-start | bytes 196612
  10.6 13.1 %copy-start.6 = (bf16[64,512]{1,0:T(8,128)(2,1)S(1)}, bf16[64,512]{1,0:T(8,128)(2,1)}, u32[]{:S(2)}) copy-start(bf16[64,512]{1,0:T(8,128)(2,1)} %param.34) | copy-start | bytes 196612
  10.6 13.1 %copy-start.8 = (bf16[128,64]{0,1:T(8,128)(2,1)S(1)}, bf16[128,64]{0,1:T(8,128)(2,1)}, u32[]{:S(2)}) copy-start(bf16[128,64]{0,1:T(8,128)(2,1)} %param.30) | copy-start | bytes 49156
  11.5 13.0 %collective-permute-start.1 = (bf16[1,64,512]{2,1,0:T(8,128)(2,1)S(1)}, bf16[1,64,512]{2,1,0:T(8,128)(2,1)S(1)}, u32[]{:S(2)}, u32[]{:S(2)}) collective-permute-start(bf16[1,64,512]{2,1,0:T(8,128)(2,1)S(1)} %maximum_bitcast_fusion.1), channel_id=1, source_target_pairs={{0,16},{1,17},{2,18},{3,19},{4,20},{5,21},{6,22},{7,23},{8,24},{9,... | collective-permute-start | bytes 196616 | tf_op jit(solution)/shard_map/ppermute | solution.py:518
  12.7 9.6 %collective-permute-start.7 = (bf16[2,64,1152]{2,1,0:T(8,128)(2,1)S(1)}, bf16[2,64,1152]{2,1,0:T(8,128)(2,1)S(1)}, u32[]{:S(2)}, u32[]{:S(2)}) collective-permute-start(bf16[2,64,1152]{2,1,0:T(8,128)(2,1)S(1)} %pad_maximum_fusion.8), channel_id=1, source_target_pairs={{0,8},{1,9},{2,10},{3,11},{4,12},{5,13},{6,14},{7,15},{8,0},{9,1},... | collective-permute-start | bytes 884744 | tf_op jit(solution)/shard_map/ppermute | solution.py:518
  16.2 50.4 %collective-permute-start = (bf16[2,2,128,512]{3,2,1,0:T(8,128)(2,1)S(1)}, bf16[2,2,128,512]{3,2,1,0:T(8,128)(2,1)S(1)}, u32[]{:S(2)}, u32[]{:S(2)}) collective-permute-start(bf16[2,2,128,512]{3,2,1,0:T(8,128)(2,1)S(1)} %pad_maximum_fusion.5), channel_id=1, source_target_pairs={{0,1},{1,2},{2,3},{3,4},{4,5},{5,6},{6,7},{7,8},{8,9},{9,10},{10,1... | collective-permute-start | bytes 1572872 | tf_op jit(solution)/shard_map/ppermute | solution.py:521
  22.4 9.9 %collective-permute-start.8 = (bf16[4,64,1152]{2,1,0:T(8,128)(2,1)S(1)}, bf16[4,64,1152]{2,1,0:T(8,128)(2,1)S(1)}, u32[]{:S(2)}, u32[]{:S(2)}) collective-permute-start(bf16[4,64,1152]{2,1,0:T(8,128)(2,1)S(1)} %pad_maximum_fusion.3), channel_id=1, source_target_pairs={{0,2},{1,5},{2,0},{3,7},{4,6},{5,1},{6,4},{7,3},{8,10},{9,13},{10,... | collective-permute-start | bytes 1769480 | tf_op jit(solution)/shard_map/ppermute | solution.py:518
  24.5 14.4 %collective-permute-start.2 = (bf16[2,64,512]{2,1,0:T(8,128)(2,1)S(1)}, bf16[2,64,512]{2,1,0:T(8,128)(2,1)S(1)}, u32[]{:S(2)}, u32[]{:S(2)}) collective-permute-start(bf16[2,64,512]{2,1,0:T(8,128)(2,1)S(1)} %pad_maximum_fusion.12), channel_id=1, source_target_pairs={{0,8},{1,9},{2,10},{3,11},{4,12},{5,13},{6,14},{7,15},{8,0},{9,1},... | collective-permute-start | bytes 393224 | tf_op jit(solution)/shard_map/ppermute | solution.py:518
  32.5 21.8 %collective-permute-start.9 = (bf16[8,64,1152]{2,1,0:T(8,128)(2,1)S(1)}, bf16[8,64,1152]{2,1,0:T(8,128)(2,1)S(1)}, u32[]{:S(2)}, u32[]{:S(2)}) collective-permute-start(bf16[8,64,1152]{2,1,0:T(8,128)(2,1)S(1)} %pad_maximum_fusion), channel_id=1, source_target_pairs={{0,4},{1,3},{2,6},{3,1},{4,0},{5,7},{6,2},{7,5},{8,12},{9,11},{10,... | collective-permute-start | bytes 3538952 | tf_op jit(solution)/shard_map/ppermute | solution.py:518
  38.9 9.3 %collective-permute-start.3 = (bf16[4,64,512]{2,1,0:T(8,128)(2,1)S(1)}, bf16[4,64,512]{2,1,0:T(8,128)(2,1)S(1)}, u32[]{:S(2)}, u32[]{:S(2)}) collective-permute-start(bf16[4,64,512]{2,1,0:T(8,128)(2,1)S(1)} %pad_maximum_fusion.10), channel_id=1, source_target_pairs={{0,2},{1,5},{2,0},{3,7},{4,6},{5,1},{6,4},{7,3},{8,10},{9,13},{10,... | collective-permute-start | bytes 786440 | tf_op jit(solution)/shard_map/ppermute | solution.py:518
  40.4 15.1 %copy-start.13 = (s32[2]{0:T(128)S(1)}, s32[2]{0:T(128)}, u32[]{:S(2)}) copy-start(s32[2]{0:T(128)} %param.21) | copy-start | bytes 28
  40.4 15.7 %copy-start.7 = (bf16[64,128]{1,0:T(8,128)(2,1)S(1)}, bf16[64,128]{1,0:T(8,128)(2,1)}, u32[]{:S(2)}) copy-start(bf16[64,128]{1,0:T(8,128)(2,1)} %shard_map.314) | copy-start | bytes 49156
  40.4 15.7 %copy-start.9 = (bf16[64,128]{1,0:T(8,128)(2,1)S(1)}, bf16[64,128]{1,0:T(8,128)(2,1)}, u32[]{:S(2)}) copy-start(bf16[64,128]{1,0:T(8,128)(2,1)} %param.27) | copy-start | bytes 49156
  40.4 15.7 %copy-start.10 = (bf16[64,128]{1,0:T(8,128)(2,1)S(1)}, bf16[64,128]{1,0:T(8,128)(2,1)}, u32[]{:S(2)}) copy-start(bf16[64,128]{1,0:T(8,128)(2,1)} %param.26) | copy-start | bytes 49156
  40.4 15.7 %copy-start.11 = (bf16[64,128]{1,0:T(8,128)(2,1)S(1)}, bf16[64,128]{1,0:T(8,128)(2,1)}, u32[]{:S(2)}) copy-start(bf16[64,128]{1,0:T(8,128)(2,1)} %param.25) | copy-start | bytes 49156
  48.3 11.6 %collective-permute-start.4 = (bf16[8,64,512]{2,1,0:T(8,128)(2,1)S(1)}, bf16[8,64,512]{2,1,0:T(8,128)(2,1)S(1)}, u32[]{:S(2)}, u32[]{:S(2)}) collective-permute-start(bf16[8,64,512]{2,1,0:T(8,128)(2,1)S(1)} %pad_maximum_fusion.6), channel_id=1, source_target_pairs={{0,4},{1,3},{2,6},{3,1},{4,0},{5,7},{6,2},{7,5},{8,12},{9,11},{10,... | collective-permute-start | bytes 1572872 | tf_op jit(solution)/shard_map/ppermute | solution.py:518
  55.4 35.4 %collective-permute-start.10 = (bf16[16,64,1152]{2,1,0:T(8,128)(2,1)}, bf16[16,64,1152]{2,1,0:T(8,128)(2,1)}, u32[]{:S(2)}, u32[]{:S(2)}) collective-permute-start(bf16[16,64,1152]{2,1,0:T(8,128)(2,1)} %constant_dynamic-update-slice_fusion.5.near_ref), channel_id=1, source_target_pairs={{0,1},{1,0},{2,3},{3,2},{4,5},{5,4},{6,7},{7,6},{8,9},{9,8},{10,11... | collective-permute-start | bytes 7077896 | tf_op jit(solution)/shard_map/ppermute | solution.py:518
  59.9 7.5 %copy-start.14 = (bf16[16,64,512]{2,1,0:T(8,128)(2,1)}, bf16[16,64,512]{2,1,0:T(8,128)(2,1)S(1)}, u32[]{:S(2)}) copy-start(bf16[16,64,512]{2,1,0:T(8,128)(2,1)S(1)} %constant_dynamic-update-slice_fusion.near_ref) | copy-start | bytes 3145732
  59.9 9.1 %collective-permute-start.5 = (bf16[16,64,512]{2,1,0:T(8,128)(2,1)S(1)}, bf16[16,64,512]{2,1,0:T(8,128)(2,1)S(1)}, u32[]{:S(2)}, u32[]{:S(2)}) collective-permute-start(bf16[16,64,512]{2,1,0:T(8,128)(2,1)S(1)} %constant_dynamic-update-slice_fusion.near_ref), channel_id=1, source_target_pairs={{0,1},{1,0},{2,3},{3,2},{4,5},{5,4},{6,7},{7,6},{8,9},{9,8},{10,11... | collective-permute-start | bytes 3145736 | tf_op jit(solution)/shard_map/ppermute | solution.py:518
  69.1 1.0 copy-start.16
  154.9 8.0 %copy-start.15 = (f32[8,512]{1,0:T(8,128)S(1)}, f32[8,512]{1,0:T(8,128)}, u32[]{:S(2)}) copy-start(f32[8,512]{1,0:T(8,128)} %get-tuple-element.69) | copy-start | bytes 49156
  159.5 10.9 %copy-start.3 = (bf16[16,64,512]{2,1,0:T(8,128)(2,1)S(1)}, bf16[16,64,512]{2,1,0:T(8,128)(2,1)}, u32[]{:S(2)}) copy-start(bf16[16,64,512]{2,1,0:T(8,128)(2,1)} %get-tuple-element.64) | copy-start | bytes 3145732
  159.5 9.9 %collective-permute-start.13 = (bf16[1040,512]{1,0:T(8,128)(2,1)S(1)}, bf16[1040,512]{1,0:T(8,128)(2,1)S(1)}, u32[]{:S(2)}, u32[]{:S(2)}) collective-permute-start(bf16[1040,512]{1,0:T(8,128)(2,1)S(1)} %concatenate.73), channel_id=1, source_target_pairs={{0,1},{1,0},{2,3},{3,2},{4,5},{5,4},{6,7},{7,6},{8,9},{9,8},{10,11... | collective-permute-start | bytes 3194888 | tf_op jit(solution)/shard_map/ppermute | solution.py:518
  162.6 65.8 %collective-permute-start.18 = (bf16[16,64,1152]{2,1,0:T(8,128)(2,1)}, bf16[16,64,1152]{2,1,0:T(8,128)(2,1)}, u32[]{:S(2)}, u32[]{:S(2)}) collective-permute-start(bf16[16,64,1152]{2,1,0:T(8,128)(2,1)} %get-tuple-element.68), channel_id=1, source_target_pairs={{0,1},{1,0},{2,3},{3,2},{4,5},{5,4},{6,7},{7,6},{8,9},{9,8},{10,11... | collective-permute-start | bytes 7077896 | tf_op jit(solution)/shard_map/ppermute | solution.py:518
  164.6 94.5 %collective-permute-start.12 = (bf16[2,128,512]{2,1,0:T(8,128)(2,1)}, bf16[2,128,512]{2,1,0:T(8,128)(2,1)S(1)}, u32[]{:S(2)}, u32[]{:S(2)}) collective-permute-start(bf16[2,128,512]{2,1,0:T(8,128)(2,1)} %slice.403), channel_id=1, source_target_pairs={{0,31},{1,0},{2,1},{3,2},{4,3},{5,4},{6,5},{7,6},{8,7},{9,8},{10,9... | collective-permute-start | bytes 786440 | tf_op jit(solution)/shard_map/ppermute | solution.py:521
  169.5 1.0 copy-start.2
  170.8 1.8 copy-start
  170.8 3.0 %copy-start.12 = (f32[1,2048]{1,0:T(1,128)S(1)}, f32[1,2048]{1,0:T(1,128)}, u32[]{:S(2)}) copy-start(f32[1,2048]{1,0:T(1,128)} %get-tuple-element.70) | copy-start | bytes 24580
  172.5 46.6 %collective-permute-start.14 = (bf16[528,512]{1,0:T(8,128)(2,1)}, bf16[528,512]{1,0:T(8,128)(2,1)}, u32[]{:S(2)}, u32[]{:S(2)}) collective-permute-start(bf16[528,512]{1,0:T(8,128)(2,1)} %pad_maximum_fusion.4), channel_id=1, source_target_pairs={{0,4},{1,3},{2,6},{3,1},{4,0},{5,7},{6,2},{7,5},{8,12},{9,11},{10,... | collective-permute-start | bytes 1622024 | tf_op jit(solution)/shard_map/ppermute | solution.py:518
  173.4 50.3 %collective-permute-start.11 = (bf16[2,2,128,512]{3,2,1,0:T(8,128)(2,1)}, bf16[2,2,128,512]{3,2,1,0:T(8,128)(2,1)}, u32[]{:S(2)}, u32[]{:S(2)}) collective-permute-start(bf16[2,2,128,512]{3,2,1,0:T(8,128)(2,1)} %pad_maximum_fusion.7), channel_id=1, source_target_pairs={{0,31},{1,0},{2,1},{3,2},{4,3},{5,4},{6,5},{7,6},{8,7},{9,8},{10,9... | collective-permute-start | bytes 1572872 | tf_op jit(solution)/shard_map/ppermute | solution.py:521
  221.3 7.0 %copy-start.1 = (bf16[16,64,1152]{2,1,0:T(8,128)(2,1)S(1)}, bf16[16,64,1152]{2,1,0:T(8,128)(2,1)}, u32[]{:S(2)}) copy-start(bf16[16,64,1152]{2,1,0:T(8,128)(2,1)} %get-tuple-element.67) | copy-start | bytes 7077892
  221.3 6.9 %collective-permute-start.15 = (bf16[272,512]{1,0:T(8,128)(2,1)S(1)}, bf16[272,512]{1,0:T(8,128)(2,1)S(1)}, u32[]{:S(2)}, u32[]{:S(2)}) collective-permute-start(bf16[272,512]{1,0:T(8,128)(2,1)S(1)} %pad_maximum_fusion.9), channel_id=1, source_target_pairs={{0,2},{1,5},{2,0},{3,7},{4,6},{5,1},{6,4},{7,3},{8,10},{9,13},{10,... | collective-permute-start | bytes 835592 | tf_op jit(solution)/shard_map/ppermute | solution.py:518
  230.8 17.2 %collective-permute-start.19 = (bf16[8,64,1152]{2,1,0:T(8,128)(2,1)S(1)}, bf16[8,64,1152]{2,1,0:T(8,128)(2,1)S(1)}, u32[]{:S(2)}, u32[]{:S(2)}) collective-permute-start(bf16[8,64,1152]{2,1,0:T(8,128)(2,1)S(1)} %slice.398), channel_id=1, source_target_pairs={{0,4},{1,3},{2,6},{3,1},{4,0},{5,7},{6,2},{7,5},{8,12},{9,11},{10,... | collective-permute-start | bytes 3538952 | tf_op jit(solution)/shard_map/ppermute | solution.py:518
  233.5 5.2 %collective-permute-start.16 = (bf16[144,512]{1,0:T(8,128)(2,1)S(1)}, bf16[144,512]{1,0:T(8,128)(2,1)S(1)}, u32[]{:S(2)}, u32[]{:S(2)}) collective-permute-start(bf16[144,512]{1,0:T(8,128)(2,1)S(1)} %pad_maximum_fusion.11), channel_id=1, source_target_pairs={{0,8},{1,9},{2,10},{3,11},{4,12},{5,13},{6,14},{7,15},{8,0},{9,1},... | collective-permute-start | bytes 442376 | tf_op jit(solution)/shard_map/ppermute | solution.py:518
  248.3 9.9 %collective-permute-start.20 = (bf16[4,64,1152]{2,1,0:T(8,128)(2,1)S(1)}, bf16[4,64,1152]{2,1,0:T(8,128)(2,1)S(1)}, u32[]{:S(2)}, u32[]{:S(2)}) collective-permute-start(bf16[4,64,1152]{2,1,0:T(8,128)(2,1)S(1)} %slice.399), channel_id=1, source_target_pairs={{0,2},{1,5},{2,0},{3,7},{4,6},{5,1},{6,4},{7,3},{8,10},{9,13},{10,... | collective-permute-start | bytes 1769480 | tf_op jit(solution)/shard_map/ppermute | solution.py:518
  249.7 5.6 %collective-permute-start.17 = (bf16[80,512]{1,0:T(8,128)(2,1)S(1)}, bf16[80,512]{1,0:T(8,128)(2,1)S(1)}, u32[]{:S(2)}, u32[]{:S(2)}) collective-permute-start(bf16[80,512]{1,0:T(8,128)(2,1)S(1)} %pad_maximum_fusion.13), channel_id=1, source_target_pairs={{0,16},{1,17},{2,18},{3,19},{4,20},{5,21},{6,22},{7,23},{8,24},{9,... | collective-permute-start | bytes 245768 | tf_op jit(solution)/shard_map/ppermute | solution.py:518
  258.4 8.1 %collective-permute-start.21 = (bf16[2,64,1152]{2,1,0:T(8,128)(2,1)S(1)}, bf16[2,64,1152]{2,1,0:T(8,128)(2,1)S(1)}, u32[]{:S(2)}, u32[]{:S(2)}) collective-permute-start(bf16[2,64,1152]{2,1,0:T(8,128)(2,1)S(1)} %slice.401), channel_id=1, source_target_pairs={{0,8},{1,9},{2,10},{3,11},{4,12},{5,13},{6,14},{7,15},{8,0},{9,1},... | collective-permute-start | bytes 884744 | tf_op jit(solution)/shard_map/ppermute | solution.py:518
  259.2 0.7 copy-start.4
  266.6 7.7 %collective-permute-start.22 = (bf16[1,64,1152]{2,1,0:T(8,128)(2,1)S(1)}, bf16[1,64,1152]{2,1,0:T(8,128)(2,1)S(1)}, u32[]{:S(2)}, u32[]{:S(2)}) collective-permute-start(bf16[1,64,1152]{2,1,0:T(8,128)(2,1)S(1)} %slice.404), channel_id=1, source_target_pairs={{0,16},{1,17},{2,18},{3,19},{4,20},{5,21},{6,22},{7,23},{8,24},{9,... | collective-permute-start | bytes 442376 | tf_op jit(solution)/shard_map/ppermute | solution.py:518

commit v2 on v1

v2 whole, which is shorter than its diff:
```python
from functools import partial
import math

import jax
import jax.numpy as jnp
from jax import lax
from jax.experimental import pallas as pl
from jax.experimental.pallas import tpu as pltpu
from jax.sharding import PartitionSpec as P

D = 512
FF = 2048
HEAD_DIM = 64
SPAN = 128
LANES = 128
EPSILON = 1e-05
NEGATIVE = -1e30
SCALE = 1.0 / math.sqrt(HEAD_DIM)
F32 = jnp.float32
BF16 = jnp.bfloat16
AXES = ("seq", "mp")
MIB = 1 << 20
VMEM = pl.BlockSpec(memory_space=pltpu.VMEM)
SMEM = pl.BlockSpec(memory_space=pltpu.SMEM)
ANY = pl.BlockSpec(memory_space=pl.ANY)


def dot(left, right):
    return lax.dot_general(left, right, (((1,), (0,)), ((), ())), preferred_element_type=F32)


def dot_cols(left, right):
    return lax.dot_general(left, right, (((1,), (1,)), ((), ())), preferred_element_type=F32)


def unit(rows):
    centred = rows - jnp.mean(rows, axis=-1, keepdims=True)
    inverse = lax.rsqrt(jnp.mean(centred * centred, axis=-1, keepdims=True) + EPSILON)
    return centred * inverse, inverse


def unit_back(grad, hat, inverse):
    shift = jnp.mean(grad, axis=-1, keepdims=True)
    slope = jnp.mean(grad * hat, axis=-1, keepdims=True)
    return (grad - shift - hat * slope) * inverse


def row_info(place, offsets, lengths, mi):
    ends = []
    for c in range(lengths.shape[1]):
        ends.append(lengths[mi, c] + (ends[-1] if ends else 0))
    return place[0], offsets[mi], ends


def doc_start(positions, ends):
    start = jnp.zeros_like(positions)
    for end in ends:
        start = jnp.where(positions >= end, end, start)
    return start


def summary_range(summary_ids, offset, ends):
    last = offset - 1 + SPAN * summary_ids
    first = jnp.maximum(doc_start(last, ends), last - (SPAN - 1))
    return first, last


def iota(shape, dim):
    return lax.broadcasted_iota(jnp.int32, shape, dim)


def roll_rows(ref, by):
    whole = pl.multiple_of((by // 8) * 8, 8)
    return pltpu.roll(ref[pl.ds(whole, SPAN + 8), :], SPAN + 8 - (by - whole), axis=0)[:SPAN]


def prepare_kernel(
    place, offsets, lengths, x_ref, cot_ref, wq_ref, wk_ref, wv_ref, out_ref, x_edge_ref, cot_edge_ref, sem
):
    rows = x_ref.shape[1]
    last_rows = pl.multiple_of(place[1] * rows + (rows - SPAN), SPAN)
    copy = pltpu.make_async_copy(cot_ref.at[:, pl.ds(last_rows, SPAN), :], cot_edge_ref, sem.at[0])
    copy.start()
    shard = wq_ref.shape[0]
    for i, ref in enumerate((wq_ref, wk_ref, wv_ref)):
        out_ref[0, 0:shard, i * LANES : (i + 1) * LANES] = ref[...]
    sums = []
    for mi in range(2):
        dev, offset, ends = row_info(place, offsets, lengths, mi)
        first, last = summary_range(dev * (rows // SPAN) + iota((8, 1), 0), offset, ends)
        pos = dev * rows + iota((1, rows), 1)
        member = jnp.where((pos >= first) & (pos <= last), 1.0, 0.0).astype(BF16)
        x_edge_ref[mi] = x_ref[mi, rows - SPAN :, :]
        hat, _ = unit(x_ref[mi].astype(F32))
        high = hat.astype(BF16)
        rest = (hat - high.astype(F32)).astype(BF16)
        total = dot(member, high) + dot(member, rest)
        sums.append(total * lax.rsqrt((last - first + 1).astype(F32)))
    both = jnp.concatenate(sums, axis=0).astype(BF16)
    for lane in range(D // LANES):
        out_ref[0, 16 * lane : 16 * lane + 16, 384:512] = both[:, lane * LANES : (lane + 1) * LANES]
    copy.wait()


def fill_masks(place, offsets, lengths, mi, bias_ref, tiles, summaries, length):
    dev, offset, ends = row_info(place, offsets, lengths, mi)
    ends_col = offset - 1 + SPAN * iota((summaries, 1), 0)
    for t in range(tiles):
        base = SPAN * (dev * tiles + t) + offset - SPAN
        qpos = base + iota((1, SPAN), 1)
        qpos = jnp.where(qpos < 0, qpos + length, qpos)
        kpos = base + iota((SPAN, 1), 0)
        kpos = jnp.where(kpos < 0, kpos + length, kpos)
        span_first = jnp.where(qpos >= base + SPAN, base + length, base)
        doc_first = doc_start(qpos, ends)
        local_ok = (kpos >= jnp.maximum(doc_first, span_first)) & (kpos <= qpos)
        summary_ok = (ends_col >= doc_first) & (ends_col < span_first)
        bias_ref[t, 0:SPAN, :] = jnp.where(local_ok, 0.0, NEGATIVE)
        bias_ref[t, SPAN : SPAN + summaries, :] = jnp.where(summary_ok, 0.0, NEGATIVE)


def split_heads(pair):
    low = iota(pair.shape, 1) < HEAD_DIM
    zero = jnp.zeros_like(pair)
    return jnp.concatenate((jnp.where(low, pair, zero), jnp.where(low, zero, pair)), axis=0)


def join_heads(turned):
    half = turned.shape[1] // 2
    return jnp.concatenate((turned[:HEAD_DIM, :half], turned[HEAD_DIM:, half:]), axis=0).T


def project_kernel(
    apart, place_ref, offsets, lengths, block_of, row_of, slots_ref, x_ref, left_ref, gain, shift, qbias, vbias,
    near_ref, far_ref, *refs
):
    if apart:
        all_ref, *refs = refs
    xs_ref, qkv_ref, skv_ref, sums_ref, w_ref, stack_ref, wide_ref, rows_ref, sem = refs
    rows = x_ref.shape[1]
    tiles = rows // SPAN
    summaries = skv_ref.shape[1]
    half, shard, _ = near_ref.shape

    def place(d, carry):
        for source, slot in ((near_ref, d), (far_ref, half + d)):
            here = pl.ds(pl.multiple_of(row_of[slot] * shard, 16), shard)
            cols = pl.ds(pl.multiple_of(block_of[slot] * 384, 128), 384)
            pltpu.make_async_copy(source.at[d, :, 0:384], w_ref.at[here, cols], sem.at[0]).start()
            if not apart:
                pltpu.make_async_copy(
                    source.at[d, 0:64, 384:512], stack_ref.at[slot], sem.at[1]
                ).start()
        return carry

    lax.fori_loop(0, half, place, 0)
    if apart:
        pltpu.make_async_copy(all_ref, stack_ref, sem.at[1]).start()
    for mi in range(2):
        wide_ref[0:SPAN, :] = left_ref[mi].astype(F32)
        wide_ref[SPAN : SPAN + rows, :] = x_ref[mi].astype(F32)
        for t in range(tiles):
            here = slice(t * SPAN, (t + 1) * SPAN)
            rolled = roll_rows(wide_ref, t * SPAN + offsets[mi])
            xs_ref[mi, here, :] = rolled.astype(BF16)
            hat, _ = unit(rolled)
            rows_ref[mi, here, :] = (hat * gain[...] + shift[...]).astype(BF16)
    pltpu.make_async_copy(stack_ref, stack_ref, sem.at[1]).wait()
    roots = []
    for mi in range(2):
        _, offset, ends = row_info(place_ref, offsets, lengths, mi)
        first, last = summary_range(iota((summaries, 1), 0), offset, ends)
        root = jnp.sqrt((last - first + 1).astype(F32))
        roots.append(root)
        for base in range(0, stack_ref.shape[0], 32):
            named = slots_ref[mi : mi + 1, 16 * base : 16 * base + 512]
            pick = jnp.where(iota((summaries, 1), 0) == named, 1.0, 0.0).astype(BF16)
            piece = jnp.concatenate(
                [
                    stack_ref[base : base + 32, 16 * lane : 16 * lane + 16, :].reshape(512, LANES)
                    for lane in range(D // LANES)
                ],
                axis=1,
            )
            found = dot(pick, piece)
            sums_ref[mi] = found if base == 0 else sums_ref[mi] + found
        summed = sums_ref[mi] * gain[...] + root * shift[...]
        high = summed.astype(BF16)
        rows_ref[mi, rows : rows + summaries, :] = high
        rows_ref[mi, rows + summaries : rows + 2 * summaries, :] = (summed - high.astype(F32)).astype(BF16)
    pltpu.make_async_copy(w_ref, w_ref, sem.at[0]).wait()
    none = jnp.zeros((1, LANES), F32)
    for m in range(4):
        lanes = slice(m * LANES, (m + 1) * LANES)
        cols = slice(m * 384, (m + 1) * 384)
        bias = jnp.concatenate((qbias[:, lanes], none, vbias[:, lanes]), axis=1)
        for mi in range(2):
            projected = dot(rows_ref[mi], w_ref[:, cols])
            qkv_ref[mi, :, cols] = (projected[:rows] + bias).astype(BF16)
            pooled = projected[rows : rows + summaries] + projected[rows + summaries :]
            skv_ref[mi, :, cols] = (pooled + roots[mi] * bias).astype(BF16)


def pair_of(ref, here, pair):
    def part(i):
        return ref[0, here, pl.ds(pl.multiple_of(pair * 384 + i * LANES, LANES), LANES)]

    return part(0), part(1), part(2)


def attend_kernel(mi, place, offsets, lengths, qkv_ref, skv_ref, *refs):
    att_ref, lse_ref, bias_ref = refs[-3:]
    rows = qkv_ref.shape[1]
    tiles = rows // SPAN
    summaries = skv_ref.shape[1]
    fill_masks(place, offsets, lengths, mi, bias_ref, tiles, summaries, summaries * SPAN)

    def heads(pair, carry):
        lanes = pl.ds(pl.multiple_of(pair * LANES, LANES), LANES)
        _, skeys, svalues = pair_of(skv_ref, slice(None), pair)
        svalues = svalues.T
        spans = [pair_of(qkv_ref, slice(t * SPAN, (t + 1) * SPAN), pair) for t in range(tiles)]
        scores = []
        for t, (queries, keys, _) in enumerate(spans):
            bias = bias_ref[t]
            keys = jnp.concatenate((keys, skeys), axis=0)
            scores.append(dot_cols(keys, split_heads(queries * SCALE)) + jnp.concatenate((bias, bias), axis=1))
        probs = []
        for t in range(tiles):
            top = jnp.max(scores[t], axis=0, keepdims=True)
            grown = jnp.exp(scores[t] - top)
            total = jnp.sum(grown, axis=0, keepdims=True)
            probs.append((grown * (1.0 / total)).astype(BF16))
            lse_ref[0, pair, t] = top + jnp.log(total)
        for t, (_, _, values) in enumerate(spans):
            values = jnp.concatenate((values.T, svalues), axis=1)
            att_ref[0, t * SPAN : (t + 1) * SPAN, lanes] = join_heads(dot(values, probs[t])).astype(BF16)
        return carry

    lax.fori_loop(0, 4, heads, 0)


def gelu_pair(u):
    c0 = math.sqrt(2.0 / math.pi)
    square = u * u
    t = jnp.tanh(c0 * u * (1.0 + 0.044715 * square))
    half = 0.5 * (1.0 + t)
    slope = half + (0.5 * c0) * u * (1.0 - t * t) * (1.0 + (3 * 0.044715) * square)
    return u * half, slope


def mlp_kernel(
    place_ref, offsets, block_of, row_of, xs_ref, att_ref, left_ref, obias, gain, shift, ubias, dbias, cot_ref,
    near_ref, far_ref,
    result_ref, gmid_ref, edge_ref, gatt_ref, small_ref, gub_ref, keep_ref, send_ref,
    wo_ref, wu_ref, wd_ref, resid_ref, acc_ref, gn_ref, n_ref, c_ref, nt_ref, ct_ref, gu_ref, gd_ref, go_ref,
    guw_ref, gdw_ref, gow_ref, wide_ref, low_ref, sem, out_sem,
):
    rows = xs_ref.shape[1]
    tiles = rows // SPAN
    half, shard, _ = near_ref.shape
    own = pl.ds(pl.multiple_of(place_ref[1] * rows, SPAN), rows)
    own_copy = pltpu.make_async_copy(cot_ref.at[:, own, :], low_ref, sem.at[3])
    own_copy.start()

    def columns(block, width):
        return pl.ds(pl.multiple_of(block * width, 128), width)

    def place(first):
        def body(d, carry):
            for source, slot in ((near_ref, d), (far_ref, half + d)):
                here = pl.ds(pl.multiple_of(row_of[slot] * shard, 16), shard)
                block = block_of[slot]
                if first:
                    pltpu.make_async_copy(
                        source.at[d, :, 0:128], wo_ref.at[here, columns(block, 128)], sem.at[0]
                    ).start()
                else:
                    wide = columns(block, 512)
                    pltpu.make_async_copy(source.at[d, :, 128:640], wu_ref.at[here, wide], sem.at[1]).start()
                    pltpu.make_async_copy(source.at[d, :, 640:1152], wd_ref.at[here, wide], sem.at[2]).start()
            return carry

        lax.fori_loop(0, half, body, 0)

    place(True)
    place(False)
    small_ref[...] = jnp.zeros_like(small_ref)
    gub_ref[...] = jnp.zeros_like(gub_ref)
    gow_ref[...] = jnp.zeros_like(gow_ref)
    own_copy.wait()
    pltpu.make_async_copy(wo_ref, wo_ref, sem.at[0]).wait()
    for mi in range(2):
        all_rows = slice(mi * rows, (mi + 1) * rows)
        wide_ref[0:SPAN, :] = left_ref[mi].astype(F32)
        wide_ref[SPAN : SPAN + rows, :] = low_ref[mi].astype(F32)
        for t in range(tiles):
            rolled = roll_rows(wide_ref, t * SPAN + offsets[mi])
            small_ref[3:4, :] += jnp.sum(rolled, axis=0, keepdims=True)
            c_ref[mi * rows + t * SPAN : mi * rows + (t + 1) * SPAN, :] = rolled.astype(BF16)
        resid = xs_ref[mi].astype(F32) + dot_cols(att_ref[mi], wo_ref[...]) + obias[...]
        resid_ref[all_rows, :] = resid
        hat, _ = unit(resid)
        normed = (hat * gain[...] + shift[...]).astype(BF16)
        n_ref[all_rows, :] = normed
        nt_ref[:, all_rows] = normed.T
        ct_ref[:, all_rows] = c_ref[all_rows, :].T
        acc_ref[all_rows, :] = resid + dbias[...]
        gn_ref[all_rows, :] = jnp.zeros((rows, D), F32)
    pltpu.make_async_copy(wu_ref, wu_ref, sem.at[1]).wait()
    pltpu.make_async_copy(wd_ref, wd_ref, sem.at[2]).wait()

    def emit(pick, copies):
        def body(d, carry):
            for target, slot in ((keep_ref, d), (send_ref, half + d)):

                @pl.when(pick(block_of[slot]))
                def _():
                    here = pl.ds(pl.multiple_of(row_of[slot] * shard, 16), shard)
                    for source, width, cols, i in copies:
                        pltpu.make_async_copy(
                            source.at[here, columns(block_of[slot], width)], target.at[d, :, cols], out_sem.at[i]
                        ).start()

            return carry

        lax.fori_loop(0, half, body, 0)

    def chunk(ch, carry):
        cols = columns(ch, 512)
        for mi in range(2):
            here = slice(mi * rows, (mi + 1) * rows)
            w_up, w_down = wu_ref[:, cols], wd_ref[:, cols]
            act, slope = gelu_pair(dot(n_ref[here, :], w_up) + ubias[:, cols])
            act = act.astype(BF16)
            grad = (dot(c_ref[here, :], w_down) * slope).astype(BF16)
            acc_ref[here, :] += dot_cols(act, w_down)
            gn_ref[here, :] += dot_cols(grad, w_up)
            grad_up, grad_down = dot(nt_ref[:, here], grad), dot(ct_ref[:, here], act)
            if mi == 0:
                guw_ref[...] = grad_up
                gdw_ref[...] = grad_down
            else:
                gu_ref[:, cols] = (guw_ref[...] + grad_up).astype(BF16)
                gd_ref[:, cols] = (gdw_ref[...] + grad_down).astype(BF16)
            gub_ref[:, cols] += jnp.sum(grad.astype(F32), axis=0, keepdims=True)
        emit(lambda b: b == ch, ((gu_ref, 512, slice(128, 640), 1), (gd_ref, 512, slice(640, 1152), 2)))
        return carry

    lax.fori_loop(0, 4, chunk, 0)
    for mi in range(2):
        here = slice(mi * rows, (mi + 1) * rows)
        result_ref[mi] = acc_ref[here, :].astype(BF16)
        hat, inverse = unit(resid_ref[here, :])
        grad = gn_ref[here, :]
        small_ref[0:1, :] += jnp.sum(grad * hat, axis=0, keepdims=True)
        small_ref[1:2, :] += jnp.sum(grad, axis=0, keepdims=True)
        branch = (c_ref[here, :].astype(F32) + unit_back(grad * gain[...], hat, inverse)).astype(BF16)
        gmid_ref[mi] = branch
        edge_ref[0, mi] = result_ref[mi, 0:SPAN, :]
        edge_ref[1, mi] = branch[0:SPAN]
        small_ref[2:3, :] += jnp.sum(branch.astype(F32), axis=0, keepdims=True)
        gatt_ref[mi] = dot(branch, wo_ref[...]).astype(BF16)
        grad_out = dot(branch.T, att_ref[mi])
        gow_ref[...] = grad_out if mi == 0 else gow_ref[...] + grad_out
    go_ref[...] = gow_ref[...].astype(BF16)
    emit(lambda b: b >= 0, ((go_ref, 128, slice(0, 128), 0),))
    pltpu.make_async_copy(gu_ref, gu_ref, out_sem.at[1]).wait()
    pltpu.make_async_copy(gd_ref, gd_ref, out_sem.at[2]).wait()
    pltpu.make_async_copy(go_ref, go_ref, out_sem.at[0]).wait()


def attend_back_kernel(mi, place, offsets, lengths, qkv_ref, skv_ref, lse_ref, gatt_ref, *refs):
    grad_ref, pooled_ref, bias_ref = refs[-3:]
    rows = qkv_ref.shape[1]
    tiles = rows // SPAN
    summaries = skv_ref.shape[1]
    fill_masks(place, offsets, lengths, mi, bias_ref, tiles, summaries, summaries * SPAN)

    def heads(pair, carry):
        lanes = pl.ds(pl.multiple_of(pair * LANES, LANES), LANES)

        def columns(i):
            return pl.ds(pl.multiple_of(pair * 384 + i * LANES, LANES), LANES)

        _, skeys, svalues = pair_of(skv_ref, slice(None), pair)
        skeys_t = skeys.T
        sum_k = jnp.zeros((summaries, LANES), F32)
        sum_v = jnp.zeros((summaries, LANES), F32)
        held = []
        for t in range(tiles):
            here = slice(t * SPAN, (t + 1) * SPAN)
            queries, keys, values = pair_of(qkv_ref, here, pair)
            queries = split_heads(queries * SCALE)
            grads = split_heads(gatt_ref[0, here, lanes])
            bias = bias_ref[t]
            scores = dot_cols(jnp.concatenate((keys, skeys), axis=0), queries)
            gprobs = dot_cols(jnp.concatenate((values, svalues), axis=0), grads)
            held.append((queries, keys, grads, scores + jnp.concatenate((bias, bias), axis=1), gprobs))
        for t, (queries, keys, grads, scores, gprobs) in enumerate(held):
            here = slice(t * SPAN, (t + 1) * SPAN)
            probs = jnp.exp(scores - lse_ref[0, pair, t])
            delta = jnp.sum(probs * gprobs, axis=0, keepdims=True)
            gscores = (probs * (gprobs - delta)).astype(BF16)
            keys_t = jnp.concatenate((keys.T, skeys_t), axis=1)
            grad_q = join_heads(dot(keys_t, gscores)) * SCALE
            grad_k = dot(gscores, queries)
            grad_v = dot(probs.astype(BF16), grads)
            grad_ref[0, here, columns(0)] = grad_q.astype(BF16)
            grad_ref[0, here, columns(1)] = grad_k[:SPAN].astype(BF16)
            grad_ref[0, here, columns(2)] = grad_v[:SPAN].astype(BF16)
            sum_k += grad_k[SPAN:]
            sum_v += grad_v[SPAN:]
        pooled_ref[0, :, columns(0)] = jnp.zeros((summaries, LANES), BF16)
        pooled_ref[0, :, columns(1)] = sum_k.astype(BF16)
        pooled_ref[0, :, columns(2)] = sum_v.astype(BF16)
        return carry

    lax.fori_loop(0, 4, heads, 0)


def weights_back_kernel(
    apart, place, offsets, lengths, block_of, row_of, slots_ref, xs_ref, grad_ref, pooled_ref, sums_ref, w_ref,
    gain, shift, small_ref, gub_ref, line_ref, keep_ref, send_ref, *refs
):
    if apart:
        all_ref, *refs = refs
    gwb_ref, back_ref, stack_ref, pad_ref, sem = refs
    rows = xs_ref.shape[1]
    summaries = pooled_ref.shape[1]
    half = block_of.shape[0] // 2
    shard = keep_ref.shape[0] // half
    turned = []
    column = jnp.zeros((1, 3 * D), F32)
    for mi in range(2):
        _, offset, ends = row_info(place, offsets, lengths, mi)
        first, last = summary_range(iota((summaries, 1), 0), offset, ends)
        root = jnp.sqrt((last - first + 1).astype(F32))
        hat, _ = unit(xs_ref[mi].astype(F32))
        turned += [hat.astype(BF16).T, sums_ref[mi].astype(BF16).T]
        column += jnp.sum(grad_ref[mi].astype(F32), axis=0, keepdims=True)
        column += jnp.sum(root * pooled_ref[mi].astype(F32), axis=0, keepdims=True)
        back_ref[mi] = dot_cols(pooled_ref[mi], w_ref[...]).astype(BF16)
    turned = jnp.concatenate(turned, axis=1)
    gain_col, shift_col = gain[...].T, shift[...].T
    grad_gain = jnp.zeros((D, 1), F32)
    grad_shift = jnp.zeros((D, 1), F32)
    for m in range(4):
        cols = slice(m * 384, (m + 1) * 384)
        lanes = slice(m * LANES, (m + 1) * LANES)
        grads = jnp.concatenate([ref[mi, :, cols] for mi in range(2) for ref in (grad_ref, pooled_ref)], axis=0)
        hats, w, sums = dot(turned, grads), w_ref[:, cols].astype(F32), column[:, cols]
        grad_gain += jnp.sum(hats * w, axis=1, keepdims=True)
        grad_shift += jnp.sum(sums * w, axis=1, keepdims=True)
        gwb_ref[:, cols] = (hats * gain_col + shift_col * sums).astype(BF16)
        line_ref[10:11, lanes] = sums[:, :128]
        line_ref[11:12, lanes] = sums[:, 256:]
    line_ref[8:9, :] = grad_gain.T
    line_ref[9:10, :] = grad_shift.T
    line_ref[0:4, :] = small_ref[0:4, :]
    for i in range(4):
        line_ref[4 + i : 5 + i, :] = gub_ref[:, i * D : (i + 1) * D]
    line_ref[12:16, :] = jnp.zeros((4, D), F32)
    for base in range(0, stack_ref.shape[0], 32):
        names = [slots_ref[mi : mi + 1, 16 * base : 16 * base + 512] for mi in range(2)]
        spread = [
            jnp.where(iota((summaries, 1), 0) == named, 1.0, 0.0).astype(BF16).T for named in names
        ]
        piece = (dot(spread[0], back_ref[0]) + dot(spread[1], back_ref[1])).astype(BF16)
        for lane in range(D // LANES):
            part = piece[:, lane * LANES : (lane + 1) * LANES]
            stack_ref[base : base + 32, 16 * lane : 16 * lane + 16, :] = part.reshape(32, 16, LANES)

    def emit(d, carry):
        for target, slot in ((keep_ref, d), (send_ref, half + d)):
            first_row = pl.multiple_of(row_of[slot] * shard, 16)
            cols = pl.ds(pl.multiple_of(block_of[slot] * 384, 128), 384)
            here = target.at[pl.ds(pl.multiple_of(d * shard, 16), shard), :]
            pltpu.make_async_copy(
                gwb_ref.at[pl.ds(first_row, shard), cols], here.at[:, 0:384], sem.at[0]
            ).start()
            if not apart:
                pltpu.make_async_copy(stack_ref.at[slot], here.at[:, 384:512], sem.at[1]).start()
        return carry

    lax.fori_loop(0, half, emit, 0)
    if apart:
        pltpu.make_async_copy(stack_ref, all_ref, sem.at[1]).start()
    else:
        high = line_ref[...].astype(BF16)
        pad_ref[0:16, :] = high
        pad_ref[16:32, :] = (line_ref[...] - high.astype(F32)).astype(BF16)
        size = half * shard
        copy = pltpu.make_async_copy(pad_ref, send_ref.at[size : size + 32, :], sem.at[2])
        copy.start()
        copy.wait()
    pltpu.make_async_copy(gwb_ref, gwb_ref, sem.at[0]).wait()
    pltpu.make_async_copy(stack_ref, stack_ref, sem.at[1]).wait()


def rows_back_kernel(grad_ref, w_ref, gn_ref, edge_ref):
    gn_ref[0] = dot_cols(grad_ref[0], w_ref[...]).astype(BF16)
    edge_ref[0] = gn_ref[0, 0:SPAN, :]


def fold_kernel(keep_ref, mine_ref, got_ref, next_ref, *send_refs):
    size = keep_ref.shape[0]
    part = size // (1 + len(send_refs))
    mine = mine_ref[0:16, :].astype(F32) + mine_ref[16:32, :].astype(F32)
    lines = mine + (got_ref[size : size + 16, :].astype(F32) + got_ref[size + 16 : size + 32, :].astype(F32))
    high = lines.astype(BF16)
    rest = (lines - high.astype(F32)).astype(BF16)
    next_ref[...] = keep_ref[0:part, :].astype(F32) + got_ref[0:part, :].astype(F32)
    for i, send_ref in enumerate(send_refs):
        here = slice((i + 1) * part, (i + 2) * part)
        send_ref[0:part, :] = (keep_ref[here, :].astype(F32) + got_ref[here, :].astype(F32)).astype(BF16)
        send_ref[part : part + 16, :] = high
        send_ref[part + 16 : part + 32, :] = rest


def lines_of(ref):
    size = ref.shape[0] - 32
    return ref[size : size + 16, :].astype(F32) + ref[size + 16 : size + 32, :].astype(F32)


def two_tiles(ref, right, mi, t):
    if (t + 2) * SPAN <= ref.shape[1]:
        return ref[mi, t * SPAN : (t + 2) * SPAN, :]
    return jnp.concatenate((ref[mi, t * SPAN :, :], right[mi]), axis=0)


def unroll_kernel(offsets, result_ref, gmid_ref, right_ref, out_ref, part_ref, wide_ref):
    mi = pl.program_id(0)
    for t in range(result_ref.shape[1] // SPAN):
        here = slice(t * SPAN, (t + 1) * SPAN)
        for i, (ref, target) in enumerate(((result_ref, out_ref), (gmid_ref, part_ref))):
            wide_ref[i] = two_tiles(ref, right_ref.at[i], 0, t).astype(F32)
            target[0, here, :] = roll_rows(wide_ref.at[i], SPAN - offsets[mi]).astype(BF16)


def input_part_kernel(offsets, x_ref, gmid_ref, gn_ref, right_ref, gain, part_ref, wide_ref):
    mi = pl.program_id(0)
    for t in range(x_ref.shape[1] // SPAN):
        here = slice(t * SPAN, (t + 1) * SPAN)
        wide_ref[...] = two_tiles(gn_ref, right_ref, 0, t).astype(F32)
        grad = roll_rows(wide_ref, SPAN - offsets[mi])
        hat, inverse = unit(x_ref[0, here, :].astype(F32))
        part_ref[0, here, :] = gmid_ref[0, here, :].astype(F32) + unit_back(grad * gain[...], hat, inverse)


def finish_rest_kernel(keep_ref, a_ref, b_ref, c_ref, wo_ref, wu_ref, wd_ref):
    total = keep_ref[...] + (a_ref[...].astype(F32) + (b_ref[...].astype(F32) + c_ref[...].astype(F32)))
    wo_ref[...] = total[:, :128]
    wu_ref[...] = total[:, 128:640]
    wd_ref[...] = total[:, 640:]


def finish_kernel(
    direct, place, offsets, lengths, x_ref, part_ref, gain, *refs
):
    if direct:
        keep_ref, mine_ref, a_ref, b_ref, c_ref, out_ref, wq_ref, wk_ref, wv_ref, *line_refs = refs
        size = keep_ref.shape[0]
        total = (keep_ref[...] + a_ref[0:size, :].astype(F32)) + (
            b_ref[0:size, :].astype(F32) + c_ref[0:size, :].astype(F32)
        )
        wq_ref[...], wk_ref[...], wv_ref[...] = total[:, :128], total[:, 128:256], total[:, 256:384]
        pooled = total[:, 384:]
        lines = (lines_of(mine_ref) + lines_of(a_ref)) + (lines_of(b_ref) + lines_of(c_ref))
        ub_ref, *line_refs = line_refs
        for i in range(4):
            ub_ref[:, i * D : (i + 1) * D] = lines[4 + i : 5 + i, :]
        for ref, i in zip(line_refs, (0, 1, 2, 3, 8, 9, 10, 11)):
            ref[...] = lines[i : i + 1, :]
    else:
        pooled_ref, out_ref = refs
        pooled = pooled_ref[...]
    rows = x_ref.shape[1]
    for mi in range(2):
        dev, offset, ends = row_info(place, offsets, lengths, mi)
        first, last = summary_range(dev * (rows // SPAN) + iota((8, 1), 0), offset, ends)
        lows = jnp.concatenate(
            [pooled[16 * i + 8 * mi : 16 * i + 8 * mi + 8, :] for i in range(D // LANES)], axis=1
        )
        lows = (lows * gain[...] * lax.rsqrt((last - first + 1).astype(F32))).astype(BF16)
        first, last = summary_range(dev * (rows // SPAN) + iota((1, 8), 1), offset, ends)
        for t in range(rows // SPAN):
            here = slice(t * SPAN, (t + 1) * SPAN)
            pos = dev * rows + t * SPAN + iota((SPAN, 1), 0)
            member = jnp.where((pos >= first) & (pos <= last), 1.0, 0.0).astype(BF16)
            hat, inverse = unit(x_ref[mi, here, :].astype(F32))
            out_ref[mi, here, :] = part_ref[mi, here, :] + unit_back(dot(member, lows), hat, inverse)


def call(kernel, outs, in_specs, out_specs=None, scratch=(), limit=56, **more):
    return pl.pallas_call(
        kernel,
        out_shape=outs,
        in_specs=in_specs,
        out_specs=out_specs if out_specs is not None else [VMEM] * len(outs),
        scratch_shapes=list(scratch),
        compiler_params=pltpu.CompilerParams(vmem_limit_bytes=limit * MIB),
        cost_estimate=pl.CostEstimate(flops=1, bytes_accessed=1, transcendentals=0),
        **more,
    )


def call_row(kernel, mi, facts, arrays, outs, before, scratch, **more):
    def block(dims):
        return pl.BlockSpec((1,) + dims[1:], lambda i: (mi,) + (0,) * (len(dims) - 1))

    aliases = {3 + len(arrays) + i: i for i in range(len(before))}
    return call(
        partial(kernel, mi), outs, [SMEM] * 3 + [block(a.shape) for a in arrays] + [ANY] * len(before),
        [block(o.shape) for o in outs], scratch, grid=(1,), input_output_aliases=aliases, **more,
    )(*facts, *arrays, *before)


def tie(value, *others):
    return lax.optimization_barrier((value,) + others)[0]


def per_device(
    block_input, cotangent, span_offset, doc_lengths, ln1_gain, ln1_bias, w_query, w_key, w_value,
    query_bias, value_bias, w_out, out_bias, ln2_gain, ln2_bias, w_up, up_bias, w_down, down_bias,
):
    groups, ranks = lax.axis_size("seq"), lax.axis_size("mp")
    count = groups * ranks
    mp_index = lax.axis_index("mp")
    dev = lax.axis_index("seq") * ranks + mp_index
    rows = block_input.shape[1]
    tiles = rows // SPAN
    summaries = tiles * count
    shard = w_query.shape[0]
    bits = count.bit_length() - 1
    stages = [(b, b) for b in range(bits - 1, 2, -1)] + [(1, 2), (2, 1)]
    direct = shard == 64

    def swap(value, stage):
        pairs = [(i, i ^ (1 << stage[i & 1])) for i in range(count)]
        return lax.ppermute(value, AXES, pairs)

    def turn(value, by):
        return lax.ppermute(value, AXES, [(i, (i + by) % count) for i in range(count)])

    core = dev & 1
    slot = jnp.arange(count, dtype=jnp.int32)
    far = slot // (count // 2)
    mask = far
    for i, (even, odd) in enumerate(stages):
        where = jnp.where((core ^ far) == 0, even, odd)
        mask = mask | (((slot >> i) & 1) << where)
    owner = dev ^ mask
    if not direct:
        owner = slot
    member_slot = jnp.arange(16, dtype=jnp.int32)
    slots = owner[:, None] * tiles + (member_slot % 8)[None, :]
    valid = (member_slot % 8 <= tiles)[None, :]
    slots = jnp.stack(
        [
            jnp.where(valid & (member_slot // 8 == mi)[None, :], slots, -1).reshape(-1)
            for mi in range(2)
        ]
    )
    block_of, row_of = owner % ranks, owner // ranks
    facts = (jnp.stack((dev, mp_index)), span_offset, doc_lengths)

    def reach(value, flip):
        return lax.ppermute(value, AXES, [(i, i ^ flip) for i in range(count)])

    def spread(values):
        return [reach(value, flip) for value, flip in zip(values, (16, 8, 24))]

    def join(near, far):
        return jnp.concatenate((near, far), axis=0)

    def fold(keep, got):
        total = keep + got.astype(F32)
        half = total.shape[0] // 2
        return total[:half], total[half:].astype(BF16)

    def whole_blocks(arrays):
        return [pl.BlockSpec(a.shape, lambda i, n=len(a.shape): (0,) * n) for a in arrays]

    def fold_lines(keep, sent, got, sends=1):
        size = keep.shape[0]
        part = size // (1 + sends)
        outs = [shape((part, D), F32)] + [shape((part + 32, D), BF16)] * sends
        mine = pl.BlockSpec((32, D), lambda i: (size // 32, 0))
        both = whole_blocks((keep, got))
        return call(fold_kernel, outs, [both[0], mine, both[1]], whole_blocks(outs), grid=(1,))(keep, sent, got)

    def gather_whole(value):
        both = lax.all_gather(value, "seq", axis=0, tiled=True)
        both = lax.all_gather(both, "mp", axis=0)
        return both[: ranks // 2], both[ranks // 2 :]

    def scatter_whole(keep, send):
        both = jnp.concatenate((keep, send), axis=0).astype(F32)
        total = lax.psum_scatter(both, "mp", scatter_dimension=0, tiled=True)[0]
        return lax.psum_scatter(total, "seq", scatter_dimension=0, tiled=True)

    def row(vector):
        return vector[None, :]

    def shape(dims, kind):
        return jax.ShapeDtypeStruct(dims, kind)

    half, tall = (count // 2, shard) if direct else (ranks // 2, shard * groups)
    width = 4 * LANES if direct else 3 * LANES
    apart = not direct
    wide, three = (2, rows, D), (2, rows, 3 * D)
    flat, pooled_dims = (2 * rows, D), (2, summaries, D)
    masks = [pltpu.VMEM((tiles, SPAN + summaries, SPAN), F32)]
    w_rest = jnp.concatenate((w_out.T, w_up, w_down.T), axis=1)

    def prepare():
        return call(
            prepare_kernel, [shape((1, max(shard, 64), D), BF16)] + [shape((2, SPAN, D), BF16)] * 2,
            [SMEM] * 3 + [VMEM, ANY] + [VMEM] * 3, [VMEM] * 3,
            scratch=[pltpu.SemaphoreType.DMA((1,))],
        )(*facts, block_input, cotangent, w_query, w_key, w_value)

    part_a, x_edge, cot_edge = prepare()
    if direct:
        got_a = spread([part_a] * 3)
        x_left = turn(tie(x_edge, part_a), 1)
        part_b = tie(w_rest[None], got_a[0])
        got_b = spread([part_b] * 3)
        part_a = tie(jnp.concatenate([part_a] + got_a, axis=0), x_left)
        part_a = tie(join(part_a, swap(part_a, stages[2])), *got_b)
        got_a = swap(part_a, stages[3])
        part_b = tie(jnp.concatenate([part_b] + got_b, axis=0), part_a)
        got_b = swap(part_b, stages[2])
        near_a = join(part_a, got_a)
        far_a = swap(near_a, (0, 0))
        part_b = join(part_b, tie(got_b, near_a))
        got_b = swap(part_b, stages[3])
        cot_left = turn(tie(cot_edge, part_b), 1)
        more = ()
    else:
        x_left, cot_left = turn(x_edge, 1), turn(cot_edge, 1)
        near_a, far_a = gather_whole(part_a[0, :shard, :384])
        near_b, far_b = gather_whole(w_rest)
        more = (lax.all_gather(part_a[0, :64, 384:], AXES, axis=0),)
        block_of, row_of = jnp.arange(ranks, dtype=jnp.int32), jnp.zeros((ranks,), jnp.int32)

    xs, qkv, skv, sums, w_full = call(
        partial(project_kernel, apart),
        [shape(wide, BF16), shape(three, BF16), shape((2, summaries, 3 * D), BF16), shape(pooled_dims, F32)]
        + [shape((D, 3 * D), BF16)],
        [SMEM] * 5 + [VMEM] * 7 + [ANY] * (2 + len(more)),
        scratch=[
            pltpu.VMEM((count, 64, LANES), BF16),
            pltpu.VMEM((rows + SPAN, D), F32),
            pltpu.VMEM((2, rows + 2 * summaries, D), BF16),
            pltpu.SemaphoreType.DMA((2,)),
        ],
    )(
        *facts, block_of, row_of, slots, block_input, x_left, row(ln1_gain), row(ln1_bias),
        row(query_bias), row(value_bias), near_a, far_a, *more,
    )
    outs = [shape(wide, BF16), shape((2, 4, tiles, 1, 2 * SPAN), F32)]
    seen = call_row(attend_kernel, 0, facts, (qkv, skv), outs, (), masks)
    if direct:
        near_b = join(part_b, tie(got_b, seen[0], cot_left))
        far_b = swap(near_b, (0, 0))
        seen = [tie(seen[0], near_b)] + list(seen[1:])
    att, lse = call_row(attend_kernel, 1, facts, (qkv, skv), outs, tuple(seen), masks)
    result, gmid, edge, gatt, small_b, grad_ub, keep_b, send_b = call(
        mlp_kernel,
        [shape(wide, BF16)] * 2 + [shape((2, 2, SPAN, D), BF16), shape(wide, BF16)] + [shape((8, D), F32), shape((1, FF), F32)]
        + [shape((half, tall, 1152), BF16)] * 2,
        [SMEM] * 4 + [VMEM] * 8 + [ANY] * 3,
        [VMEM] * 6 + [ANY] * 2,
        scratch=[
            pltpu.VMEM((D, D), BF16), pltpu.VMEM((D, FF), BF16), pltpu.VMEM((D, FF), BF16),
            pltpu.VMEM(flat, F32), pltpu.VMEM(flat, F32), pltpu.VMEM(flat, F32),
            pltpu.VMEM(flat, BF16), pltpu.VMEM(flat, BF16),
            pltpu.VMEM((D, 2 * rows), BF16), pltpu.VMEM((D, 2 * rows), BF16),
            pltpu.VMEM((D, FF), BF16), pltpu.VMEM((D, FF), BF16), pltpu.VMEM((D, D), BF16),
            pltpu.VMEM((D, D), F32), pltpu.VMEM((D, D), F32), pltpu.VMEM((D, D), F32),
            pltpu.VMEM((rows + SPAN, D), F32), pltpu.VMEM(wide, BF16),
            pltpu.SemaphoreType.DMA((4,)), pltpu.SemaphoreType.DMA((3,)),
        ],
    )(
        facts[0], span_offset, block_of, row_of, xs, att, cot_left, row(out_bias), row(ln2_gain), row(ln2_bias),
        row(up_bias), row(down_bias), cotangent, near_b, far_b,
    )
    arrays = (qkv, skv, lse, gatt)
    outs = [shape(three, BF16), shape((2, summaries, 3 * D), BF16)]
    if direct:
        got_b = swap(send_b, (0, 0))
        back = turn(tie(edge, send_b), -1)
    grads = call_row(attend_back_kernel, 0, facts, arrays, outs, (), masks)
    if direct:
        keep_b, send_b = fold(keep_b.astype(F32), tie(got_b, grads[0], back))
        got_b = swap(send_b, stages[3])
        grads = [tie(grads[0], send_b)] + list(grads[1:])
    grads = call_row(attend_back_kernel, 1, facts, arrays, outs, tuple(grads), masks)
    lines, keep_a, send_a, *more = call(
        partial(weights_back_kernel, apart),
        [shape((16, D), F32)]
        + [shape((half * tall, width), BF16), shape((half * tall + (32 if direct else 0), width), BF16)]
        + [shape((count, 64, LANES), BF16)] * apart,
        [SMEM] * 5 + [VMEM] * 10,
        [VMEM] + [ANY] * (2 + apart),
        scratch=[
            pltpu.VMEM((D, 3 * D), BF16), pltpu.VMEM(pooled_dims, BF16), pltpu.VMEM((count, 64, LANES), BF16),
            pltpu.VMEM((32, D), BF16), pltpu.SemaphoreType.DMA((3,)),
        ],
    )(
        *facts, block_of, row_of, slots, xs, *grads, sums, w_full, row(ln1_gain), row(ln1_bias), small_b, grad_ub,
    )

    def by_row(dims):
        return pl.BlockSpec((1,) + dims[1:], lambda i: (i,) + (0,) * (len(dims) - 1))

    once = pl.BlockSpec((1, D), lambda i: (0, 0))
    edge_dims = (2, SPAN, D)

    def rows_back(*after):
        return call(
            rows_back_kernel, [shape(wide, BF16), shape(edge_dims, BF16)],
            [by_row(three), pl.BlockSpec((D, 3 * D), lambda i: (0, 0))], [by_row(wide), by_row(edge_dims)], grid=(2,),
        )(grads[0], tie(w_full, *after))

    def unroll(back):
        return call(
            unroll_kernel, [shape(wide, BF16)] * 2,
            [SMEM, by_row(wide), by_row(wide), pl.BlockSpec((2, 1, SPAN, D), lambda i: (0, i, 0, 0))],
            [by_row(wide)] * 2, [pltpu.VMEM((2, 2 * SPAN, D), F32)], grid=(2,),
        )(span_offset, result, gmid, back)

    def input_part(gmid, gn, back):
        return call(
            input_part_kernel, [shape(wide, F32)], [SMEM] + [by_row(wide)] * 3 + [by_row(edge_dims), once],
            [by_row(wide)], [pltpu.VMEM((2 * SPAN, D), F32)], grid=(2,),
        )(span_offset, block_input, gmid, gn, back, row(ln1_gain))[0]

    final = [SMEM] * 3 + [VMEM] * 3
    if direct:
        got_a = swap(send_a, (0, 0))
        keep_b, send_b = fold(keep_b, tie(got_b, send_a))
        got_b = swap(send_b, stages[2])
        gn, edge = rows_back(send_b)
        keep_a, send_a = fold_lines(keep_a, send_a, tie(got_a, gn))
        got_a = swap(send_a, stages[3])
        gn_back = turn(tie(edge, send_a), -1)
        total = keep_b + tie(got_b, send_a).astype(F32)
        got_b = spread([total[i].astype(BF16) for i in (1, 2, 3)])
        keep_b = total[0]
        result_own, gmid_own = unroll(tie(back, send_a))
        keep_a, send_a = fold_lines(keep_a, send_a, tie(got_a, gmid_own))
        got_a = swap(send_a, stages[2])
        part = input_part(gmid_own, gn, tie(gn_back, send_a))
        keep_a, *send_a = fold_lines(keep_a, send_a, tie(got_a, part), 3)
        got_a = spread(send_a)
        grad_wo, grad_wu, grad_wd = call(
            finish_rest_kernel, [shape((shard, LANES), F32), shape((shard, 512), F32), shape((shard, 512), F32)],
            [VMEM] * 4,
        )(keep_b, *(tie(got, send_a[0]) for got in got_b))
        input_grad, grad_wq, grad_wk, grad_wv, grad_ub, *small = call(
            partial(finish_kernel, True),
            [shape(wide, F32)] + [shape((shard, LANES), F32)] * 3 + [shape((1, FF), F32)] + [shape((1, D), F32)] * 8,
            final + [VMEM] * 5,
        )(*facts, block_input, part, row(ln1_gain), keep_a, send_a[0], *(tie(got, grad_wo) for got in got_a))
        grad_wo, grad_wd = grad_wo.T, grad_wd.T
        small = [a.reshape(D) for a in small]
        grad_ub = grad_ub.reshape(FF)
    else:
        keep_a, send_a = (a.reshape(half, tall, width) for a in (keep_a, send_a))
        result_own, gmid_own = unroll(turn(edge, -1))
        gn, edge = rows_back()
        part = input_part(gmid_own, gn, turn(edge, -1))
        sum_a, sum_b = scatter_whole(keep_a, send_a), scatter_whole(keep_b, send_b)
        grad_wq, grad_wk, grad_wv = (sum_a[:, i : i + LANES] for i in (0, 128, 256))
        grad_wo, grad_wu, grad_wd = sum_b[:, :128].T, sum_b[:, 128:640], sum_b[:, 640:].T
        pooled = lax.psum_scatter(more[0].astype(F32), AXES, scatter_dimension=0, tiled=True)[0]
        lines = lax.psum(lines, AXES)
        grad_ub = lines[4:8].reshape(FF)
        small = [lines[i] for i in (0, 1, 2, 3, 8, 9, 10, 11)]
        input_grad = call(partial(finish_kernel, False), [shape(wide, F32)], final + [VMEM])(
            *facts, block_input, part, row(ln1_gain), pooled
        )[0]
    grad_gain_two, grad_shift_two, grad_obias, grad_dbias, grad_gain_one, grad_shift_one, grad_qb, grad_vb = small
    return (
        result_own,
        input_grad,
        grad_gain_one,
        grad_shift_one,
        grad_wq,
        grad_wk,
        grad_wv,
        grad_qb,
        grad_vb,
        grad_wo,
        grad_obias,
        grad_gain_two,
        grad_shift_two,
        grad_wu,
        grad_ub,
        grad_wd,
        grad_dbias,
    )


def solution(mesh):
    vector, matrix, turned = P(), P("seq", "mp"), P("mp", "seq")
    own, group = P(None, ("seq", "mp"), None), P(None, "seq", None)
    return jax.shard_map(
        per_device,
        mesh=mesh,
        in_specs=(own, group, vector, vector, vector, vector, matrix, matrix, matrix, vector, vector)
        + (turned, vector, vector, vector, matrix, vector, turned, vector),
        out_specs=(own, own, vector, vector, matrix, matrix, matrix, vector, vector, turned, vector)
        + (vector, vector, matrix, vector, turned, vector),
        check_vma=False,
    )
```

time: 277 us -> 200 us (0.72)
  blocking collectives: 44.7 us -> 0 us
  waiting for transfers between devices: 59.6 us -> 36.4 us
  local copies, waits for them, and re-layouts: 24.4 us -> 11.4 us
  other arithmetic: 17.3 us -> 5.47 us
  starting transfers between devices: 27.7 us -> 39.5 us
  Pallas kernels: 94.2 us -> 105 us
  between operations: 7.72 us -> 1.16 us
    ppermute x20 -> x12, waiting for transfers between devices: 59.6 us -> 13.5 us  [swap(): return lax.ppermute(value, AXES, pairs)]
    psum x1 -> x0, blocking collectives: 44.7 us -> none  [per_device(): early = lax.psum((small_b[:4], grad_ub), AXES)]
    ppermute x0 -> x12, waiting for transfers between devices: none -> 22.9 us  [reach(): return lax.ppermute(value, AXES, [(i, i ^ flip) for i in range(count)])]
    ppermute x0 -> x12, starting transfers between devices: none -> 19.3 us  [reach(): return lax.ppermute(value, AXES, [(i, i ^ flip) for i in range(count)])]
    ppermute x20 -> x12, starting transfers between devices: 23.5 us -> 11.5 us  [swap(): return lax.ppermute(value, AXES, pairs)]
    pallas_call x6 -> x16, Pallas kernels: 94.2 us -> 105 us  [the longest x1 29.6 us: per_device(): call(mlp_kernel, [shape(wide, BF16)] * 2 + [shape((2, 2, SPAN, D), BF16),...]
    slice x21 -> x2, local copies, waits for them, and re-layouts: 5.94 us -> 0.23 us  [fold(): return (total[:half], total[half:].astype(BF16))]
    ppermute x3 -> x4, starting transfers between devices: 4.14 us -> 8.66 us  [turn(): lax.ppermute(value, AXES, [(i, (i + by) % count) for i in range(count)])]
  transfers between devices with their start and end apart: 23 -> 28, of which waited for: 12 -> 12; matrix products, arithmetic and copies ran while one was open for 12% -> 2% of each run, Pallas kernels for 11% -> 34%
where the time goes in v2:
time: 200 us; the launch traced here: 199 us
  Pallas kernels  105 us (52%)
  starting transfers between devices  39.5 us (20%)
  waiting for transfers between devices  36.4 us (18%)
  local copies, waits for them, and re-layouts  11.4 us (6%)
  other arithmetic  5.47 us (3%)
    pallas_call x1, Pallas kernels, per_device(): call(mlp_kernel, [shape(wide, BF16)] * 2 + [shape((2, 2, SPAN, D), BF16),...  29.6 us
    pallas_call x4, Pallas kernels, call_row(): call(partial(kernel, mi), outs, [SMEM] * 3 + [block(a.shape) for a in arr...  25.6 us
    ppermute x12, waiting for transfers between devices, reach(): return lax.ppermute(value, AXES, [(i, i ^ flip) for i in range(count)])  22.9 us
    ppermute x12, starting transfers between devices, reach(): return lax.ppermute(value, AXES, [(i, i ^ flip) for i in range(count)])  19.3 us
    ppermute x12, waiting for transfers between devices, swap(): return lax.ppermute(value, AXES, pairs)  13.5 us
    ppermute x12, starting transfers between devices, swap(): return lax.ppermute(value, AXES, pairs)  11.5 us
    pallas_call x1, Pallas kernels, per_device(): call(partial(weights_back_kernel, apart), [shape((16, D), F32)] + [shape(...  9.75 us
    pallas_call x1, Pallas kernels, per_device(): call(partial(project_kernel, apart), [shape(wide, BF16), shape(three, BF1...  8.74 us
  transfers between devices with their start and end apart: 28, of which 12 were waited for; matrix products, arithmetic and copies ran while one was open for 2% of the time, Pallas kernels for 34%

profile of v2, /device:TPU:0, one launch (start us, length us, event | category | flops | bytes accessed | tf_op | source)
XLA Modules:
  0.0 199.0 jit_solution(9727798136594079447)
XLA Ops:
  0.7 0.6 pad_add_fusion.1.place.place_ref
  1.3 3.8 %shard_map.314 = (bf16[1,64,512]{2,1,0:T(8,128)(2,1)}, bf16[2,128,512]{2,1,0:T(8,128)(2,1)}, bf16[2,128,512]{2,1,0:T(8,128)(2,1)}) custom-call(s32[2]{0:T(128)} %pad_add_fusion.1.place.place_ref, s32[2]{0:T(128)} %offsets.21, s32[2,8]{1,0:T(2,128)} %lengths.15, bf16[2,512,512]{2,1,0:T(8,128)(2,1)} %x_ref.7, bf16[2,2048,512]{2,1,0:T(8,128)(2,1)} %cot_ref.3, ...), custom_call_target="tpu_custom_call" | custom-call | flops 1 | bytes 1 | tf_op jit(solution)/shard_map/pallas_call | solution.py:718
  5.1 0.5 collective-permute-start
  5.6 4.7 %collective-permute-start.3 = (bf16[1,64,512]{2,1,0:T(8,128)(2,1)}, bf16[1,64,512]{2,1,0:T(8,128)(2,1)S(1)}, u32[]{:S(2)}, u32[]{:S(2)}) collective-permute-start(bf16[1,64,512]{2,1,0:T(8,128)(2,1)} %get-tuple-element.99), channel_id=1, source_target_pairs={{0,24},{1,25},{2,26},{3,27},{4,28},{5,29},{6,30},{7,31},{8,16},{9,... | collective-permute-start | bytes 196616 | tf_op jit(solution)/shard_map/ppermute | solution.py:669
  10.3 0.6 collective-permute-start.1
  10.9 1.9 collective-permute-done.3
  12.8 3.9 %collective-permute-done.2 = bf16[1,64,512]{2,1,0:T(8,128)(2,1)S(1)} collective-permute-done((bf16[1,64,512]{2,1,0:T(8,128)(2,1)}, bf16[1,64,512]{2,1,0:T(8,128)(2,1)S(1)}, u32[]{:S(2)}, u32[]{:S(2)}) %collective-permute-start.2) | collective-permute-done | bytes 65568 | tf_op jit(solution)/shard_map/ppermute | solution.py:669
  16.7 0.9 pad_maximum_fusion.2
  17.6 1.6 collective-permute-start.4
  19.2 2.4 %collective-permute-start.7 = (bf16[1,64,1152]{2,1,0:T(8,128)(2,1)S(1)}, bf16[1,64,1152]{2,1,0:T(8,128)(2,1)S(1)}, u32[]{:S(2)}, u32[]{:S(2)}) collective-permute-start(bf16[1,64,1152]{2,1,0:T(8,128)(2,1)S(1)} %maximum_bitcast_fusion), channel_id=1, source_target_pairs={{0,24},{1,25},{2,26},{3,27},{4,28},{5,29},{6,30},{7,31},{8,16},{9,... | collective-permute-start | bytes 442376 | tf_op jit(solution)/shard_map/ppermute | solution.py:669
  21.8 1.9 collective-permute-start.5
  24.1 3.7 %collective-permute-done.7 = bf16[1,64,1152]{2,1,0:T(8,128)(2,1)S(1)} collective-permute-done((bf16[1,64,1152]{2,1,0:T(8,128)(2,1)S(1)}, bf16[1,64,1152]{2,1,0:T(8,128)(2,1)S(1)}, u32[]{:S(2)}, u32[]{:S(2)}) %collective-permute-start.7) | collective-permute-done | bytes 147488 | tf_op jit(solution)/shard_map/ppermute | solution.py:669
  27.8 2.9 %collective-permute-done.6 = bf16[1,64,1152]{2,1,0:T(8,128)(2,1)S(1)} collective-permute-done((bf16[1,64,1152]{2,1,0:T(8,128)(2,1)S(1)}, bf16[1,64,1152]{2,1,0:T(8,128)(2,1)S(1)}, u32[]{:S(2)}, u32[]{:S(2)}) %collective-permute-start.6) | collective-permute-done | bytes 147488 | tf_op jit(solution)/shard_map/ppermute | solution.py:669
  30.7 4.7 %collective-permute-done.5 = bf16[1,64,1152]{2,1,0:T(8,128)(2,1)S(1)} collective-permute-done((bf16[1,64,1152]{2,1,0:T(8,128)(2,1)S(1)}, bf16[1,64,1152]{2,1,0:T(8,128)(2,1)S(1)}, u32[]{:S(2)}, u32[]{:S(2)}) %collective-permute-start.5) | collective-permute-done | bytes 147488 | tf_op jit(solution)/shard_map/ppermute | solution.py:669
  35.4 0.5 collective-permute-start.8
  36.1 1.9 collective-permute-start.10
  38.0 1.0 constant_dynamic-update-slice_fusion.3
  39.0 10.9 %collective-permute-done.8 = bf16[8,64,512]{2,1,0:T(8,128)(2,1)S(1)} collective-permute-done((bf16[8,64,512]{2,1,0:T(8,128)(2,1)S(1)}, bf16[8,64,512]{2,1,0:T(8,128)(2,1)S(1)}, u32[]{:S(2)}, u32[]{:S(2)}) %collective-permute-start.8) | collective-permute-done | bytes 524320 | tf_op jit(solution)/shard_map/ppermute | solution.py:641
  50.0 1.1 constant_dynamic-update-slice_fusion.2
  51.1 0.5 collective-permute-start.11
  51.6 0.8 collective-permute-start.9
  52.8 0.5 and_select_fusion.2
  53.4 0.6 pad_add_fusion.slots_ref
  54.0 0.8 collective-permute-done.9.far_ref
  54.8 8.7 %shard_map.315 = (bf16[2,512,512]{2,1,0:T(8,128)(2,1)}, bf16[2,512,1536]{2,1,0:T(8,128)(2,1)}, bf16[2,128,1536]{2,1,0:T(8,128)(2,1)}, f32[2,128,512]{2,1,0:T(8,128)}, bf16[512,1536]{1,0:T(8,128)(2,1)}) custom-call(s32[2]{0:T(128)} %pad_add_fusion.1.place.place_ref, s32[2]{0:T(128)} %offsets.21, s32[2,8]{1,0:T(2,128)} %lengths.15, ...), custom_call_target="tpu_custom_call" | custom-call | flops 1 | bytes 1 | tf_op jit(solution)/shard_map/pallas_call | solution.py:748
  63.5 5.6 %shard_map.316 = (bf16[2,512,512]{2,1,0:T(8,128)(2,1)}, f32[2,4,4,1,256]{4,3,2,1,0:T(1,128)}) custom-call(s32[2]{0:T(128)} %pad_add_fusion.1.place.place_ref, s32[2]{0:T(128)} %offsets.21, s32[2,8]{1,0:T(2,128)} %lengths.15, bf16[2,512,1536]{2,1,0:T(8,128)(2,1)} %get-tuple-element.105.qkv_ref, bf16[2,128,1536]{2,1,0:T(8,128)(2,1)} %get-tuple-element.106.skv_ref), custom_call_target="tpu_custom_call" | custom-call | flops 1 | bytes 1 | tf_op jit(solution)/shard_map/pallas_call | solution.py:613
  69.1 1.3 collective-permute-done.11
  70.4 1.4 constant_dynamic-update-slice_fusion.4.near_ref
  72.0 6.4 %shard_map.317 = (bf16[2,512,512]{2,1,0:T(8,128)(2,1)}, f32[2,4,4,1,256]{4,3,2,1,0:T(1,128)}) custom-call(s32[2]{0:T(128)} %pad_add_fusion.1.place.place_ref, s32[2]{0:T(128)} %offsets.21, s32[2,8]{1,0:T(2,128)} %lengths.15, bf16[2,512,1536]{2,1,0:T(8,128)(2,1)} %get-tuple-element.105.qkv_ref, ...), custom_call_target="tpu_custom_call", output_to_operand_aliasing={{0}: (5, {}), {1}: (6, {})} | custom-call | flops 1 | bytes 1 | tf_op jit(solution)/shard_map/pallas_call | solution.py:613
  78.3 1.5 copy-done.2
  79.8 29.6 %shard_map.318 = (bf16[2,512,512]{2,1,0:T(8,128)(2,1)}, bf16[2,512,512]{2,1,0:T(8,128)(2,1)}, bf16[2,2,128,512]{3,2,1,0:T(8,128)(2,1)}, bf16[2,512,512]{2,1,0:T(...) custom-call(s32[2]{0:T(128)} %pad_add_fusion.1.place.place_ref, ...), custom_call_target="tpu_custom_call" | custom-call | flops 1 | bytes 1 | tf_op jit(solution)/shard_map/pallas_call | solution.py:770
  109.5 3.3 %collective-permute-start.14 = (bf16[2,2,128,512]{3,2,1,0:T(8,128)(2,1)}, bf16[2,2,128,512]{3,2,1,0:T(8,128)(2,1)S(1)}, u32[]{:S(2)}, u32[]{:S(2)}) collective-permute-start(bf16[2,2,128,512]{3,2,1,0:T(8,128)(2,1)} %get-tuple-element.120), channel_id=1, source_target_pairs={{0,31},{1,0},{2,1},{3,2},{4,3},{5,4},{6,5},{7,6},{8,7},{9,8},{10,9... | collective-permute-start | bytes 1572872 | tf_op jit(solution)/shard_map/ppermute | solution.py:644
  112.8 7.0 %shard_map.319 = (bf16[2,512,1536]{2,1,0:T(8,128)(2,1)}, bf16[2,128,1536]{2,1,0:T(8,128)(2,1)}) custom-call(s32[2]{0:T(128)} %pad_add_fusion.1.place.place_ref, s32[2]{0:T(128)} %offsets.21, s32[2,8]{1,0:T(2,128)} %lengths.15, bf16[2,512,1536]{2,1,0:T(8,128)(2,1)} %get-tuple-element.105.qkv_ref, bf16[2,128,1536]{2,1,0:T(8,128)(2,1)} %get-tuple-element.106.skv_ref, ...), custom_call_target="tpu_custom_call" | custom-call | flops 1 | bytes 1 | tf_op jit(solution)/shard_map/pallas_call | solution.py:613
  119.8 0.8 copy-done.6
  120.7 0.7 copy-done.3
  121.4 2.2 %convert_add_fusion = f32[16,64,1152]{2,1,0:T(8,128)S(1)} fusion(bf16[16,64,1152]{2,1,0:T(8,128)(2,1)} %copy-done.3, bf16[16,64,1152]{2,1,0:T(8,128)(2,1)S(1)} %copy-done.1), kind=kLoop, calls=%fused_computation | loop fusion | flops 3538944 | bytes 9437184 | tf_op jit(solution)/shard_map/add | solution.py:678
  123.9 6.7 %shard_map.320 = (bf16[2,512,1536]{2,1,0:T(8,128)(2,1)}, bf16[2,128,1536]{2,1,0:T(8,128)(2,1)}) custom-call(s32[2]{0:T(128)} %pad_add_fusion.1.place.place_ref, s32[2]{0:T(128)} %offsets.21, s32[2,8]{1,0:T(2,128)} %lengths.15, bf16[2,512,1536]{2,1,0:T(8,128)(2,1)} %get-tuple-element.105.qkv_ref, ...), custom_call_target="tpu_custom_call", output_to_operand_aliasing={{0}: (7, {}), {1}: (8, {})} | custom-call | flops 1 | bytes 1 | tf_op jit(solution)/shard_map/pallas_call | solution.py:613
  130.5 9.8 %shard_map.321 = (f32[16,512]{1,0:T(8,128)}, bf16[1024,512]{1,0:T(8,128)(2,1)}, bf16[1056,512]{1,0:T(8,128)(2,1)}) custom-call(s32[2]{0:T(128)} %pad_add_fusion.1.place.place_ref, s32[2]{0:T(128)} %offsets.21, s32[2,8]{1,0:T(2,128)} %lengths.15, s32[32]{0:T(128)} %get-tuple-element.191.block_of, s32[32]{0:T(128)} %get-tuple-element.190.row_of, ...), custom_call_target="tpu_custom_call" | custom-call | flops 1 | bytes 1 | tf_op jit(solution)/shard_map/pallas_call | solution.py:801
  140.8 0.7 collective-permute-start.22
  141.4 4.8 %shard_map.322 = (bf16[2,512,512]{2,1,0:T(8,128)(2,1)}, bf16[2,128,512]{2,1,0:T(8,128)(2,1)}) custom-call(bf16[2,512,1536]{2,1,0:T(8,128)(2,1)} %get-tuple-element.128.grad_ref, bf16[512,1536]{1,0:T(8,128)(2,1)} %get-tuple-element.137.w_ref), custom_call_target="tpu_custom_call" | custom-call | flops 1 | bytes 1 | tf_op jit(solution)/shard_map/pallas_call | solution.py:823
  146.2 2.9 %shard_map.323 = (f32[512,512]{1,0:T(8,128)}, bf16[544,512]{1,0:T(8,128)(2,1)}) custom-call(bf16[1024,512]{1,0:T(8,128)(2,1)} %get-tuple-element.134.keep_ref, bf16[1056,512]{1,0:T(8,128)(2,1)} %get-tuple-element.135.mine_ref, bf16[1056,512]{1,0:T(8,128)(2,1)} %collective-permute-done.16.got_ref), custom_call_target="tpu_custom_call" | custom-call | flops 1 | bytes 1 | tf_op jit(solution)/shard_map/pallas_call | solution.py:691
  149.1 1.5 collective-permute-start.19
  150.6 4.6 %collective-permute-start.18 = (bf16[2,128,512]{2,1,0:T(8,128)(2,1)S(1)}, bf16[2,128,512]{2,1,0:T(8,128)(2,1)S(1)}, u32[]{:S(2)}, u32[]{:S(2)}) collective-permute-start(bf16[2,128,512]{2,1,0:T(8,128)(2,1)S(1)} %copy-done.19), channel_id=1, source_target_pairs={{0,31},{1,0},{2,1},{3,2},{4,3},{5,4},{6,5},{7,6},{8,7},{9,8},{10,9... | collective-permute-start | bytes 786440 | tf_op jit(solution)/shard_map/ppermute | solution.py:644
  155.3 4.1 %shard_map.324 = (bf16[2,512,512]{2,1,0:T(8,128)(2,1)}, bf16[2,512,512]{2,1,0:T(8,128)(2,1)}) custom-call(s32[2]{0:T(128)} %offsets.21, bf16[2,512,512]{2,1,0:T(8,128)(2,1)} %get-tuple-element.116.result_ref, bf16[2,512,512]{2,1,0:T(8,128)(2,1)} %get-tuple-element.117.gmid_ref, bf16[2,2,128,512]{3,2,1,0:T(8,128)(2,1)} %copy-done.6), custom_call_target="tpu_custom_call" | custom-call | flops 1 | bytes 1 | tf_op jit(solution)/shard_map/pallas_call | solution.py:829
  159.4 0.8 copy-done.5
  160.2 2.4 %shard_map.325 = (f32[256,512]{1,0:T(8,128)}, bf16[288,512]{1,0:T(8,128)(2,1)}) custom-call(f32[512,512]{1,0:T(8,128)} %get-tuple-element.146.keep_ref, bf16[544,512]{1,0:T(8,128)(2,1)} %get-tuple-element.140.mine_ref, bf16[544,512]{1,0:T(8,128)(2,1)} %copy-done.5), custom_call_target="tpu_custom_call" | custom-call | flops 1 | bytes 1 | tf_op jit(solution)/shard_map/pallas_call | solution.py:691
  162.5 3.7 %collective-permute-start.20 = (bf16[288,512]{1,0:T(8,128)(2,1)}, bf16[288,512]{1,0:T(8,128)(2,1)S(1)}, u32[]{:S(2)}, u32[]{:S(2)}) collective-permute-start(bf16[288,512]{1,0:T(8,128)(2,1)} %get-tuple-element.148.mine_ref), channel_id=1, source_target_pairs={{0,2},{1,5},{2,0},{3,7},{4,6},{5,1},{6,4},{7,3},{8,10},{9,13},{10,... | collective-permute-start | bytes 884744 | tf_op jit(solution)/shard_map/ppermute | solution.py:641
  166.5 4.5 %collective-permute-start.25 = (bf16[64,1152]{1,0:T(8,128)(2,1)S(1)}, bf16[64,1152]{1,0:T(8,128)(2,1)S(1)}, u32[]{:S(2)}, u32[]{:S(2)}) collective-permute-start(bf16[64,1152]{1,0:T(8,128)(2,1)S(1)} %get-tuple-element.181), channel_id=1, source_target_pairs={{0,24},{1,25},{2,26},{3,27},{4,28},{5,29},{6,30},{7,31},{8,16},{9,... | collective-permute-start | bytes 442376 | tf_op jit(solution)/shard_map/ppermute | solution.py:669
  171.0 0.7 copy-done.9
  171.7 4.8 %shard_map.326.part_ref = f32[2,512,512]{2,1,0:T(8,128)} custom-call(s32[2]{0:T(128)} %offsets.21, bf16[2,512,512]{2,1,0:T(8,128)(2,1)} %x_ref.7, bf16[2,512,512]{2,1,0:T(8,128)(2,1)} %get-tuple-element.143.gmid_ref, bf16[2,512,512]{2,1,0:T(8,128)(2,1)} %get-tuple-element.138.gn_ref, bf16[2,128,512]{2,1,0:T(8,128)(2,1)} %copy-done.9, f32[1,512]{1,0:T(1,128)} %bitcast.37), custom_call_target="tpu_custom_call" | custom-call | flops 1 | bytes 1 | tf_op jit(solution)/shard_map/pallas_call | solution.py:836
  176.5 0.6 collective-permute-start.23
  177.0 0.7 copy-done.7
  177.8 1.9 shard_map.327
  179.7 1.4 collective-permute-start.26
  181.1 2.4 %collective-permute-start.27 = (bf16[96,512]{1,0:T(8,128)(2,1)}, bf16[96,512]{1,0:T(8,128)(2,1)S(1)}, u32[]{:S(2)}, u32[]{:S(2)}) collective-permute-start(bf16[96,512]{1,0:T(8,128)(2,1)} %get-tuple-element.162), channel_id=1, source_target_pairs={{0,24},{1,25},{2,26},{3,27},{4,28},{5,29},{6,30},{7,31},{8,16},{9,... | collective-permute-start | bytes 294920 | tf_op jit(solution)/shard_map/ppermute | solution.py:669
  183.6 0.6 collective-permute-start.21
  184.1 0.7 slice_bitcast_fusion.keep_ref
  184.9 1.4 collective-permute-done.23.a_ref
  186.3 0.7 copy-done.12
  186.9 1.9 shard_map.328
  188.8 0.5 collective-permute-done.27.refs_4_
  189.3 3.9 %collective-permute-done.21.refs_2_ = bf16[96,512]{1,0:T(8,128)(2,1)S(1)} collective-permute-done((bf16[96,512]{1,0:T(8,128)(2,1)}, bf16[96,512]{1,0:T(8,128)(2,1)S(1)}, u32[]{:S(2)}, u32[]{:S(2)}) %collective-permute-start.21) | collective-permute-done | bytes 98336 | tf_op jit(solution)/shard_map/ppermute | solution.py:669
  193.2 0.6 copy-done.15
  193.8 4.9 %shard_map.329 = (f32[2,512,512]{2,1,0:T(8,128)}, f32[64,128]{1,0:T(8,128)}, f32[64,128]{1,0:T(8,128)}, f32[64,128]{1,0:T(8,128)}, f32[1,2048]{1,0:T(1,128)}, /*...) custom-call(s32[2]{0:T(128)} %pad_add_fusion.1.place.place_ref, ...), custom_call_target="tpu_custom_call" | custom-call | flops 1 | bytes 1 | tf_op jit(solution)/shard_map/pallas_call | solution.py:863
  (73 shorter events, 2.4 us)
Async XLA Ops:
  1.3 17.9 %copy-start.16 = (bf16[512,64]{0,1:T(8,128)(2,1)S(1)}, bf16[512,64]{0,1:T(8,128)(2,1)}, u32[]{:S(2)}) copy-start(bf16[512,64]{0,1:T(8,128)(2,1)} %param.36) | copy-start | bytes 196612
  1.3 17.9 %copy-start.17 = (bf16[64,512]{1,0:T(8,128)(2,1)S(1)}, bf16[64,512]{1,0:T(8,128)(2,1)}, u32[]{:S(2)}) copy-start(bf16[64,512]{1,0:T(8,128)(2,1)} %param.34) | copy-start | bytes 196612
  1.3 17.9 %copy-start.18 = (bf16[128,64]{0,1:T(8,128)(2,1)S(1)}, bf16[128,64]{0,1:T(8,128)(2,1)}, u32[]{:S(2)}) copy-start(bf16[128,64]{0,1:T(8,128)(2,1)} %param.30) | copy-start | bytes 49156
  5.1 12.5 %collective-permute-start = (bf16[2,128,512]{2,1,0:T(8,128)(2,1)}, bf16[2,128,512]{2,1,0:T(8,128)(2,1)S(1)}, u32[]{:S(2)}, u32[]{:S(2)}) collective-permute-start(bf16[2,128,512]{2,1,0:T(8,128)(2,1)} %get-tuple-element.100), channel_id=1, source_target_pairs={{0,1},{1,2},{2,3},{3,4},{4,5},{5,6},{6,7},{7,8},{8,9},{9,10},{10,1... | collective-permute-start | bytes 786440 | tf_op jit(solution)/shard_map/ppermute | solution.py:644
  5.6 7.2 %collective-permute-start.3 = (bf16[1,64,512]{2,1,0:T(8,128)(2,1)}, bf16[1,64,512]{2,1,0:T(8,128)(2,1)S(1)}, u32[]{:S(2)}, u32[]{:S(2)}) collective-permute-start(bf16[1,64,512]{2,1,0:T(8,128)(2,1)} %get-tuple-element.99), channel_id=1, source_target_pairs={{0,24},{1,25},{2,26},{3,27},{4,28},{5,29},{6,30},{7,31},{8,16},{9,... | collective-permute-start | bytes 196616 | tf_op jit(solution)/shard_map/ppermute | solution.py:669
  10.3 6.5 %collective-permute-start.2 = (bf16[1,64,512]{2,1,0:T(8,128)(2,1)}, bf16[1,64,512]{2,1,0:T(8,128)(2,1)S(1)}, u32[]{:S(2)}, u32[]{:S(2)}) collective-permute-start(bf16[1,64,512]{2,1,0:T(8,128)(2,1)} %get-tuple-element.99), channel_id=1, source_target_pairs={{0,8},{1,9},{2,10},{3,11},{4,12},{5,13},{6,14},{7,15},{8,0},{9,1},... | collective-permute-start | bytes 196616 | tf_op jit(solution)/shard_map/ppermute | solution.py:669
  10.3 6.5 %collective-permute-start.1 = (bf16[1,64,512]{2,1,0:T(8,128)(2,1)}, bf16[1,64,512]{2,1,0:T(8,128)(2,1)S(1)}, u32[]{:S(2)}, u32[]{:S(2)}) collective-permute-start(bf16[1,64,512]{2,1,0:T(8,128)(2,1)} %get-tuple-element.99), channel_id=1, source_target_pairs={{0,16},{1,17},{2,18},{3,19},{4,20},{5,21},{6,22},{7,23},{8,24},{9,... | collective-permute-start | bytes 196616 | tf_op jit(solution)/shard_map/ppermute | solution.py:669
  17.6 6.1 %copy-start.8 = (bf16[2,128,512]{2,1,0:T(8,128)(2,1)}, bf16[2,128,512]{2,1,0:T(8,128)(2,1)S(1)}, u32[]{:S(2)}) copy-start(bf16[2,128,512]{2,1,0:T(8,128)(2,1)S(1)} %collective-permute-done.left_ref) | copy-start | bytes 786436
  17.6 6.4 %collective-permute-start.4 = (bf16[4,64,512]{2,1,0:T(8,128)(2,1)S(1)}, bf16[4,64,512]{2,1,0:T(8,128)(2,1)S(1)}, u32[]{:S(2)}, u32[]{:S(2)}) collective-permute-start(bf16[4,64,512]{2,1,0:T(8,128)(2,1)S(1)} %pad_maximum_fusion.2), channel_id=1, source_target_pairs={{0,2},{1,5},{2,0},{3,7},{4,6},{5,1},{6,4},{7,3},{8,10},{9,13},{10,... | collective-permute-start | bytes 786440 | tf_op jit(solution)/shard_map/ppermute | solution.py:641
  19.2 8.6 %collective-permute-start.7 = (bf16[1,64,1152]{2,1,0:T(8,128)(2,1)S(1)}, bf16[1,64,1152]{2,1,0:T(8,128)(2,1)S(1)}, u32[]{:S(2)}, u32[]{:S(2)}) collective-permute-start(bf16[1,64,1152]{2,1,0:T(8,128)(2,1)S(1)} %maximum_bitcast_fusion), channel_id=1, source_target_pairs={{0,24},{1,25},{2,26},{3,27},{4,28},{5,29},{6,30},{7,31},{8,16},{9,... | collective-permute-start | bytes 442376 | tf_op jit(solution)/shard_map/ppermute | solution.py:669
  21.6 9.1 %collective-permute-start.6 = (bf16[1,64,1152]{2,1,0:T(8,128)(2,1)S(1)}, bf16[1,64,1152]{2,1,0:T(8,128)(2,1)S(1)}, u32[]{:S(2)}, u32[]{:S(2)}) collective-permute-start(bf16[1,64,1152]{2,1,0:T(8,128)(2,1)S(1)} %maximum_bitcast_fusion), channel_id=1, source_target_pairs={{0,8},{1,9},{2,10},{3,11},{4,12},{5,13},{6,14},{7,15},{8,0},{9,1},... | collective-permute-start | bytes 442376 | tf_op jit(solution)/shard_map/ppermute | solution.py:669
  21.8 13.7 %collective-permute-start.5 = (bf16[1,64,1152]{2,1,0:T(8,128)(2,1)S(1)}, bf16[1,64,1152]{2,1,0:T(8,128)(2,1)S(1)}, u32[]{:S(2)}, u32[]{:S(2)}) collective-permute-start(bf16[1,64,1152]{2,1,0:T(8,128)(2,1)S(1)} %maximum_bitcast_fusion), channel_id=1, source_target_pairs={{0,16},{1,17},{2,18},{3,19},{4,20},{5,21},{6,22},{7,23},{8,24},{9,... | collective-permute-start | bytes 442376 | tf_op jit(solution)/shard_map/ppermute | solution.py:669
  35.4 14.5 %collective-permute-start.8 = (bf16[8,64,512]{2,1,0:T(8,128)(2,1)S(1)}, bf16[8,64,512]{2,1,0:T(8,128)(2,1)S(1)}, u32[]{:S(2)}, u32[]{:S(2)}) collective-permute-start(bf16[8,64,512]{2,1,0:T(8,128)(2,1)S(1)} %pad_maximum_fusion.1), channel_id=1, source_target_pairs={{0,4},{1,3},{2,6},{3,1},{4,0},{5,7},{6,2},{7,5},{8,12},{9,11},{10,... | collective-permute-start | bytes 1572872 | tf_op jit(solution)/shard_map/ppermute | solution.py:641
  36.1 13.9 %collective-permute-start.10 = (bf16[4,64,1152]{2,1,0:T(8,128)(2,1)S(1)}, bf16[4,64,1152]{2,1,0:T(8,128)(2,1)S(1)}, u32[]{:S(2)}, u32[]{:S(2)}) collective-permute-start(bf16[4,64,1152]{2,1,0:T(8,128)(2,1)S(1)} %pad_maximum_fusion), channel_id=1, source_target_pairs={{0,2},{1,5},{2,0},{3,7},{4,6},{5,1},{6,4},{7,3},{8,10},{9,13},{10,... | collective-permute-start | bytes 1769480 | tf_op jit(solution)/shard_map/ppermute | solution.py:641
  50.0 4.8 %copy-start.4 = (bf16[16,64,512]{2,1,0:T(8,128)(2,1)}, bf16[16,64,512]{2,1,0:T(8,128)(2,1)S(1)}, u32[]{:S(2)}) copy-start(bf16[16,64,512]{2,1,0:T(8,128)(2,1)S(1)} %constant_dynamic-update-slice_fusion.near_ref) | copy-start | bytes 3145732
  51.1 19.3 %collective-permute-start.11 = (bf16[8,64,1152]{2,1,0:T(8,128)(2,1)}, bf16[8,64,1152]{2,1,0:T(8,128)(2,1)}, u32[]{:S(2)}, u32[]{:S(2)}) collective-permute-start(bf16[8,64,1152]{2,1,0:T(8,128)(2,1)} %get-tuple-element.184), channel_id=1, source_target_pairs={{0,4},{1,3},{2,6},{3,1},{4,0},{5,7},{6,2},{7,5},{8,12},{9,11},{10,... | collective-permute-start | bytes 3538952 | tf_op jit(solution)/shard_map/ppermute | solution.py:641
  51.6 3.2 %collective-permute-start.9 = (bf16[16,64,512]{2,1,0:T(8,128)(2,1)S(1)}, bf16[16,64,512]{2,1,0:T(8,128)(2,1)}, u32[]{:S(2)}, u32[]{:S(2)}) collective-permute-start(bf16[16,64,512]{2,1,0:T(8,128)(2,1)S(1)} %constant_dynamic-update-slice_fusion.near_ref), channel_id=1, source_target_pairs={{0,1},{1,0},{2,3},{3,2},{4,5},{5,4},{6,7},{7,6},{8,9},{9,8},{10,11... | collective-permute-start | bytes 3145736 | tf_op jit(solution)/shard_map/ppermute | solution.py:641
  52.4 16.7 %collective-permute-start.12 = (bf16[2,128,512]{2,1,0:T(8,128)(2,1)}, bf16[2,128,512]{2,1,0:T(8,128)(2,1)}, u32[]{:S(2)}, u32[]{:S(2)}) collective-permute-start(bf16[2,128,512]{2,1,0:T(8,128)(2,1)} %get-tuple-element.111), channel_id=1, source_target_pairs={{0,1},{1,2},{2,3},{3,4},{4,5},{5,6},{6,7},{7,8},{8,9},{9,10},{10,1... | collective-permute-start | bytes 786440 | tf_op jit(solution)/shard_map/ppermute | solution.py:644
  71.9 6.5 %copy-start = (bf16[16,64,1152]{2,1,0:T(8,128)(2,1)}, bf16[16,64,1152]{2,1,0:T(8,128)(2,1)S(1)}, u32[]{:S(2)}) copy-start(bf16[16,64,1152]{2,1,0:T(8,128)(2,1)S(1)} %constant_dynamic-update-slice_fusion.4.near_ref) | copy-start | bytes 7077892
  71.9 6.4 %collective-permute-start.13 = (bf16[16,64,1152]{2,1,0:T(8,128)(2,1)S(1)}, bf16[16,64,1152]{2,1,0:T(8,128)(2,1)S(1)}, u32[]{:S(2)}, u32[]{:S(2)}) collective-permute-start(bf16[16,64,1152]{2,1,0:T(8,128)(2,1)S(1)} %constant_dynamic-update-slice_fusion.4.near_ref), channel_id=1, source_target_pairs={{0,1},{1,0},{2,3},{3,2},{4,5},{5,4},{6,7},{7,6},{8,9},{9,8},{10,11... | collective-permute-start | bytes 7077896 | tf_op jit(solution)/shard_map/ppermute | solution.py:641
  78.3 1.5 copy-start.2
  109.4 10.4 %collective-permute-start.15 = (bf16[16,64,1152]{2,1,0:T(8,128)(2,1)}, bf16[16,64,1152]{2,1,0:T(8,128)(2,1)S(1)}, u32[]{:S(2)}, u32[]{:S(2)}) collective-permute-start(bf16[16,64,1152]{2,1,0:T(8,128)(2,1)} %get-tuple-element.119), channel_id=1, source_target_pairs={{0,1},{1,0},{2,3},{3,2},{4,5},{5,4},{6,7},{7,6},{8,9},{9,8},{10,11... | collective-permute-start | bytes 7077896 | tf_op jit(solution)/shard_map/ppermute | solution.py:641
  109.5 10.3 %collective-permute-start.14 = (bf16[2,2,128,512]{3,2,1,0:T(8,128)(2,1)}, bf16[2,2,128,512]{3,2,1,0:T(8,128)(2,1)S(1)}, u32[]{:S(2)}, u32[]{:S(2)}) collective-permute-start(bf16[2,2,128,512]{3,2,1,0:T(8,128)(2,1)} %get-tuple-element.120), channel_id=1, source_target_pairs={{0,31},{1,0},{2,1},{3,2},{4,3},{5,4},{6,5},{7,6},{8,7},{9,8},{10,9... | collective-permute-start | bytes 1572872 | tf_op jit(solution)/shard_map/ppermute | solution.py:644
  112.8 8.6 %copy-start.1 = (bf16[16,64,1152]{2,1,0:T(8,128)(2,1)S(1)}, bf16[16,64,1152]{2,1,0:T(8,128)(2,1)}, u32[]{:S(2)}) copy-start(bf16[16,64,1152]{2,1,0:T(8,128)(2,1)} %get-tuple-element.124) | copy-start | bytes 7077892
  119.8 0.8 copy-start.6
  119.8 1.6 copy-start.3
  123.8 16.7 %collective-permute-start.17 = (bf16[8,64,1152]{2,1,0:T(8,128)(2,1)S(1)}, bf16[8,64,1152]{2,1,0:T(8,128)(2,1)S(1)}, u32[]{:S(2)}, u32[]{:S(2)}) collective-permute-start(bf16[8,64,1152]{2,1,0:T(8,128)(2,1)S(1)} %slice.53), channel_id=1, source_target_pairs={{0,4},{1,3},{2,6},{3,1},{4,0},{5,7},{6,2},{7,5},{8,12},{9,11},{10,... | collective-permute-start | bytes 3538952 | tf_op jit(solution)/shard_map/ppermute | solution.py:641
  140.3 5.9 %collective-permute-start.16 = (bf16[1056,512]{1,0:T(8,128)(2,1)}, bf16[1056,512]{1,0:T(8,128)(2,1)}, u32[]{:S(2)}, u32[]{:S(2)}) collective-permute-start(bf16[1056,512]{1,0:T(8,128)(2,1)} %get-tuple-element.135.mine_ref), channel_id=1, source_target_pairs={{0,1},{1,0},{2,3},{3,2},{4,5},{5,4},{6,7},{7,6},{8,9},{9,8},{10,11... | collective-permute-start | bytes 3244040 | tf_op jit(solution)/shard_map/ppermute | solution.py:641
  140.8 25.5 %collective-permute-start.22 = (bf16[4,64,1152]{2,1,0:T(8,128)(2,1)S(1)}, bf16[4,64,1152]{2,1,0:T(8,128)(2,1)S(1)}, u32[]{:S(2)}, u32[]{:S(2)}) collective-permute-start(bf16[4,64,1152]{2,1,0:T(8,128)(2,1)S(1)} %slice.54), channel_id=1, source_target_pairs={{0,2},{1,5},{2,0},{3,7},{4,6},{5,1},{6,4},{7,3},{8,10},{9,13},{10,... | collective-permute-start | bytes 1769480 | tf_op jit(solution)/shard_map/ppermute | solution.py:641
  146.2 4.4 %copy-start.19 = (bf16[2,128,512]{2,1,0:T(8,128)(2,1)S(1)}, bf16[2,128,512]{2,1,0:T(8,128)(2,1)}, u32[]{:S(2)}) copy-start(bf16[2,128,512]{2,1,0:T(8,128)(2,1)} %get-tuple-element.145) | copy-start | bytes 786436
  149.1 10.3 %collective-permute-start.19 = (bf16[544,512]{1,0:T(8,128)(2,1)}, bf16[544,512]{1,0:T(8,128)(2,1)S(1)}, u32[]{:S(2)}, u32[]{:S(2)}) collective-permute-start(bf16[544,512]{1,0:T(8,128)(2,1)} %get-tuple-element.140.mine_ref), channel_id=1, source_target_pairs={{0,4},{1,3},{2,6},{3,1},{4,0},{5,7},{6,2},{7,5},{8,12},{9,11},{10,... | collective-permute-start | bytes 1671176 | tf_op jit(solution)/shard_map/ppermute | solution.py:641
  150.6 20.4 %collective-permute-start.18 = (bf16[2,128,512]{2,1,0:T(8,128)(2,1)S(1)}, bf16[2,128,512]{2,1,0:T(8,128)(2,1)S(1)}, u32[]{:S(2)}, u32[]{:S(2)}) collective-permute-start(bf16[2,128,512]{2,1,0:T(8,128)(2,1)S(1)} %copy-done.19), channel_id=1, source_target_pairs={{0,31},{1,0},{2,1},{3,2},{4,3},{5,4},{6,5},{7,6},{8,7},{9,8},{10,9... | collective-permute-start | bytes 786440 | tf_op jit(solution)/shard_map/ppermute | solution.py:644
  159.4 0.8 copy-start.5
  162.5 14.5 %collective-permute-start.20 = (bf16[288,512]{1,0:T(8,128)(2,1)}, bf16[288,512]{1,0:T(8,128)(2,1)S(1)}, u32[]{:S(2)}, u32[]{:S(2)}) collective-permute-start(bf16[288,512]{1,0:T(8,128)(2,1)} %get-tuple-element.148.mine_ref), channel_id=1, source_target_pairs={{0,2},{1,5},{2,0},{3,7},{4,6},{5,1},{6,4},{7,3},{8,10},{9,13},{10,... | collective-permute-start | bytes 884744 | tf_op jit(solution)/shard_map/ppermute | solution.py:641
  166.5 17.1 %collective-permute-start.25 = (bf16[64,1152]{1,0:T(8,128)(2,1)S(1)}, bf16[64,1152]{1,0:T(8,128)(2,1)S(1)}, u32[]{:S(2)}, u32[]{:S(2)}) collective-permute-start(bf16[64,1152]{1,0:T(8,128)(2,1)S(1)} %get-tuple-element.181), channel_id=1, source_target_pairs={{0,24},{1,25},{2,26},{3,27},{4,28},{5,29},{6,30},{7,31},{8,16},{9,... | collective-permute-start | bytes 442376 | tf_op jit(solution)/shard_map/ppermute | solution.py:669
  171.0 0.7 copy-start.9
  176.5 8.4 %collective-permute-start.24 = (bf16[64,1152]{1,0:T(8,128)(2,1)S(1)}, bf16[64,1152]{1,0:T(8,128)(2,1)S(1)}, u32[]{:S(2)}, u32[]{:S(2)}) collective-permute-start(bf16[64,1152]{1,0:T(8,128)(2,1)S(1)} %get-tuple-element.182), channel_id=1, source_target_pairs={{0,8},{1,9},{2,10},{3,11},{4,12},{5,13},{6,14},{7,15},{8,0},{9,1},... | collective-permute-start | bytes 442376 | tf_op jit(solution)/shard_map/ppermute | solution.py:669
  176.5 9.8 %collective-permute-start.23 = (bf16[64,1152]{1,0:T(8,128)(2,1)S(1)}, bf16[64,1152]{1,0:T(8,128)(2,1)S(1)}, u32[]{:S(2)}, u32[]{:S(2)}) collective-permute-start(bf16[64,1152]{1,0:T(8,128)(2,1)S(1)} %get-tuple-element.183), channel_id=1, source_target_pairs={{0,16},{1,17},{2,18},{3,19},{4,20},{5,21},{6,22},{7,23},{8,24},{9,... | collective-permute-start | bytes 442376 | tf_op jit(solution)/shard_map/ppermute | solution.py:669
  177.0 0.7 copy-start.7
  179.7 9.6 %collective-permute-start.26 = (bf16[96,512]{1,0:T(8,128)(2,1)}, bf16[96,512]{1,0:T(8,128)(2,1)S(1)}, u32[]{:S(2)}, u32[]{:S(2)}) collective-permute-start(bf16[96,512]{1,0:T(8,128)(2,1)} %get-tuple-element.160), channel_id=1, source_target_pairs={{0,8},{1,9},{2,10},{3,11},{4,12},{5,13},{6,14},{7,15},{8,0},{9,1},... | collective-permute-start | bytes 294920 | tf_op jit(solution)/shard_map/ppermute | solution.py:669
  181.1 8.1 %collective-permute-start.27 = (bf16[96,512]{1,0:T(8,128)(2,1)}, bf16[96,512]{1,0:T(8,128)(2,1)S(1)}, u32[]{:S(2)}, u32[]{:S(2)}) collective-permute-start(bf16[96,512]{1,0:T(8,128)(2,1)} %get-tuple-element.162), channel_id=1, source_target_pairs={{0,24},{1,25},{2,26},{3,27},{4,28},{5,29},{6,30},{7,31},{8,16},{9,... | collective-permute-start | bytes 294920 | tf_op jit(solution)/shard_map/ppermute | solution.py:669
  183.6 2.7 %copy-start.10 = (bf16[64,1152]{1,0:T(8,128)(2,1)}, bf16[64,1152]{1,0:T(8,128)(2,1)S(1)}, u32[]{:S(2)}) copy-start(bf16[64,1152]{1,0:T(8,128)(2,1)S(1)} %collective-permute-done.25.c_ref) | copy-start | bytes 442372
  183.6 9.6 %collective-permute-start.21 = (bf16[96,512]{1,0:T(8,128)(2,1)}, bf16[96,512]{1,0:T(8,128)(2,1)S(1)}, u32[]{:S(2)}, u32[]{:S(2)}) collective-permute-start(bf16[96,512]{1,0:T(8,128)(2,1)} %get-tuple-element.153.refs_1_), channel_id=1, source_target_pairs={{0,16},{1,17},{2,18},{3,19},{4,20},{5,21},{6,22},{7,23},{8,24},{9,... | collective-permute-start | bytes 294920 | tf_op jit(solution)/shard_map/ppermute | solution.py:669
  184.9 1.4 copy-start.11
  186.3 0.7 copy-start.12
  189.3 3.9 %copy-start.14 = (bf16[96,512]{1,0:T(8,128)(2,1)}, bf16[96,512]{1,0:T(8,128)(2,1)S(1)}, u32[]{:S(2)}) copy-start(bf16[96,512]{1,0:T(8,128)(2,1)S(1)} %collective-permute-done.27.refs_4_) | copy-start | bytes 294916
  189.3 3.9 %copy-start.13 = (bf16[96,512]{1,0:T(8,128)(2,1)}, bf16[96,512]{1,0:T(8,128)(2,1)S(1)}, u32[]{:S(2)}) copy-start(bf16[96,512]{1,0:T(8,128)(2,1)S(1)} %collective-permute-done.26.refs_3_) | copy-start | bytes 294916
  193.2 0.6 copy-start.15

commit v3 on v2

--- a/solution.py
+++ b/solution.py
@@ -23,6 +23,7 @@
 VMEM = pl.BlockSpec(memory_space=pltpu.VMEM)
 SMEM = pl.BlockSpec(memory_space=pltpu.SMEM)
 ANY = pl.BlockSpec(memory_space=pl.ANY)
+HBM = pl.BlockSpec(memory_space=pltpu.HBM)
 
 
 def dot(left, right):
@@ -75,31 +76,36 @@
 
 
 def prepare_kernel(
-    place, offsets, lengths, x_ref, cot_ref, wq_ref, wk_ref, wv_ref, out_ref, x_edge_ref, cot_edge_ref, sem
+    place, offsets, lengths, x_ref, cot_ref, wq_ref, wk_ref, wv_ref, out_ref, edge_ref, rows_ref, sem
 ):
     rows = x_ref.shape[1]
     last_rows = pl.multiple_of(place[1] * rows + (rows - SPAN), SPAN)
-    copy = pltpu.make_async_copy(cot_ref.at[:, pl.ds(last_rows, SPAN), :], cot_edge_ref, sem.at[0])
-    copy.start()
     shard = wq_ref.shape[0]
-    for i, ref in enumerate((wq_ref, wk_ref, wv_ref)):
-        out_ref[0, 0:shard, i * LANES : (i + 1) * LANES] = ref[...]
+    copies = [pltpu.make_async_copy(x_ref.at[mi], rows_ref.at[mi], sem.at[mi]) for mi in range(2)]
+    copies += [
+        pltpu.make_async_copy(ref, out_ref.at[0, 0:shard, i * LANES : (i + 1) * LANES], sem.at[2 + i])
+        for i, ref in enumerate((wq_ref, wk_ref, wv_ref))
+    ]
+    copies.append(pltpu.make_async_copy(cot_ref.at[:, pl.ds(last_rows, SPAN), :], edge_ref, sem.at[5]))
+    for copy in copies:
+        copy.start()
     sums = []
     for mi in range(2):
         dev, offset, ends = row_info(place, offsets, lengths, mi)
         first, last = summary_range(dev * (rows // SPAN) + iota((8, 1), 0), offset, ends)
         pos = dev * rows + iota((1, rows), 1)
         member = jnp.where((pos >= first) & (pos <= last), 1.0, 0.0).astype(BF16)
-        x_edge_ref[mi] = x_ref[mi, rows - SPAN :, :]
-        hat, _ = unit(x_ref[mi].astype(F32))
+        copies[mi].wait()
+        hat, _ = unit(rows_ref[mi].astype(F32))
         high = hat.astype(BF16)
         rest = (hat - high.astype(F32)).astype(BF16)
         total = dot(member, high) + dot(member, rest)
         sums.append(total * lax.rsqrt((last - first + 1).astype(F32)))
     both = jnp.concatenate(sums, axis=0).astype(BF16)
+    for copy in copies[2:]:
+        copy.wait()
     for lane in range(D // LANES):
         out_ref[0, 16 * lane : 16 * lane + 16, 384:512] = both[:, lane * LANES : (lane + 1) * LANES]
-    copy.wait()
 
 
 def fill_masks(place, offsets, lengths, mi, bias_ref, tiles, summaries, length):
@@ -254,7 +260,7 @@
     near_ref, far_ref,
     result_ref, gmid_ref, edge_ref, gatt_ref, small_ref, gub_ref, keep_ref, send_ref,
     wo_ref, wu_ref, wd_ref, resid_ref, acc_ref, gn_ref, n_ref, c_ref, nt_ref, ct_ref, gu_ref, gd_ref, go_ref,
-    guw_ref, gdw_ref, gow_ref, wide_ref, low_ref, sem, out_sem,
+    wide_ref, low_ref, sem, out_sem,
 ):
     rows = xs_ref.shape[1]
     tiles = rows // SPAN
@@ -287,7 +293,6 @@
     place(False)
     small_ref[...] = jnp.zeros_like(small_ref)
     gub_ref[...] = jnp.zeros_like(gub_ref)
-    gow_ref[...] = jnp.zeros_like(gow_ref)
     own_copy.wait()
     pltpu.make_async_copy(wo_ref, wo_ref, sem.at[0]).wait()
     for mi in range(2):
@@ -327,27 +332,27 @@
         lax.fori_loop(0, half, body, 0)
 
     def chunk(ch, carry):
-        cols = columns(ch, 512)
-        for mi in range(2):
-            here = slice(mi * rows, (mi + 1) * rows)
-            w_up, w_down = wu_ref[:, cols], wd_ref[:, cols]
-            act, slope = gelu_pair(dot(n_ref[here, :], w_up) + ubias[:, cols])
-            act = act.astype(BF16)
-            grad = (dot(c_ref[here, :], w_down) * slope).astype(BF16)
-            acc_ref[here, :] += dot_cols(act, w_down)
-            gn_ref[here, :] += dot_cols(grad, w_up)
-            grad_up, grad_down = dot(nt_ref[:, here], grad), dot(ct_ref[:, here], act)
-            if mi == 0:
-                guw_ref[...] = grad_up
-                gdw_ref[...] = grad_down
-            else:
-                gu_ref[:, cols] = (guw_ref[...] + grad_up).astype(BF16)
-                gd_ref[:, cols] = (gdw_ref[...] + grad_down).astype(BF16)
-            gub_ref[:, cols] += jnp.sum(grad.astype(F32), axis=0, keepdims=True)
-        emit(lambda b: b == ch, ((gu_ref, 512, slice(128, 640), 1), (gd_ref, 512, slice(640, 1152), 2)))
+        cols = columns(ch, 1024)
+        halves = [slice(mi * rows, (mi + 1) * rows) for mi in range(2)]
+        w_up, w_down = wu_ref[:, cols], wd_ref[:, cols]
+        ups = [dot(n_ref[here, :], w_up) + ubias[:, cols] for here in halves]
+        backs = [dot(c_ref[here, :], w_down) for here in halves]
+        acts, grads = [], []
+        for here, up, back in zip(halves, ups, backs):
+            act, slope = gelu_pair(up)
+            grad = back * slope
+            gub_ref[:, cols] += jnp.sum(grad, axis=0, keepdims=True)
+            acts.append(act.astype(BF16))
+            grads.append(grad.astype(BF16))
+            acc_ref[here, :] += dot_cols(acts[-1], w_down)
+            gn_ref[here, :] += dot_cols(grads[-1], w_up)
+        gu_ref[:, cols] = dot(nt_ref[...], jnp.concatenate(grads, axis=0)).astype(BF16)
+        gd_ref[:, cols] = dot(ct_ref[...], jnp.concatenate(acts, axis=0)).astype(BF16)
+        emit(lambda b: b // 2 == ch, ((gu_ref, 512, slice(128, 640), 1), (gd_ref, 512, slice(640, 1152), 2)))
         return carry
 
-    lax.fori_loop(0, 4, chunk, 0)
+    lax.fori_loop(0, 2, chunk, 0)
+    branches = []
     for mi in range(2):
         here = slice(mi * rows, (mi + 1) * rows)
         result_ref[mi] = acc_ref[here, :].astype(BF16)
@@ -357,13 +362,11 @@
         small_ref[1:2, :] += jnp.sum(grad, axis=0, keepdims=True)
         branch = (c_ref[here, :].astype(F32) + unit_back(grad * gain[...], hat, inverse)).astype(BF16)
         gmid_ref[mi] = branch
-        edge_ref[0, mi] = result_ref[mi, 0:SPAN, :]
-        edge_ref[1, mi] = branch[0:SPAN]
+        edge_ref[mi] = result_ref[mi, 0:SPAN, :]
         small_ref[2:3, :] += jnp.sum(branch.astype(F32), axis=0, keepdims=True)
         gatt_ref[mi] = dot(branch, wo_ref[...]).astype(BF16)
-        grad_out = dot(branch.T, att_ref[mi])
-        gow_ref[...] = grad_out if mi == 0 else gow_ref[...] + grad_out
-    go_ref[...] = gow_ref[...].astype(BF16)
+        branches.append(branch.T)
+    go_ref[...] = dot(jnp.concatenate(branches, axis=1), jnp.concatenate((att_ref[0], att_ref[1]), axis=0)).astype(BF16)
     emit(lambda b: b >= 0, ((go_ref, 128, slice(0, 128), 0),))
     pltpu.make_async_copy(gu_ref, gu_ref, out_sem.at[1]).wait()
     pltpu.make_async_copy(gd_ref, gd_ref, out_sem.at[2]).wait()
@@ -498,9 +501,12 @@
     pltpu.make_async_copy(stack_ref, stack_ref, sem.at[1]).wait()
 
 
-def rows_back_kernel(grad_ref, w_ref, gn_ref, edge_ref):
-    gn_ref[0] = dot_cols(grad_ref[0], w_ref[...]).astype(BF16)
-    edge_ref[0] = gn_ref[0, 0:SPAN, :]
+def rows_back_kernel(grad_ref, w_ref, xs_ref, gmid_ref, gain, part_ref, edge_ref):
+    grad = dot_cols(grad_ref[0], w_ref[...]) * gain[...]
+    hat, inverse = unit(xs_ref[0].astype(F32))
+    part = gmid_ref[0].astype(F32) + unit_back(grad, hat, inverse)
+    part_ref[0] = part
+    edge_ref[0] = part[0:SPAN].astype(BF16)
 
 
 def fold_kernel(keep_ref, mine_ref, got_ref, next_ref, *send_refs):
@@ -515,51 +521,43 @@
         here = slice((i + 1) * part, (i + 2) * part)
         send_ref[0:part, :] = (keep_ref[here, :].astype(F32) + got_ref[here, :].astype(F32)).astype(BF16)
         send_ref[part : part + 16, :] = high
-        send_ref[part + 16 : part + 32, :] = rest
+        if len(send_refs) == 1:
+            send_ref[part + 16 : part + 32, :] = rest
 
 
 def lines_of(ref):
-    size = ref.shape[0] - 32
-    return ref[size : size + 16, :].astype(F32) + ref[size + 16 : size + 32, :].astype(F32)
+    return ref[ref.shape[0] - 16 :, :].astype(F32)
 
 
 def two_tiles(ref, right, mi, t):
     if (t + 2) * SPAN <= ref.shape[1]:
         return ref[mi, t * SPAN : (t + 2) * SPAN, :]
-    return jnp.concatenate((ref[mi, t * SPAN :, :], right[mi]), axis=0)
-
-
-def unroll_kernel(offsets, result_ref, gmid_ref, right_ref, out_ref, part_ref, wide_ref):
+    return jnp.concatenate((ref[mi, t * SPAN :, :], right[mi].astype(ref.dtype)), axis=0)
+
+
+def unroll_kernel(offsets, result_ref, right_ref, x_ref, out_ref, hat_ref, inverse_ref, wide_ref):
     mi = pl.program_id(0)
     for t in range(result_ref.shape[1] // SPAN):
         here = slice(t * SPAN, (t + 1) * SPAN)
-        for i, (ref, target) in enumerate(((result_ref, out_ref), (gmid_ref, part_ref))):
-            wide_ref[i] = two_tiles(ref, right_ref.at[i], 0, t).astype(F32)
-            target[0, here, :] = roll_rows(wide_ref.at[i], SPAN - offsets[mi]).astype(BF16)
-
-
-def input_part_kernel(offsets, x_ref, gmid_ref, gn_ref, right_ref, gain, part_ref, wide_ref):
-    mi = pl.program_id(0)
-    for t in range(x_ref.shape[1] // SPAN):
-        here = slice(t * SPAN, (t + 1) * SPAN)
-        wide_ref[...] = two_tiles(gn_ref, right_ref, 0, t).astype(F32)
-        grad = roll_rows(wide_ref, SPAN - offsets[mi])
+        wide_ref[...] = two_tiles(result_ref, right_ref, 0, t).astype(F32)
+        out_ref[0, here, :] = roll_rows(wide_ref, SPAN - offsets[mi]).astype(BF16)
         hat, inverse = unit(x_ref[0, here, :].astype(F32))
-        part_ref[0, here, :] = gmid_ref[0, here, :].astype(F32) + unit_back(grad * gain[...], hat, inverse)
-
-
-def finish_rest_kernel(keep_ref, a_ref, b_ref, c_ref, wo_ref, wu_ref, wd_ref):
-    total = keep_ref[...] + (a_ref[...].astype(F32) + (b_ref[...].astype(F32) + c_ref[...].astype(F32)))
+        hat_ref[0, here, :] = hat.astype(BF16)
+        inverse_ref[0, here, :] = jnp.broadcast_to(inverse, (SPAN, LANES))
+
+
+def finish_rest_kernel(keep_ref, got_ref, wo_ref, wu_ref, wd_ref):
+    total = keep_ref[0] + got_ref[0].astype(F32)
     wo_ref[...] = total[:, :128]
     wu_ref[...] = total[:, 128:640]
     wd_ref[...] = total[:, 640:]
 
 
 def finish_kernel(
-    direct, place, offsets, lengths, x_ref, part_ref, gain, *refs
+    direct, place, offsets, lengths, hat_ref, inverse_ref, part_ref, right_ref, gain, *refs
 ):
     if direct:
-        keep_ref, mine_ref, a_ref, b_ref, c_ref, out_ref, wq_ref, wk_ref, wv_ref, *line_refs = refs
+        keep_ref, mine_ref, a_ref, b_ref, c_ref, out_ref, wq_ref, wk_ref, wv_ref, *line_refs, wide_ref = refs
         size = keep_ref.shape[0]
         total = (keep_ref[...] + a_ref[0:size, :].astype(F32)) + (
             b_ref[0:size, :].astype(F32) + c_ref[0:size, :].astype(F32)
@@ -573,26 +571,32 @@
         for ref, i in zip(line_refs, (0, 1, 2, 3, 8, 9, 10, 11)):
             ref[...] = lines[i : i + 1, :]
     else:
-        pooled_ref, out_ref = refs
+        pooled_ref, out_ref, wide_ref = refs
         pooled = pooled_ref[...]
-    rows = x_ref.shape[1]
+    rows = hat_ref.shape[1]
     for mi in range(2):
         dev, offset, ends = row_info(place, offsets, lengths, mi)
         first, last = summary_range(dev * (rows // SPAN) + iota((8, 1), 0), offset, ends)
         lows = jnp.concatenate(
             [pooled[16 * i + 8 * mi : 16 * i + 8 * mi + 8, :] for i in range(D // LANES)], axis=1
         )
-        lows = (lows * gain[...] * lax.rsqrt((last - first + 1).astype(F32))).astype(BF16)
+        lows = lows * gain[...] * lax.rsqrt((last - first + 1).astype(F32))
+        level = (lows - jnp.mean(lows, axis=-1, keepdims=True)).astype(BF16)
+        lows = lows.astype(BF16)
         first, last = summary_range(dev * (rows // SPAN) + iota((1, 8), 1), offset, ends)
         for t in range(rows // SPAN):
             here = slice(t * SPAN, (t + 1) * SPAN)
             pos = dev * rows + t * SPAN + iota((SPAN, 1), 0)
-            member = jnp.where((pos >= first) & (pos <= last), 1.0, 0.0).astype(BF16)
-            hat, inverse = unit(x_ref[mi, here, :].astype(F32))
-            out_ref[mi, here, :] = part_ref[mi, here, :] + unit_back(dot(member, lows), hat, inverse)
-
-
-def call(kernel, outs, in_specs, out_specs=None, scratch=(), limit=56, **more):
+            member = jnp.where((pos >= first) & (pos <= last), 1.0, 0.0)
+            hat = hat_ref[mi, here, :]
+            slope = jnp.sum(member * dot_cols(hat, lows), axis=1, keepdims=True) * (1.0 / D)
+            inverse = inverse_ref[mi, here, 0:1]
+            wide_ref[...] = two_tiles(part_ref, right_ref, mi, t)
+            own = roll_rows(wide_ref, SPAN - offset)
+            out_ref[mi, here, :] = own + (dot(member.astype(BF16), level) - hat.astype(F32) * slope) * inverse
+
+
+def call(kernel, outs, in_specs, out_specs=None, scratch=(), limit=8, **more):
     return pl.pallas_call(
         kernel,
         out_shape=outs,
@@ -685,7 +689,7 @@
     def fold_lines(keep, sent, got, sends=1):
         size = keep.shape[0]
         part = size // (1 + sends)
-        outs = [shape((part, D), F32)] + [shape((part + 32, D), BF16)] * sends
+        outs = [shape((part, D), F32)] + [shape((part + (32 if sends == 1 else 16), D), BF16)] * sends
         mine = pl.BlockSpec((32, D), lambda i: (size // 32, 0))
         both = whole_blocks((keep, got))
         return call(fold_kernel, outs, [both[0], mine, both[1]], whole_blocks(outs), grid=(1,))(keep, sent, got)
@@ -711,35 +715,36 @@
     apart = not direct
     wide, three = (2, rows, D), (2, rows, 3 * D)
     flat, pooled_dims = (2 * rows, D), (2, summaries, D)
+    room = 12 if direct else 56
     masks = [pltpu.VMEM((tiles, SPAN + summaries, SPAN), F32)]
     w_rest = jnp.concatenate((w_out.T, w_up, w_down.T), axis=1)
 
     def prepare():
         return call(
-            prepare_kernel, [shape((1, max(shard, 64), D), BF16)] + [shape((2, SPAN, D), BF16)] * 2,
-            [SMEM] * 3 + [VMEM, ANY] + [VMEM] * 3, [VMEM] * 3,
-            scratch=[pltpu.SemaphoreType.DMA((1,))],
+            prepare_kernel, [shape((1, max(shard, 64), D), BF16), shape((2, SPAN, D), BF16)],
+            [SMEM] * 3 + [HBM] * 5, [VMEM] * 2,
+            scratch=[pltpu.VMEM(wide, BF16), pltpu.SemaphoreType.DMA((6,))],
+            limit=56,
         )(*facts, block_input, cotangent, w_query, w_key, w_value)
 
-    part_a, x_edge, cot_edge = prepare()
+    x_left = turn(block_input[:, rows - SPAN :], 1)
+    part_a, cot_edge = prepare()
     if direct:
-        got_a = spread([part_a] * 3)
-        x_left = turn(tie(x_edge, part_a), 1)
+        got_a = spread([tie(part_a, x_left)] * 3)
         part_b = tie(w_rest[None], got_a[0])
-        got_b = spread([part_b] * 3)
-        part_a = tie(jnp.concatenate([part_a] + got_a, axis=0), x_left)
-        part_a = tie(join(part_a, swap(part_a, stages[2])), *got_b)
+        got_b = swap(part_b, stages[0])
+        part_a = jnp.concatenate([part_a] + got_a, axis=0)
+        part_a = tie(join(part_a, swap(part_a, stages[2])), got_b)
+        part_b = join(part_b, got_b)
+        got_b = swap(part_b, stages[1])
         got_a = swap(part_a, stages[3])
-        part_b = tie(jnp.concatenate([part_b] + got_b, axis=0), part_a)
-        got_b = swap(part_b, stages[2])
-        near_a = join(part_a, got_a)
+        near_a = join(part_a, tie(got_a, got_b))
         far_a = swap(near_a, (0, 0))
         part_b = join(part_b, tie(got_b, near_a))
-        got_b = swap(part_b, stages[3])
-        cot_left = turn(tie(cot_edge, part_b), 1)
+        got_b = swap(part_b, stages[2])
         more = ()
     else:
-        x_left, cot_left = turn(x_edge, 1), turn(cot_edge, 1)
+        cot_left = turn(cot_edge, 1)
         near_a, far_a = gather_whole(part_a[0, :shard, :384])
         near_b, far_b = gather_whole(w_rest)
         more = (lax.all_gather(part_a[0, :64, 384:], AXES, axis=0),)
@@ -756,22 +761,27 @@
             pltpu.VMEM((2, rows + 2 * summaries, D), BF16),
             pltpu.SemaphoreType.DMA((2,)),
         ],
+        limit=24 if direct else 56,
     )(
         *facts, block_of, row_of, slots, block_input, x_left, row(ln1_gain), row(ln1_bias),
         row(query_bias), row(value_bias), near_a, far_a, *more,
     )
     outs = [shape(wide, BF16), shape((2, 4, tiles, 1, 2 * SPAN), F32)]
-    seen = call_row(attend_kernel, 0, facts, (qkv, skv), outs, (), masks)
     if direct:
-        near_b = join(part_b, tie(got_b, seen[0], cot_left))
+        part_b = join(part_b, tie(got_b, skv))
+        got_b = swap(part_b, stages[3])
+        qkv = tie(qkv, part_b)
+    seen = call_row(attend_kernel, 0, facts, (qkv, skv), outs, (), masks, limit=room)
+    att, lse = call_row(attend_kernel, 1, facts, (qkv, skv), outs, tuple(seen), masks, limit=room)
+    if direct:
+        near_b = join(part_b, tie(got_b, att))
         far_b = swap(near_b, (0, 0))
-        seen = [tie(seen[0], near_b)] + list(seen[1:])
-    att, lse = call_row(attend_kernel, 1, facts, (qkv, skv), outs, tuple(seen), masks)
+        cot_left = turn(tie(cot_edge, near_b), 1)
     result, gmid, edge, gatt, small_b, grad_ub, keep_b, send_b = call(
         mlp_kernel,
-        [shape(wide, BF16)] * 2 + [shape((2, 2, SPAN, D), BF16), shape(wide, BF16)] + [shape((8, D), F32), shape((1, FF), F32)]
+        [shape(wide, BF16)] * 2 + [shape((2, SPAN, D), BF16), shape(wide, BF16)] + [shape((8, D), F32), shape((1, FF), F32)]
         + [shape((half, tall, 1152), BF16)] * 2,
-        [SMEM] * 4 + [VMEM] * 8 + [ANY] * 3,
+        [SMEM] * 4 + [VMEM] * 8 + [HBM] + [ANY] * 2,
         [VMEM] * 6 + [ANY] * 2,
         scratch=[
             pltpu.VMEM((D, D), BF16), pltpu.VMEM((D, FF), BF16), pltpu.VMEM((D, FF), BF16),
@@ -779,10 +789,10 @@
             pltpu.VMEM(flat, BF16), pltpu.VMEM(flat, BF16),
             pltpu.VMEM((D, 2 * rows), BF16), pltpu.VMEM((D, 2 * rows), BF16),
             pltpu.VMEM((D, FF), BF16), pltpu.VMEM((D, FF), BF16), pltpu.VMEM((D, D), BF16),
-            pltpu.VMEM((D, D), F32), pltpu.VMEM((D, D), F32), pltpu.VMEM((D, D), F32),
             pltpu.VMEM((rows + SPAN, D), F32), pltpu.VMEM(wide, BF16),
             pltpu.SemaphoreType.DMA((4,)), pltpu.SemaphoreType.DMA((3,)),
         ],
+        limit=40,
     )(
         facts[0], span_offset, block_of, row_of, xs, att, cot_left, row(out_bias), row(ln2_gain), row(ln2_bias),
         row(up_bias), row(down_bias), cotangent, near_b, far_b,
@@ -792,12 +802,14 @@
     if direct:
         got_b = swap(send_b, (0, 0))
         back = turn(tie(edge, send_b), -1)
-    grads = call_row(attend_back_kernel, 0, facts, arrays, outs, (), masks)
+    grads = call_row(attend_back_kernel, 0, facts, arrays, outs, (), masks, limit=room)
     if direct:
-        keep_b, send_b = fold(keep_b.astype(F32), tie(got_b, grads[0], back))
+        keep_b, send_b = fold(keep_b.astype(F32), tie(got_b, grads[0]))
         got_b = swap(send_b, stages[3])
         grads = [tie(grads[0], send_b)] + list(grads[1:])
-    grads = call_row(attend_back_kernel, 1, facts, arrays, outs, tuple(grads), masks)
+    grads = call_row(attend_back_kernel, 1, facts, arrays, outs, tuple(grads), masks, limit=room)
+    if direct:
+        grads = [tie(grads[0], back), grads[1]]
     lines, keep_a, send_a, *more = call(
         partial(weights_back_kernel, apart),
         [shape((16, D), F32)]
@@ -809,6 +821,7 @@
             pltpu.VMEM((D, 3 * D), BF16), pltpu.VMEM(pooled_dims, BF16), pltpu.VMEM((count, 64, LANES), BF16),
             pltpu.VMEM((32, D), BF16), pltpu.SemaphoreType.DMA((3,)),
         ],
+        limit=24 if direct else 56,
     )(
         *facts, block_of, row_of, slots, xs, *grads, sums, w_full, row(ln1_gain), row(ln1_bias), small_b, grad_ub,
     )
@@ -821,58 +834,54 @@
 
     def rows_back(*after):
         return call(
-            rows_back_kernel, [shape(wide, BF16), shape(edge_dims, BF16)],
-            [by_row(three), pl.BlockSpec((D, 3 * D), lambda i: (0, 0))], [by_row(wide), by_row(edge_dims)], grid=(2,),
-        )(grads[0], tie(w_full, *after))
+            rows_back_kernel, [shape(wide, F32), shape(edge_dims, BF16)],
+            [by_row(three), pl.BlockSpec((D, 3 * D), lambda i: (0, 0)), by_row(wide), by_row(wide), once],
+            [by_row(wide), by_row(edge_dims)], grid=(2,), limit=16,
+        )(grads[0], tie(w_full, *after), xs, gmid, row(ln1_gain))
 
     def unroll(back):
         return call(
-            unroll_kernel, [shape(wide, BF16)] * 2,
-            [SMEM, by_row(wide), by_row(wide), pl.BlockSpec((2, 1, SPAN, D), lambda i: (0, i, 0, 0))],
-            [by_row(wide)] * 2, [pltpu.VMEM((2, 2 * SPAN, D), F32)], grid=(2,),
-        )(span_offset, result, gmid, back)
-
-    def input_part(gmid, gn, back):
-        return call(
-            input_part_kernel, [shape(wide, F32)], [SMEM] + [by_row(wide)] * 3 + [by_row(edge_dims), once],
-            [by_row(wide)], [pltpu.VMEM((2 * SPAN, D), F32)], grid=(2,),
-        )(span_offset, block_input, gmid, gn, back, row(ln1_gain))[0]
-
-    final = [SMEM] * 3 + [VMEM] * 3
+            unroll_kernel, [shape(wide, BF16)] * 2 + [shape((2, rows, LANES), F32)],
+            [SMEM, by_row(wide), by_row(edge_dims), by_row(wide)], [by_row(wide)] * 2 + [by_row((2, rows, LANES))],
+            [pltpu.VMEM((2 * SPAN, D), F32)], grid=(2,),
+        )(span_offset, result, back, block_input)
+
+    final = [SMEM] * 3 + [VMEM] * 5
+    rolled = [pltpu.VMEM((2 * SPAN, D), F32)]
     if direct:
         got_a = swap(send_a, (0, 0))
         keep_b, send_b = fold(keep_b, tie(got_b, send_a))
         got_b = swap(send_b, stages[2])
-        gn, edge = rows_back(send_b)
-        keep_a, send_a = fold_lines(keep_a, send_a, tie(got_a, gn))
+        part, edge = rows_back(send_b)
+        keep_a, send_a = fold_lines(keep_a, send_a, tie(got_a, part))
         got_a = swap(send_a, stages[3])
-        gn_back = turn(tie(edge, send_a), -1)
-        total = keep_b + tie(got_b, send_a).astype(F32)
-        got_b = spread([total[i].astype(BF16) for i in (1, 2, 3)])
-        keep_b = total[0]
-        result_own, gmid_own = unroll(tie(back, send_a))
-        keep_a, send_a = fold_lines(keep_a, send_a, tie(got_a, gmid_own))
+        part_back = turn(tie(edge, send_a), -1)
+        keep_b, send_b = fold(keep_b, tie(got_b, send_a))
+        got_b = swap(send_b, stages[1])
+        result_own, *hats = unroll(tie(back, send_a))
+        keep_a, send_a = fold_lines(keep_a, send_a, tie(got_a, result_own))
         got_a = swap(send_a, stages[2])
-        part = input_part(gmid_own, gn, tie(gn_back, send_a))
-        keep_a, *send_a = fold_lines(keep_a, send_a, tie(got_a, part), 3)
+        keep_b, send_b = fold(keep_b, tie(got_b, send_a))
+        got_b = swap(send_b, stages[0])
+        keep_a, *send_a = fold_lines(keep_a, send_a, tie(got_a, send_b), 3)
         got_a = spread(send_a)
         grad_wo, grad_wu, grad_wd = call(
             finish_rest_kernel, [shape((shard, LANES), F32), shape((shard, 512), F32), shape((shard, 512), F32)],
-            [VMEM] * 4,
-        )(keep_b, *(tie(got, send_a[0]) for got in got_b))
+            [VMEM] * 2,
+        )(keep_b, tie(got_b, send_a[0]))
         input_grad, grad_wq, grad_wk, grad_wv, grad_ub, *small = call(
             partial(finish_kernel, True),
             [shape(wide, F32)] + [shape((shard, LANES), F32)] * 3 + [shape((1, FF), F32)] + [shape((1, D), F32)] * 8,
-            final + [VMEM] * 5,
-        )(*facts, block_input, part, row(ln1_gain), keep_a, send_a[0], *(tie(got, grad_wo) for got in got_a))
+            final + [VMEM] * 5, scratch=rolled, limit=16,
+        )(*facts, *hats, part, part_back, row(ln1_gain), keep_a, send_a[0], *(tie(got, grad_wo) for got in got_a))
         grad_wo, grad_wd = grad_wo.T, grad_wd.T
         small = [a.reshape(D) for a in small]
         grad_ub = grad_ub.reshape(FF)
     else:
         keep_a, send_a = (a.reshape(half, tall, width) for a in (keep_a, send_a))
-        result_own, gmid_own = unroll(turn(edge, -1))
-        gn, edge = rows_back()
-        part = input_part(gmid_own, gn, turn(edge, -1))
+        result_own, *hats = unroll(turn(edge, -1))
+        part, edge = rows_back()
+        part_back = turn(edge, -1)
         sum_a, sum_b = scatter_whole(keep_a, send_a), scatter_whole(keep_b, send_b)
         grad_wq, grad_wk, grad_wv = (sum_a[:, i : i + LANES] for i in (0, 128, 256))
         grad_wo, grad_wu, grad_wd = sum_b[:, :128].T, sum_b[:, 128:640], sum_b[:, 640:].T
@@ -880,8 +889,8 @@
         lines = lax.psum(lines, AXES)
         grad_ub = lines[4:8].reshape(FF)
         small = [lines[i] for i in (0, 1, 2, 3, 8, 9, 10, 11)]
-        input_grad = call(partial(finish_kernel, False), [shape(wide, F32)], final + [VMEM])(
-            *facts, block_input, part, row(ln1_gain), pooled
+        input_grad = call(partial(finish_kernel, False), [shape(wide, F32)], final + [VMEM], scratch=rolled, limit=16)(
+            *facts, *hats, part, part_back, row(ln1_gain), pooled
         )[0]
     grad_gain_two, grad_shift_two, grad_obias, grad_dbias, grad_gain_one, grad_shift_one, grad_qb, grad_vb = small
     return (

time: 200 us -> 166 us (0.83)
  Pallas kernels: 105 us -> 68.9 us
  waiting for transfers between devices: 36.4 us -> 63.1 us
  starting transfers between devices: 39.5 us -> 25 us
  local copies, waits for them, and re-layouts: 11.4 us -> 4.41 us
  other arithmetic: 5.47 us -> 2.7 us
    ppermute x12 -> x16, waiting for transfers between devices: 13.5 us -> 44.2 us  [swap(): return lax.ppermute(value, AXES, pairs)]
    ppermute x12 -> x6, waiting for transfers between devices: 22.9 us -> 5.08 us  [reach(): return lax.ppermute(value, AXES, [(i, i ^ flip) for i in range(count)])]
    ppermute x4, waiting for transfers between devices: 0.01 us -> 13.8 us  [turn(): lax.ppermute(value, AXES, [(i, (i + by) % count) for i in range(count)])]
    pallas_call x5 -> x4, Pallas kernels: 47 us -> 34.4 us  [the longest x1 24.8 us: per_device(): call(mlp_kernel, [shape(wide, BF16)] * 2 + [shape((2, SPAN, D), BF16), sh...]
    ppermute x12 -> x6, starting transfers between devices: 19.3 us -> 7.93 us  [reach(): return lax.ppermute(value, AXES, [(i, i ^ flip) for i in range(count)])]
    pallas_call x4, Pallas kernels: 25.6 us -> 16.4 us  [call_row(): call(partial(kernel, mi), outs, [SMEM] * 3 + [block(a.shape) for a in arr...]
    ppermute x4, starting transfers between devices: 8.66 us -> 1.15 us  [turn(): lax.ppermute(value, AXES, [(i, (i + by) % count) for i in range(count)])]
    pallas_call x3, Pallas kernels: 7.17 us -> 0.39 us  [fold_lines(): call(fold_kernel, outs, [both[0], mine, both[1]], whole_blocks(outs), gri...]
  transfers between devices with their start and end apart: 28 -> 26, of which waited for: 12 -> 14; matrix products, arithmetic and copies ran while one was open for 2% -> 2% of each run, Pallas kernels for 34% -> 24%
where the time goes in v3:
time: 166 us
  Pallas kernels  68.9 us (42%)
  waiting for transfers between devices  63.1 us (38%)
  starting transfers between devices  25 us (15%)
  local copies, waits for them, and re-layouts  4.41 us (3%)
  other arithmetic  2.7 us (2%)
    ppermute x16, waiting for transfers between devices, swap(): return lax.ppermute(value, AXES, pairs)  44.2 us
    pallas_call x1, Pallas kernels, per_device(): call(mlp_kernel, [shape(wide, BF16)] * 2 + [shape((2, SPAN, D), BF16), sh...  24.8 us
    pallas_call x4, Pallas kernels, call_row(): call(partial(kernel, mi), outs, [SMEM] * 3 + [block(a.shape) for a in arr...  16.4 us
    ppermute x16, starting transfers between devices, swap(): return lax.ppermute(value, AXES, pairs)  16 us
    ppermute x4, waiting for transfers between devices, turn(): lax.ppermute(value, AXES, [(i, (i + by) % count) for i in range(count)])  13.8 us
    ppermute x6, starting transfers between devices, reach(): return lax.ppermute(value, AXES, [(i, i ^ flip) for i in range(count)])  7.93 us
    pallas_call x1, Pallas kernels, per_device(): call(partial(weights_back_kernel, apart), [shape((16, D), F32)] + [shape(...  6.84 us
    pallas_call x1, Pallas kernels, per_device(): call(partial(project_kernel, apart), [shape(wide, BF16), shape(three, BF1...  6.53 us
  transfers between devices with their start and end apart: 26, of which 14 were waited for; matrix products, arithmetic and copies ran while one was open for 2% of the time, Pallas kernels for 24%

profile of v3, /device:TPU:0, one launch (start us, length us, event | category | flops | bytes accessed | tf_op | source)
XLA Modules:
  0.0 165.5 jit_solution(2769836182951584536)
XLA Ops:
  0.7 1.0 slice.31
  1.6 0.5 collective-permute-start
  2.1 0.6 pad_add_fusion.1.place.place_ref
  2.7 3.8 %shard_map.314 = (bf16[1,64,512]{2,1,0:T(8,128)(2,1)}, bf16[2,128,512]{2,1,0:T(8,128)(2,1)}) custom-call(s32[2]{0:T(128)} %pad_add_fusion.1.place.place_ref, s32[2]{0:T(128)} %offsets.19, s32[2,8]{1,0:T(2,128)} %lengths.15, bf16[2,512,512]{2,1,0:T(8,128)(2,1)} %x_ref.5, bf16[2,2048,512]{2,1,0:T(8,128)(2,1)} %cot_ref.3, bf16[64,128]{1,0:T(8,128)(2,1)} %wq_ref.1, ...), custom_call_target="tpu_custom_call" | custom-call | flops 1 | bytes 1 | tf_op jit(solution)/shard_map/pallas_call | solution.py:723
  6.5 0.8 constant_dynamic-update-slice_fusion.4
  7.4 4.7 %collective-permute-done.left_ref = bf16[2,128,512]{2,1,0:T(8,128)(2,1)S(1)} collective-permute-done((bf16[2,128,512]{2,1,0:T(8,128)(2,1)S(1)}, bf16[2,128,512]{2,1,0:T(8,128)(2,1)S(1)}, u32[]{:S(2)}, u32[]{:S(2)}) %collective-permute-start) | collective-permute-done | bytes 262176 | tf_op jit(solution)/shard_map/ppermute | solution.py:648
  12.1 2.2 %collective-permute-start.3 = (bf16[1,64,512]{2,1,0:T(8,128)(2,1)}, bf16[1,64,512]{2,1,0:T(8,128)(2,1)S(1)}, u32[]{:S(2)}, u32[]{:S(2)}) collective-permute-start(bf16[1,64,512]{2,1,0:T(8,128)(2,1)} %get-tuple-element.98), channel_id=1, source_target_pairs={{0,24},{1,25},{2,26},{3,27},{4,28},{5,29},{6,30},{7,31},{8,16},{9,... | collective-permute-start | bytes 196616 | tf_op jit(solution)/shard_map/ppermute | solution.py:673
  14.3 2.2 %collective-permute-start.1 = (bf16[1,64,512]{2,1,0:T(8,128)(2,1)}, bf16[1,64,512]{2,1,0:T(8,128)(2,1)S(1)}, u32[]{:S(2)}, u32[]{:S(2)}) collective-permute-start(bf16[1,64,512]{2,1,0:T(8,128)(2,1)} %get-tuple-element.98), channel_id=1, source_target_pairs={{0,16},{1,17},{2,18},{3,19},{4,20},{5,21},{6,22},{7,23},{8,24},{9,... | collective-permute-start | bytes 196616 | tf_op jit(solution)/shard_map/ppermute | solution.py:673
  16.5 3.5 %collective-permute-done.1 = bf16[1,64,512]{2,1,0:T(8,128)(2,1)S(1)} collective-permute-done((bf16[1,64,512]{2,1,0:T(8,128)(2,1)}, bf16[1,64,512]{2,1,0:T(8,128)(2,1)S(1)}, u32[]{:S(2)}, u32[]{:S(2)}) %collective-permute-start.1) | collective-permute-done | bytes 65568 | tf_op jit(solution)/shard_map/ppermute | solution.py:673
  20.0 2.0 %collective-permute-start.5 = (bf16[1,64,1152]{2,1,0:T(8,128)(2,1)S(1)}, bf16[1,64,1152]{2,1,0:T(8,128)(2,1)S(1)}, u32[]{:S(2)}, u32[]{:S(2)}) collective-permute-start(bf16[1,64,1152]{2,1,0:T(8,128)(2,1)S(1)} %maximum_bitcast_fusion), channel_id=1, source_target_pairs={{0,16},{1,17},{2,18},{3,19},{4,20},{5,21},{6,22},{7,23},{8,24},{9,... | collective-permute-start | bytes 442376 | tf_op jit(solution)/shard_map/ppermute | solution.py:645
  22.0 0.9 pad_maximum_fusion.2
  22.9 0.8 collective-permute-start.4
  23.7 5.6 %collective-permute-done.4 = bf16[4,64,512]{2,1,0:T(8,128)(2,1)S(1)} collective-permute-done((bf16[4,64,512]{2,1,0:T(8,128)(2,1)S(1)}, bf16[4,64,512]{2,1,0:T(8,128)(2,1)S(1)}, u32[]{:S(2)}, u32[]{:S(2)}) %collective-permute-start.4) | collective-permute-done | bytes 262176 | tf_op jit(solution)/shard_map/ppermute | solution.py:645
  29.3 1.2 collective-permute-start.6
  30.6 0.8 collective-permute-start.7
  31.4 0.1 add_select_fusion.1
  31.4 0.1 select_n.110
  31.5 0.1 select_n.112
  31.8 7.9 %collective-permute-done.7 = bf16[2,64,1152]{2,1,0:T(8,128)(2,1)S(1)} collective-permute-done((bf16[2,64,1152]{2,1,0:T(8,128)(2,1)S(1)}, bf16[2,64,1152]{2,1,0:T(8,128)(2,1)S(1)}, u32[]{:S(2)}, u32[]{:S(2)}) %collective-permute-start.7) | collective-permute-done | bytes 294944 | tf_op jit(solution)/shard_map/ppermute | solution.py:645
  39.7 0.1 collective-permute-start.8
  39.8 0.1 pad_maximum_fusion
  39.9 0.5 collective-permute-start.9
  40.5 1.9 %collective-permute-done.8.far_ref = bf16[16,64,512]{2,1,0:T(8,128)(2,1)S(1)} collective-permute-done((bf16[16,64,512]{2,1,0:T(8,128)(2,1)S(1)}, bf16[16,64,512]{2,1,0:T(8,128)(2,1)S(1)}, u32[]{:S(2)}, u32[]{:S(2)}) %collective-permute-start.8) | collective-permute-done | bytes 1048608 | tf_op jit(solution)/shard_map/ppermute | solution.py:645
  42.5 6.5 %shard_map.315 = (bf16[2,512,512]{2,1,0:T(8,128)(2,1)S(1)}, bf16[2,512,1536]{2,1,0:T(8,128)(2,1)S(1)}, bf16[2,128,1536]{2,1,0:T(8,128)(2,1)S(1)}, f32[2,128,512]{2,1,0:T(8,128)S(1)}, bf16[512,1536]{1,0:T(8,128)(2,1)S(1)}) custom-call(s32[2]{0:T(128)S(1)} %copy-done.3, s32[2]{0:T(128)S(1)} %copy-done.2, s32[2,8]{1,0:T(2,128)S(1)} %copy-done.1, ...), custom_call_target="tpu_custom_call" | custom-call | flops 1 | bytes 1 | tf_op jit(solution)/shard_map/pallas_call | solution.py:753
  49.0 0.8 collective-permute-done.9
  49.8 0.2 constant_dynamic-update-slice_fusion.12
  50.0 0.2 collective-permute-start.10
  50.2 3.9 %shard_map.316 = (bf16[2,512,512]{2,1,0:T(8,128)(2,1)S(1)}, f32[2,4,4,1,256]{4,3,2,1,0:T(1,128)S(1)}) custom-call(s32[2]{0:T(128)S(1)} %copy-done.3, s32[2]{0:T(128)S(1)} %copy-done.2, s32[2,8]{1,0:T(2,128)S(1)} %copy-done.1, bf16[2,512,1536]{2,1,0:T(8,128)(2,1)S(1)} %get-tuple-element.107.qkv_ref, bf16[2,128,1536]{2,1,0:T(8,128)(2,1)S(1)} %get-tuple-element.105.skv_ref), custom_call_target="tpu_custom_call" | custom-call | flops 1 | bytes 1 | tf_op jit(solution)/shard_map/pallas_call | solution.py:617
  54.1 3.9 %shard_map.317 = (bf16[2,512,512]{2,1,0:T(8,128)(2,1)S(1)}, f32[2,4,4,1,256]{4,3,2,1,0:T(1,128)S(1)}) custom-call(s32[2]{0:T(128)S(1)} %copy-done.3, s32[2]{0:T(128)S(1)} %copy-done.2, s32[2,8]{1,0:T(2,128)S(1)} %copy-done.1, bf16[2,512,1536]{2,1,0:T(8,128)(2,1)S(1)} %get-tuple-element.107.qkv_ref, ...), custom_call_target="tpu_custom_call", output_to_operand_aliasing={{0}: (5, {}), {1}: (6, {})} | custom-call | flops 1 | bytes 1 | tf_op jit(solution)/shard_map/pallas_call | solution.py:617
  58.0 8.3 %collective-permute-done.10 = bf16[8,64,1152]{2,1,0:T(8,128)(2,1)S(1)} collective-permute-done((bf16[8,64,1152]{2,1,0:T(8,128)(2,1)S(1)}, bf16[8,64,1152]{2,1,0:T(8,128)(2,1)S(1)}, u32[]{:S(2)}, u32[]{:S(2)}) %collective-permute-start.10) | collective-permute-done | bytes 1179680 | tf_op jit(solution)/shard_map/ppermute | solution.py:645
  66.3 0.2 constant_dynamic-update-slice_fusion.11.near_ref
  66.6 0.5 collective-permute-start.11
  67.1 9.1 %collective-permute-done.11.left_ref = bf16[2,128,512]{2,1,0:T(8,128)(2,1)S(1)} collective-permute-done((bf16[2,128,512]{2,1,0:T(8,128)(2,1)S(1)}, bf16[2,128,512]{2,1,0:T(8,128)(2,1)S(1)}, u32[]{:S(2)}, u32[]{:S(2)}) %collective-permute-start.11) | collective-permute-done | bytes 262176 | tf_op jit(solution)/shard_map/ppermute | solution.py:648
  76.2 1.4 copy-done.13
  77.6 24.8 %shard_map.318 = (bf16[2,512,512]{2,1,0:T(8,128)(2,1)S(1)}, bf16[2,512,512]{2,1,0:T(8,128)(2,1)S(1)}, bf16[2,128,512]{2,1,0:T(8,128)(2,1)S(1)}, bf16[2,512,512]{...) custom-call(s32[2]{0:T(128)S(1)} %copy-done.3, ...), custom_call_target="tpu_custom_call" | custom-call | flops 1 | bytes 1 | tf_op jit(solution)/shard_map/pallas_call | solution.py:780
  102.4 0.1 collective-permute-start.14
  102.5 4.4 %shard_map.319 = (bf16[2,512,1536]{2,1,0:T(8,128)(2,1)S(1)}, bf16[2,128,1536]{2,1,0:T(8,128)(2,1)S(1)}) custom-call(s32[2]{0:T(128)S(1)} %copy-done.3, s32[2]{0:T(128)S(1)} %copy-done.2, s32[2,8]{1,0:T(2,128)S(1)} %copy-done.1, bf16[2,512,1536]{2,1,0:T(8,128)(2,1)S(1)} %get-tuple-element.107.qkv_ref, bf16[2,128,1536]{2,1,0:T(8,128)(2,1)S(1)} %get-tuple-element.105.skv_ref, ...), custom_call_target="tpu_custom_call" | custom-call | flops 1 | bytes 1 | tf_op jit(solution)/shard_map/pallas_call | solution.py:617
  106.9 0.1 collective-permute-done.14
  107.0 0.6 convert_add_fusion
  107.6 0.2 slice.55
  107.8 0.1 collective-permute-start.16
  107.8 0.1 collective-permute-start.13
  107.9 4.2 %shard_map.320 = (bf16[2,512,1536]{2,1,0:T(8,128)(2,1)S(1)}, bf16[2,128,1536]{2,1,0:T(8,128)(2,1)S(1)}) custom-call(s32[2]{0:T(128)S(1)} %copy-done.3, s32[2]{0:T(128)S(1)} %copy-done.2, s32[2,8]{1,0:T(2,128)S(1)} %copy-done.1, bf16[2,512,1536]{2,1,0:T(8,128)(2,1)S(1)} %get-tuple-element.107.qkv_ref, ...), custom_call_target="tpu_custom_call", output_to_operand_aliasing={{0}: (7, {}), {1}: (8, {})} | custom-call | flops 1 | bytes 1 | tf_op jit(solution)/shard_map/pallas_call | solution.py:617
  112.1 6.8 %shard_map.321 = (f32[16,512]{1,0:T(8,128)}, bf16[1024,512]{1,0:T(8,128)(2,1)S(1)}, bf16[1056,512]{1,0:T(8,128)(2,1)S(1)}) custom-call(s32[2]{0:T(128)S(1)} %copy-done.3, s32[2]{0:T(128)S(1)} %copy-done.2, s32[2,8]{1,0:T(2,128)S(1)} %copy-done.1, s32[32]{0:T(128)S(1)} %get-tuple-element.188.block_of, s32[32]{0:T(128)S(1)} %get-tuple-element.187.row_of, ...), custom_call_target="tpu_custom_call" | custom-call | flops 1 | bytes 1 | tf_op jit(solution)/shard_map/pallas_call | solution.py:813
  119.0 5.1 %collective-permute-start.15 = (bf16[1056,512]{1,0:T(8,128)(2,1)S(1)}, bf16[1056,512]{1,0:T(8,128)(2,1)S(1)}, u32[]{:S(2)}, u32[]{:S(2)}) collective-permute-start(bf16[1056,512]{1,0:T(8,128)(2,1)S(1)} %get-tuple-element.133.mine_ref), channel_id=1, source_target_pairs={{0,1},{1,0},{2,3},{3,2},{4,5},{5,4},{6,7},{7,6},{8,9},{9,8},{10,11... | collective-permute-start | bytes 3244040 | tf_op jit(solution)/shard_map/ppermute | solution.py:645
  124.0 0.3 slice_add_fusion
  124.4 2.5 %collective-permute-start.20 = (bf16[4,64,1152]{2,1,0:T(8,128)(2,1)S(1)}, bf16[4,64,1152]{2,1,0:T(8,128)(2,1)S(1)}, u32[]{:S(2)}, u32[]{:S(2)}) collective-permute-start(bf16[4,64,1152]{2,1,0:T(8,128)(2,1)S(1)} %slice.56), channel_id=1, source_target_pairs={{0,2},{1,5},{2,0},{3,7},{4,6},{5,1},{6,4},{7,3},{8,10},{9,13},{10,... | collective-permute-start | bytes 1769480 | tf_op jit(solution)/shard_map/ppermute | solution.py:645
  126.9 2.6 %shard_map.322 = (f32[2,512,512]{2,1,0:T(8,128)S(1)}, bf16[2,128,512]{2,1,0:T(8,128)(2,1)S(1)}) custom-call(bf16[2,512,1536]{2,1,0:T(8,128)(2,1)S(1)} %get-tuple-element.126.grad_ref, bf16[512,1536]{1,0:T(8,128)(2,1)S(1)} %get-tuple-element.135.w_ref, bf16[2,512,512]{2,1,0:T(8,128)(2,1)S(1)} %get-tuple-element.102.xs_ref, ...), custom_call_target="tpu_custom_call" | custom-call | flops 1 | bytes 1 | tf_op jit(solution)/shard_map/pallas_call | solution.py:836
  129.5 0.2 shard_map.323
  129.8 0.1 collective-permute-start.18
  129.9 8.6 %collective-permute-done.20 = bf16[4,64,1152]{2,1,0:T(8,128)(2,1)S(1)} collective-permute-done((bf16[4,64,1152]{2,1,0:T(8,128)(2,1)S(1)}, bf16[4,64,1152]{2,1,0:T(8,128)(2,1)S(1)}, u32[]{:S(2)}, u32[]{:S(2)}) %collective-permute-start.20) | collective-permute-done | bytes 589856 | tf_op jit(solution)/shard_map/ppermute | solution.py:645
  138.5 0.1 slice_add_fusion.1
  138.8 3.2 %shard_map.324 = (bf16[2,512,512]{2,1,0:T(8,128)(2,1)}, bf16[2,512,512]{2,1,0:T(8,128)(2,1)S(1)}, f32[2,512,128]{2,1,0:T(8,128)S(1)}) custom-call(s32[2]{0:T(128)S(1)} %copy-done.2, bf16[2,512,512]{2,1,0:T(8,128)(2,1)S(1)} %get-tuple-element.114.result_ref, bf16[2,128,512]{2,1,0:T(8,128)(2,1)S(1)} %collective-permute-done.13.right_ref, ...), custom_call_target="tpu_custom_call" | custom-call | flops 1 | bytes 1 | tf_op jit(solution)/shard_map/pallas_call | solution.py:843
  142.0 0.1 shard_map.325
  142.1 2.5 %collective-permute-start.19 = (bf16[288,512]{1,0:T(8,128)(2,1)S(1)}, bf16[288,512]{1,0:T(8,128)(2,1)S(1)}, u32[]{:S(2)}, u32[]{:S(2)}) collective-permute-start(bf16[288,512]{1,0:T(8,128)(2,1)S(1)} %get-tuple-element.149.mine_ref), channel_id=1, source_target_pairs={{0,2},{1,5},{2,0},{3,7},{4,6},{5,1},{6,4},{7,3},{8,10},{9,13},{10,... | collective-permute-start | bytes 884744 | tf_op jit(solution)/shard_map/ppermute | solution.py:645
  144.7 2.0 %collective-permute-done.21 = bf16[2,64,1152]{2,1,0:T(8,128)(2,1)S(1)} collective-permute-done((bf16[2,64,1152]{2,1,0:T(8,128)(2,1)S(1)}, bf16[2,64,1152]{2,1,0:T(8,128)(2,1)S(1)}, u32[]{:S(2)}, u32[]{:S(2)}) %collective-permute-start.21) | collective-permute-done | bytes 294944 | tf_op jit(solution)/shard_map/ppermute | solution.py:645
  146.8 4.8 %collective-permute-done.19.got_ref = bf16[288,512]{1,0:T(8,128)(2,1)S(1)} collective-permute-done((bf16[288,512]{1,0:T(8,128)(2,1)S(1)}, bf16[288,512]{1,0:T(8,128)(2,1)S(1)}, u32[]{:S(2)}, u32[]{:S(2)}) %collective-permute-start.19) | collective-permute-done | bytes 294944 | tf_op jit(solution)/shard_map/ppermute | solution.py:645
  151.6 0.1 collective-permute-start.24
  151.7 0.1 collective-permute-start.25
  151.8 3.3 %collective-permute-start.22 = (bf16[80,512]{1,0:T(8,128)(2,1)S(1)}, bf16[80,512]{1,0:T(8,128)(2,1)S(1)}, u32[]{:S(2)}, u32[]{:S(2)}) collective-permute-start(bf16[80,512]{1,0:T(8,128)(2,1)S(1)} %get-tuple-element.154.refs_1_), channel_id=1, source_target_pairs={{0,16},{1,17},{2,18},{3,19},{4,20},{5,21},{6,22},{7,23},{8,24},{9,... | collective-permute-start | bytes 245768 | tf_op jit(solution)/shard_map/ppermute | solution.py:673
  155.2 4.2 %collective-permute-done.23.got_ref = bf16[1,64,1152]{2,1,0:T(8,128)(2,1)S(1)} collective-permute-done((bf16[1,64,1152]{2,1,0:T(8,128)(2,1)S(1)}, bf16[1,64,1152]{2,1,0:T(8,128)(2,1)S(1)}, u32[]{:S(2)}, u32[]{:S(2)}) %collective-permute-start.23) | collective-permute-done | bytes 147488 | tf_op jit(solution)/shard_map/ppermute | solution.py:645
  159.4 0.7 shard_map.327
  160.1 1.6 collective-permute-done.22.refs_2_
  161.7 3.6 %shard_map.328 = (f32[2,512,512]{2,1,0:T(8,128)}, f32[64,128]{1,0:T(8,128)}, f32[64,128]{1,0:T(8,128)}, f32[64,128]{1,0:T(8,128)}, f32[1,2048]{1,0:T(1,128)}, /*...) custom-call(s32[2]{0:T(128)S(1)} %copy-done.3, ...), custom_call_target="tpu_custom_call" | custom-call | flops 1 | bytes 1 | tf_op jit(solution)/shard_map/pallas_call | solution.py:872
  (74 shorter events, 1.0 us)
Async XLA Ops:
  1.6 10.5 %collective-permute-start = (bf16[2,128,512]{2,1,0:T(8,128)(2,1)S(1)}, bf16[2,128,512]{2,1,0:T(8,128)(2,1)S(1)}, u32[]{:S(2)}, u32[]{:S(2)}) collective-permute-start(bf16[2,128,512]{2,1,0:T(8,128)(2,1)S(1)} %slice.31), channel_id=1, source_target_pairs={{0,1},{1,2},{2,3},{3,4},{4,5},{5,6},{6,7},{7,8},{8,9},{9,10},{10,1... | collective-permute-start | bytes 786440 | tf_op jit(solution)/shard_map/ppermute | solution.py:648
  2.7 4.6 %copy-start.14 = (bf16[512,64]{0,1:T(8,128)(2,1)S(1)}, bf16[512,64]{0,1:T(8,128)(2,1)}, u32[]{:S(2)}) copy-start(bf16[512,64]{0,1:T(8,128)(2,1)} %param.36) | copy-start | bytes 196612
  2.7 4.6 %copy-start.15 = (bf16[64,512]{1,0:T(8,128)(2,1)S(1)}, bf16[64,512]{1,0:T(8,128)(2,1)}, u32[]{:S(2)}) copy-start(bf16[64,512]{1,0:T(8,128)(2,1)} %param.34) | copy-start | bytes 196612
  2.7 4.6 %copy-start.16 = (bf16[128,64]{0,1:T(8,128)(2,1)S(1)}, bf16[128,64]{0,1:T(8,128)(2,1)}, u32[]{:S(2)}) copy-start(bf16[128,64]{0,1:T(8,128)(2,1)} %param.30) | copy-start | bytes 49156
  12.1 9.9 %collective-permute-start.3 = (bf16[1,64,512]{2,1,0:T(8,128)(2,1)}, bf16[1,64,512]{2,1,0:T(8,128)(2,1)S(1)}, u32[]{:S(2)}, u32[]{:S(2)}) collective-permute-start(bf16[1,64,512]{2,1,0:T(8,128)(2,1)} %get-tuple-element.98), channel_id=1, source_target_pairs={{0,24},{1,25},{2,26},{3,27},{4,28},{5,29},{6,30},{7,31},{8,16},{9,... | collective-permute-start | bytes 196616 | tf_op jit(solution)/shard_map/ppermute | solution.py:673
  14.3 7.7 %collective-permute-start.2 = (bf16[1,64,512]{2,1,0:T(8,128)(2,1)}, bf16[1,64,512]{2,1,0:T(8,128)(2,1)S(1)}, u32[]{:S(2)}, u32[]{:S(2)}) collective-permute-start(bf16[1,64,512]{2,1,0:T(8,128)(2,1)} %get-tuple-element.98), channel_id=1, source_target_pairs={{0,8},{1,9},{2,10},{3,11},{4,12},{5,13},{6,14},{7,15},{8,0},{9,1},... | collective-permute-start | bytes 196616 | tf_op jit(solution)/shard_map/ppermute | solution.py:673
  14.3 5.7 %collective-permute-start.1 = (bf16[1,64,512]{2,1,0:T(8,128)(2,1)}, bf16[1,64,512]{2,1,0:T(8,128)(2,1)S(1)}, u32[]{:S(2)}, u32[]{:S(2)}) collective-permute-start(bf16[1,64,512]{2,1,0:T(8,128)(2,1)} %get-tuple-element.98), channel_id=1, source_target_pairs={{0,16},{1,17},{2,18},{3,19},{4,20},{5,21},{6,22},{7,23},{8,24},{9,... | collective-permute-start | bytes 196616 | tf_op jit(solution)/shard_map/ppermute | solution.py:673
  20.0 9.3 %collective-permute-start.5 = (bf16[1,64,1152]{2,1,0:T(8,128)(2,1)S(1)}, bf16[1,64,1152]{2,1,0:T(8,128)(2,1)S(1)}, u32[]{:S(2)}, u32[]{:S(2)}) collective-permute-start(bf16[1,64,1152]{2,1,0:T(8,128)(2,1)S(1)} %maximum_bitcast_fusion), channel_id=1, source_target_pairs={{0,16},{1,17},{2,18},{3,19},{4,20},{5,21},{6,22},{7,23},{8,24},{9,... | collective-permute-start | bytes 442376 | tf_op jit(solution)/shard_map/ppermute | solution.py:645
  22.9 6.4 %collective-permute-start.4 = (bf16[4,64,512]{2,1,0:T(8,128)(2,1)S(1)}, bf16[4,64,512]{2,1,0:T(8,128)(2,1)S(1)}, u32[]{:S(2)}, u32[]{:S(2)}) collective-permute-start(bf16[4,64,512]{2,1,0:T(8,128)(2,1)S(1)} %pad_maximum_fusion.2), channel_id=1, source_target_pairs={{0,2},{1,5},{2,0},{3,7},{4,6},{5,1},{6,4},{7,3},{8,10},{9,13},{10,... | collective-permute-start | bytes 786440 | tf_op jit(solution)/shard_map/ppermute | solution.py:645
  29.3 10.3 %collective-permute-start.6 = (bf16[8,64,512]{2,1,0:T(8,128)(2,1)S(1)}, bf16[8,64,512]{2,1,0:T(8,128)(2,1)S(1)}, u32[]{:S(2)}, u32[]{:S(2)}) collective-permute-start(bf16[8,64,512]{2,1,0:T(8,128)(2,1)S(1)} %constant_dynamic-update-slice_fusion), channel_id=1, source_target_pairs={{0,4},{1,3},{2,6},{3,1},{4,0},{5,7},{6,2},{7,5},{8,12},{9,11},{10,... | collective-permute-start | bytes 1572872 | tf_op jit(solution)/shard_map/ppermute | solution.py:645
  30.6 9.1 %collective-permute-start.7 = (bf16[2,64,1152]{2,1,0:T(8,128)(2,1)S(1)}, bf16[2,64,1152]{2,1,0:T(8,128)(2,1)S(1)}, u32[]{:S(2)}, u32[]{:S(2)}) collective-permute-start(bf16[2,64,1152]{2,1,0:T(8,128)(2,1)S(1)} %pad_maximum_fusion.1), channel_id=1, source_target_pairs={{0,8},{1,9},{2,10},{3,11},{4,12},{5,13},{6,14},{7,15},{8,0},{9,1},... | collective-permute-start | bytes 884744 | tf_op jit(solution)/shard_map/ppermute | solution.py:645
  31.6 10.8 %copy-start = (bf16[2,512,512]{2,1,0:T(8,128)(2,1)S(1)}, bf16[2,512,512]{2,1,0:T(8,128)(2,1)}, u32[]{:S(2)}) copy-start(bf16[2,512,512]{2,1,0:T(8,128)(2,1)} %x_ref.5) | copy-start | bytes 3145732
  31.6 10.8 %copy-start.1 = (s32[2,8]{1,0:T(2,128)S(1)}, s32[2,8]{1,0:T(2,128)}, u32[]{:S(2)}) copy-start(s32[2,8]{1,0:T(2,128)} %lengths.15) | copy-start | bytes 196
  31.6 10.8 %copy-start.2 = (s32[2]{0:T(128)S(1)}, s32[2]{0:T(128)}, u32[]{:S(2)}) copy-start(s32[2]{0:T(128)} %offsets.19) | copy-start | bytes 28
  31.7 10.8 %copy-start.3 = (s32[2]{0:T(128)S(1)}, s32[2]{0:T(128)}, u32[]{:S(2)}) copy-start(s32[2]{0:T(128)} %pad_add_fusion.1.place.place_ref) | copy-start | bytes 28
  31.7 10.8 %copy-start.4 = (f32[512]{0:T(512)S(1)}, f32[512]{0:T(512)}, u32[]{:S(2)}) copy-start(f32[512]{0:T(512)} %param.23) | copy-start | bytes 6148
  31.7 10.8 %copy-start.6 = (f32[512]{0:T(512)S(1)}, f32[512]{0:T(512)}, u32[]{:S(2)}) copy-start(f32[512]{0:T(512)} %param.24) | copy-start | bytes 6148
  31.7 10.8 %copy-start.11 = (f32[512]{0:T(512)S(1)}, f32[512]{0:T(512)}, u32[]{:S(2)}) copy-start(f32[512]{0:T(512)} %param.28) | copy-start | bytes 6148
  31.7 10.8 %copy-start.12 = (f32[512]{0:T(512)S(1)}, f32[512]{0:T(512)}, u32[]{:S(2)}) copy-start(f32[512]{0:T(512)} %param.29) | copy-start | bytes 6148
  39.7 2.7 %collective-permute-start.8 = (bf16[16,64,512]{2,1,0:T(8,128)(2,1)S(1)}, bf16[16,64,512]{2,1,0:T(8,128)(2,1)S(1)}, u32[]{:S(2)}, u32[]{:S(2)}) collective-permute-start(bf16[16,64,512]{2,1,0:T(8,128)(2,1)S(1)} %constant_dynamic-update-slice_fusion.5.near_ref), channel_id=1, source_target_pairs={{0,1},{1,0},{2,3},{3,2},{4,5},{5,4},{6,7},{7,6},{8,9},{9,8},{10,11... | collective-permute-start | bytes 3145736 | tf_op jit(solution)/shard_map/ppermute | solution.py:645
  39.9 9.9 %collective-permute-start.9 = (bf16[4,64,1152]{2,1,0:T(8,128)(2,1)S(1)}, bf16[4,64,1152]{2,1,0:T(8,128)(2,1)S(1)}, u32[]{:S(2)}, u32[]{:S(2)}) collective-permute-start(bf16[4,64,1152]{2,1,0:T(8,128)(2,1)S(1)} %pad_maximum_fusion), channel_id=1, source_target_pairs={{0,2},{1,5},{2,0},{3,7},{4,6},{5,1},{6,4},{7,3},{8,10},{9,13},{10,... | collective-permute-start | bytes 1769480 | tf_op jit(solution)/shard_map/ppermute | solution.py:645
  50.0 16.3 %collective-permute-start.10 = (bf16[8,64,1152]{2,1,0:T(8,128)(2,1)S(1)}, bf16[8,64,1152]{2,1,0:T(8,128)(2,1)S(1)}, u32[]{:S(2)}, u32[]{:S(2)}) collective-permute-start(bf16[8,64,1152]{2,1,0:T(8,128)(2,1)S(1)} %get-tuple-element.178), channel_id=1, source_target_pairs={{0,4},{1,3},{2,6},{3,1},{4,0},{5,7},{6,2},{7,5},{8,12},{9,11},{10,... | collective-permute-start | bytes 3538952 | tf_op jit(solution)/shard_map/ppermute | solution.py:645
  57.9 8.6 %copy-start.17 = (bf16[2,128,512]{2,1,0:T(8,128)(2,1)S(1)}, bf16[2,128,512]{2,1,0:T(8,128)(2,1)}, u32[]{:S(2)}) copy-start(bf16[2,128,512]{2,1,0:T(8,128)(2,1)} %get-tuple-element.113) | copy-start | bytes 786436
  58.0 19.7 %copy-start.5 = (f32[2048]{0:T(1024)S(1)}, f32[2048]{0:T(1024)}, u32[]{:S(2)}) copy-start(f32[2048]{0:T(1024)} %param.35) | copy-start | bytes 24580
  58.0 19.7 %copy-start.7 = (f32[512]{0:T(512)S(1)}, f32[512]{0:T(512)}, u32[]{:S(2)}) copy-start(f32[512]{0:T(512)} %param.31) | copy-start | bytes 6148
  58.0 19.6 %copy-start.8 = (f32[512]{0:T(512)S(1)}, f32[512]{0:T(512)}, u32[]{:S(2)}) copy-start(f32[512]{0:T(512)} %param.32) | copy-start | bytes 6148
  58.0 19.6 %copy-start.9 = (f32[512]{0:T(512)S(1)}, f32[512]{0:T(512)}, u32[]{:S(2)}) copy-start(f32[512]{0:T(512)} %param.33) | copy-start | bytes 6148
  58.0 19.6 %copy-start.10 = (f32[512]{0:T(512)S(1)}, f32[512]{0:T(512)}, u32[]{:S(2)}) copy-start(f32[512]{0:T(512)} %param.37) | copy-start | bytes 6148
  66.5 9.7 %collective-permute-start.12 = (bf16[16,64,1152]{2,1,0:T(8,128)(2,1)S(1)}, bf16[16,64,1152]{2,1,0:T(8,128)(2,1)S(1)}, u32[]{:S(2)}, u32[]{:S(2)}) collective-permute-start(bf16[16,64,1152]{2,1,0:T(8,128)(2,1)S(1)} %constant_dynamic-update-slice_fusion.11.near_ref), channel_id=1, source_target_pairs={{0,1},{1,0},{2,3},{3,2},{4,5},{5,4},{6,7},{7,6},{8,9},{9,8},{10,11... | collective-permute-start | bytes 7077896 | tf_op jit(solution)/shard_map/ppermute | solution.py:645
  66.6 9.6 %collective-permute-start.11 = (bf16[2,128,512]{2,1,0:T(8,128)(2,1)S(1)}, bf16[2,128,512]{2,1,0:T(8,128)(2,1)S(1)}, u32[]{:S(2)}, u32[]{:S(2)}) collective-permute-start(bf16[2,128,512]{2,1,0:T(8,128)(2,1)S(1)} %copy-done.17), channel_id=1, source_target_pairs={{0,1},{1,2},{2,3},{3,4},{4,5},{5,6},{6,7},{7,8},{8,9},{9,10},{10,1... | collective-permute-start | bytes 786440 | tf_op jit(solution)/shard_map/ppermute | solution.py:648
  76.2 1.4 copy-start.13
  102.4 4.6 %collective-permute-start.14 = (bf16[16,64,1152]{2,1,0:T(8,128)(2,1)S(1)}, bf16[16,64,1152]{2,1,0:T(8,128)(2,1)S(1)}, u32[]{:S(2)}, u32[]{:S(2)}) collective-permute-start(bf16[16,64,1152]{2,1,0:T(8,128)(2,1)S(1)} %get-tuple-element.116), channel_id=1, source_target_pairs={{0,1},{1,0},{2,3},{3,2},{4,5},{5,4},{6,7},{7,6},{8,9},{9,8},{10,11... | collective-permute-start | bytes 7077896 | tf_op jit(solution)/shard_map/ppermute | solution.py:645
  107.8 16.3 %collective-permute-start.16 = (bf16[8,64,1152]{2,1,0:T(8,128)(2,1)S(1)}, bf16[8,64,1152]{2,1,0:T(8,128)(2,1)S(1)}, u32[]{:S(2)}, u32[]{:S(2)}) collective-permute-start(bf16[8,64,1152]{2,1,0:T(8,128)(2,1)S(1)} %slice.55), channel_id=1, source_target_pairs={{0,4},{1,3},{2,6},{3,1},{4,0},{5,7},{6,2},{7,5},{8,12},{9,11},{10,... | collective-permute-start | bytes 3538952 | tf_op jit(solution)/shard_map/ppermute | solution.py:645
  107.8 4.3 %collective-permute-start.13 = (bf16[2,128,512]{2,1,0:T(8,128)(2,1)S(1)}, bf16[2,128,512]{2,1,0:T(8,128)(2,1)S(1)}, u32[]{:S(2)}, u32[]{:S(2)}) collective-permute-start(bf16[2,128,512]{2,1,0:T(8,128)(2,1)S(1)} %get-tuple-element.117), channel_id=1, source_target_pairs={{0,31},{1,0},{2,1},{3,2},{4,3},{5,4},{6,5},{7,6},{8,7},{9,8},{10,9... | collective-permute-start | bytes 786440 | tf_op jit(solution)/shard_map/ppermute | solution.py:648
  119.0 10.5 %collective-permute-start.15 = (bf16[1056,512]{1,0:T(8,128)(2,1)S(1)}, bf16[1056,512]{1,0:T(8,128)(2,1)S(1)}, u32[]{:S(2)}, u32[]{:S(2)}) collective-permute-start(bf16[1056,512]{1,0:T(8,128)(2,1)S(1)} %get-tuple-element.133.mine_ref), channel_id=1, source_target_pairs={{0,1},{1,0},{2,3},{3,2},{4,5},{5,4},{6,7},{7,6},{8,9},{9,8},{10,11... | collective-permute-start | bytes 3244040 | tf_op jit(solution)/shard_map/ppermute | solution.py:645
  124.4 14.1 %collective-permute-start.20 = (bf16[4,64,1152]{2,1,0:T(8,128)(2,1)S(1)}, bf16[4,64,1152]{2,1,0:T(8,128)(2,1)S(1)}, u32[]{:S(2)}, u32[]{:S(2)}) collective-permute-start(bf16[4,64,1152]{2,1,0:T(8,128)(2,1)S(1)} %slice.56), channel_id=1, source_target_pairs={{0,2},{1,5},{2,0},{3,7},{4,6},{5,1},{6,4},{7,3},{8,10},{9,13},{10,... | collective-permute-start | bytes 1769480 | tf_op jit(solution)/shard_map/ppermute | solution.py:645
  129.8 12.2 %collective-permute-start.18 = (bf16[544,512]{1,0:T(8,128)(2,1)S(1)}, bf16[544,512]{1,0:T(8,128)(2,1)S(1)}, u32[]{:S(2)}, u32[]{:S(2)}) collective-permute-start(bf16[544,512]{1,0:T(8,128)(2,1)S(1)} %get-tuple-element.139.mine_ref), channel_id=1, source_target_pairs={{0,4},{1,3},{2,6},{3,1},{4,0},{5,7},{6,2},{7,5},{8,12},{9,11},{10,... | collective-permute-start | bytes 1671176 | tf_op jit(solution)/shard_map/ppermute | solution.py:645
  138.6 8.0 %collective-permute-start.21 = (bf16[2,64,1152]{2,1,0:T(8,128)(2,1)S(1)}, bf16[2,64,1152]{2,1,0:T(8,128)(2,1)S(1)}, u32[]{:S(2)}, u32[]{:S(2)}) collective-permute-start(bf16[2,64,1152]{2,1,0:T(8,128)(2,1)S(1)} %slice.57), channel_id=1, source_target_pairs={{0,8},{1,9},{2,10},{3,11},{4,12},{5,13},{6,14},{7,15},{8,0},{9,1},... | collective-permute-start | bytes 884744 | tf_op jit(solution)/shard_map/ppermute | solution.py:645
  138.7 23.0 %collective-permute-start.17 = (bf16[2,128,512]{2,1,0:T(8,128)(2,1)S(1)}, bf16[2,128,512]{2,1,0:T(8,128)(2,1)S(1)}, u32[]{:S(2)}, u32[]{:S(2)}) collective-permute-start(bf16[2,128,512]{2,1,0:T(8,128)(2,1)S(1)} %get-tuple-element.145), channel_id=1, source_target_pairs={{0,31},{1,0},{2,1},{3,2},{4,3},{5,4},{6,5},{7,6},{8,7},{9,8},{10,9... | collective-permute-start | bytes 786440 | tf_op jit(solution)/shard_map/ppermute | solution.py:648
  142.1 9.5 %collective-permute-start.19 = (bf16[288,512]{1,0:T(8,128)(2,1)S(1)}, bf16[288,512]{1,0:T(8,128)(2,1)S(1)}, u32[]{:S(2)}, u32[]{:S(2)}) collective-permute-start(bf16[288,512]{1,0:T(8,128)(2,1)S(1)} %get-tuple-element.149.mine_ref), channel_id=1, source_target_pairs={{0,2},{1,5},{2,0},{3,7},{4,6},{5,1},{6,4},{7,3},{8,10},{9,13},{10,... | collective-permute-start | bytes 884744 | tf_op jit(solution)/shard_map/ppermute | solution.py:645
  146.7 12.7 %collective-permute-start.23 = (bf16[1,64,1152]{2,1,0:T(8,128)(2,1)S(1)}, bf16[1,64,1152]{2,1,0:T(8,128)(2,1)S(1)}, u32[]{:S(2)}, u32[]{:S(2)}) collective-permute-start(bf16[1,64,1152]{2,1,0:T(8,128)(2,1)S(1)} %slice.58), channel_id=1, source_target_pairs={{0,16},{1,17},{2,18},{3,19},{4,20},{5,21},{6,22},{7,23},{8,24},{9,... | collective-permute-start | bytes 442376 | tf_op jit(solution)/shard_map/ppermute | solution.py:645
  151.6 8.5 %collective-permute-start.24 = (bf16[80,512]{1,0:T(8,128)(2,1)S(1)}, bf16[80,512]{1,0:T(8,128)(2,1)S(1)}, u32[]{:S(2)}, u32[]{:S(2)}) collective-permute-start(bf16[80,512]{1,0:T(8,128)(2,1)S(1)} %get-tuple-element.158), channel_id=1, source_target_pairs={{0,8},{1,9},{2,10},{3,11},{4,12},{5,13},{6,14},{7,15},{8,0},{9,1},... | collective-permute-start | bytes 245768 | tf_op jit(solution)/shard_map/ppermute | solution.py:673
  151.7 8.4 %collective-permute-start.25 = (bf16[80,512]{1,0:T(8,128)(2,1)S(1)}, bf16[80,512]{1,0:T(8,128)(2,1)S(1)}, u32[]{:S(2)}, u32[]{:S(2)}) collective-permute-start(bf16[80,512]{1,0:T(8,128)(2,1)S(1)} %get-tuple-element.160), channel_id=1, source_target_pairs={{0,24},{1,25},{2,26},{3,27},{4,28},{5,29},{6,30},{7,31},{8,16},{9,... | collective-permute-start | bytes 245768 | tf_op jit(solution)/shard_map/ppermute | solution.py:673
  151.8 9.8 %collective-permute-start.22 = (bf16[80,512]{1,0:T(8,128)(2,1)S(1)}, bf16[80,512]{1,0:T(8,128)(2,1)S(1)}, u32[]{:S(2)}, u32[]{:S(2)}) collective-permute-start(bf16[80,512]{1,0:T(8,128)(2,1)S(1)} %get-tuple-element.154.refs_1_), channel_id=1, source_target_pairs={{0,16},{1,17},{2,18},{3,19},{4,20},{5,21},{6,22},{7,23},{8,24},{9,... | collective-permute-start | bytes 245768 | tf_op jit(solution)/shard_map/ppermute | solution.py:673
